TPU v7x, 512 devices: a whole 4x8x8 slice. The times are simulated.
512 devices in a mesh: depth: 32 (over x, z_hi, core), res: 16 (over z_lo, y).
Axes of the slice: x: 4, y: 8, z: 8 (z_hi: 4, z_lo: 2; z = z_hi * 2 + z_lo), core: 2. Of those that a mesh axis runs over, the one named last changes fastest.
Arguments:
- aligned_activations: bfloat16 [64, 1024, 64], P('depth', 'res'), may hold values from -6 to 6
- couple_offset: bfloat16 [8, 1024, 1024], P(None, ('res', 'depth')), may hold values from -320 to 320
- mapping_matrix: bfloat16 [64, 256], replicated, may hold values from -0.75 to 0.75
- final_matrix: bfloat16 [64, 64], replicated, may hold values from -0.75 to 0.75
- result_cotangent: bfloat16 [64, 1024, 64], P('depth', 'res'), may hold values from -6 to 6
Outputs:
- update: bfloat16 [64, 1024, 64], P('depth', 'res')
- d_msa: bfloat16 [64, 1024, 64], P('depth', 'res')
- d_bias: float32 [8, 1024, 1024], P(None, ('res', 'depth'))
All inputs are finite; a program needn't handle non-finite values.
Results may differ from a plain program's by a relative error of at most 0.025.
Values may be sent and summed in bfloat16 or wider, within the bound.
No kernel may reach another device: no remote copies, remote signals or barrier semaphores. Data moves between devices by JAX's collectives and lax.ppermute only.
A program may use at most 64 MiB of HBM per device.

v0:
```python
import math

import jax
import jax.numpy as jnp
from jax import lax
from jax.sharding import PartitionSpec as P

ATTENDER_TALLY = 8


EPS = 1e-05


def centering_statistic(x):
    row_average = jnp.mean(x, -1, keepdims=True)
    cent = x - row_average
    var = jnp.mean(cent * cent, -1, keepdims=True)
    reciprocal_spread = lax.rsqrt(var + EPS)
    return (cent * reciprocal_spread, reciprocal_spread)


def per_device(aligned_activations, couple_offset, mapping_matrix, final_matrix, result_cotangent):
    aligned_position, lines_tally, mapping_span = aligned_activations.shape
    head_dim = mapping_span // ATTENDER_TALLY
    logit_factor = 1.0 / math.sqrt(head_dim)
    rescaled_source, reciprocal_spread = centering_statistic(
        aligned_activations.astype(jnp.float32)
    )
    mapped_splits = jnp.einsum(
        "qod,dn->qon",
        rescaled_source.astype(jnp.bfloat16),
        mapping_matrix,
        preferred_element_type=jnp.float32,
    )
    asker_vectors = (mapped_splits[..., :mapping_span] * logit_factor).astype(jnp.bfloat16)
    keyval = mapped_splits[..., mapping_span : 3 * mapping_span].astype(jnp.bfloat16)
    sigmoid_switch = jax.nn.sigmoid(mapped_splits[..., 3 * mapping_span :])
    panel = lax.all_gather(couple_offset, "depth", axis=1, tiled=True)
    keys_all = lax.all_gather(keyval, "res", axis=1, tiled=True)
    accrued_sum_value = keys_all.shape[1]
    block = math.gcd(accrued_sum_value, 512)
    count = accrued_sum_value // block
    query_heads = asker_vectors.reshape(aligned_position, lines_tally, ATTENDER_TALLY, head_dim)

    def score_block(start):
        piece = lax.dynamic_slice_in_dim(keys_all, start, block, 1)
        key_heads = piece[..., :mapping_span].reshape(
            aligned_position, block, ATTENDER_TALLY, head_dim
        )
        value_heads = piece[..., mapping_span:].reshape(
            aligned_position, block, ATTENDER_TALLY, head_dim
        )
        bias_block = lax.dynamic_slice_in_dim(panel, start, block, 2).astype(jnp.float32)
        scores = (
            jnp.einsum(
                "sihd,sjhd->shij", query_heads, key_heads, preferred_element_type=jnp.float32
            )
            + bias_block[None]
        )
        return (scores, key_heads, value_heads)

    def stat_step(index, carry):
        top, summed = carry
        scores, unused_keys, unused_values = score_block(index * block)
        newtop = jnp.maximum(top, jnp.max(scores, -1))
        summed = summed * jnp.exp(top - newtop) + jnp.sum(jnp.exp(scores - newtop[..., None]), -1)
        return (newtop, summed)

    start_top = jnp.full((aligned_position, ATTENDER_TALLY, lines_tally), -jnp.inf, jnp.float32)
    start_sum = jnp.zeros((aligned_position, ATTENDER_TALLY, lines_tally), jnp.float32)
    top, summed = lax.fori_loop(0, count, stat_step, (start_top, start_sum))
    lse = top + jnp.log(summed)

    def value_step(index, acc):
        scores, unused_keys, value_heads = score_block(index * block)
        softmax_brain = jnp.exp(scores - lse[..., None]).astype(jnp.bfloat16)
        return acc + jnp.einsum(
            "shij,sjhd->sihd", softmax_brain, value_heads, preferred_element_type=jnp.float32
        )

    attending_per_split = lax.fori_loop(
        0,
        count,
        value_step,
        jnp.zeros((aligned_position, lines_tally, ATTENDER_TALLY, head_dim), jnp.float32),
    )
    attending_result = attending_per_split.reshape(aligned_position, lines_tally, mapping_span)
    gated = (sigmoid_switch * attending_result).astype(jnp.bfloat16)
    update = jnp.einsum(
        "qod,dn->qon", gated, final_matrix, preferred_element_type=jnp.float32
    ).astype(jnp.bfloat16)
    d_gated = jnp.einsum(
        "sre,ce->src", result_cotangent, final_matrix, preferred_element_type=jnp.float32
    )
    d_attn = (d_gated * sigmoid_switch).astype(jnp.bfloat16)
    d_gate = d_gated * attending_result * sigmoid_switch * (1.0 - sigmoid_switch)
    cot_heads = d_attn.reshape(aligned_position, lines_tally, ATTENDER_TALLY, head_dim)
    delta = jnp.sum(cot_heads.astype(jnp.float32) * attending_per_split, -1)
    delta_rows = jnp.transpose(delta, (0, 2, 1))

    def step(index, carry):
        start = index * block
        scores, key_heads, value_heads = score_block(start)
        probs = jnp.exp(scores - lse[..., None])
        softmax_brain = probs.astype(jnp.bfloat16)
        d_probs = jnp.einsum(
            "sihd,sjhd->shij", cot_heads, value_heads, preferred_element_type=jnp.float32
        )
        d_scores = probs * (d_probs - delta_rows[..., None])
        cotangent_logits_brain = d_scores.astype(jnp.bfloat16)
        cotangent_asker = carry[0] + jnp.einsum(
            "shij,sjhd->sihd", cotangent_logits_brain, key_heads, preferred_element_type=jnp.float32
        )
        grad_panel = lax.dynamic_update_slice_in_dim(carry[1], jnp.sum(d_scores, 0), start, 2)
        return (cotangent_asker, grad_panel)

    first = (
        jnp.zeros((aligned_position, lines_tally, ATTENDER_TALLY, head_dim), jnp.float32),
        jnp.zeros((ATTENDER_TALLY, lines_tally, accrued_sum_value), jnp.float32),
    )
    cotangent_asker, grad_panel = lax.fori_loop(0, count, step, first)
    columns = lax.all_to_all(panel, "res", split_axis=2, concat_axis=1, tiled=True)
    stats = jnp.concatenate([jnp.transpose(lse, (0, 2, 1)), delta], -1)
    all_stats = lax.all_gather(stats, "res", axis=1, tiled=True)
    packed_rows = jnp.concatenate([asker_vectors, d_attn], -1)
    local_keys = keyval[..., :mapping_span].reshape(
        aligned_position, lines_tally, ATTENDER_TALLY, head_dim
    )
    local_values = keyval[..., mapping_span:].reshape(
        aligned_position, lines_tally, ATTENDER_TALLY, head_dim
    )
    blank = jnp.zeros((aligned_position, lines_tally, ATTENDER_TALLY, head_dim), jnp.float32)
    piece = lax.all_gather(packed_rows, "res", axis=1, tiled=True)
    rows = piece.shape[1]
    sub = math.gcd(rows, 512)

    def inner(index, matrix_cotangents):
        offset = index * sub
        part = lax.dynamic_slice_in_dim(piece, offset, sub, 1)
        part_query = part[..., :mapping_span].reshape(
            aligned_position, sub, ATTENDER_TALLY, head_dim
        )
        part_cot = part[..., mapping_span:].reshape(aligned_position, sub, ATTENDER_TALLY, head_dim)
        part_stats = lax.dynamic_slice_in_dim(all_stats, offset, sub, 1)
        part_lse = jnp.transpose(part_stats[..., :ATTENDER_TALLY], (0, 2, 1))
        part_delta = jnp.transpose(part_stats[..., ATTENDER_TALLY:], (0, 2, 1))
        bias_rows = lax.dynamic_slice_in_dim(columns, offset, sub, 1).astype(jnp.float32)
        scores = (
            jnp.einsum(
                "sihd,sjhd->shij", part_query, local_keys, preferred_element_type=jnp.float32
            )
            + bias_rows[None]
        )
        probs = jnp.exp(scores - part_lse[..., None])
        softmax_brain = probs.astype(jnp.bfloat16)
        d_probs = jnp.einsum(
            "sihd,sjhd->shij", part_cot, local_values, preferred_element_type=jnp.float32
        )
        cotangent_logits_brain = (probs * (d_probs - part_delta[..., None])).astype(jnp.bfloat16)
        new_key = matrix_cotangents[0] + jnp.einsum(
            "shij,sihd->sjhd",
            cotangent_logits_brain,
            part_query,
            preferred_element_type=jnp.float32,
        )
        new_value = matrix_cotangents[1] + jnp.einsum(
            "shij,sihd->sjhd", softmax_brain, part_cot, preferred_element_type=jnp.float32
        )
        return (new_key, new_value)

    key_grad, value_grad = lax.fori_loop(0, rows // sub, inner, (blank, blank))
    cotangent_keyside = key_grad.reshape(aligned_position, lines_tally, mapping_span)
    cotangent_payload = value_grad.reshape(aligned_position, lines_tally, mapping_span)
    bias_grad = lax.psum_scatter(
        grad_panel.astype(jnp.bfloat16), "depth", scatter_dimension=1, tiled=True
    ).astype(jnp.float32)
    cotangent_asker = (
        cotangent_asker.reshape(aligned_position, lines_tally, mapping_span) * logit_factor
    )
    d_proj = jnp.concatenate(
        [cotangent_asker, cotangent_keyside, cotangent_payload, d_gate], -1
    ).astype(jnp.bfloat16)
    normalized_gradient = jnp.einsum(
        "sre,ce->src", d_proj, mapping_matrix, preferred_element_type=jnp.float32
    )
    input_gradient = reciprocal_spread * (
        normalized_gradient
        - jnp.mean(normalized_gradient, -1, keepdims=True)
        - rescaled_source * jnp.mean(normalized_gradient * rescaled_source, -1, keepdims=True)
    )
    return (update, input_gradient.astype(jnp.bfloat16), bias_grad)


def solution(mesh):
    return jax.shard_map(
        per_device,
        mesh=mesh,
        in_specs=(
            P("depth", "res", None),
            P(None, ("res", "depth"), None),
            P(),
            P(),
            P("depth", "res", None),
        ),
        out_specs=(
            P("depth", "res", None),
            P("depth", "res", None),
            P(None, ("res", "depth"), None),
        ),
        check_vma=False,
    )
```

profile of v0, /device:TPU:6, one launch (start us, length us, event | category | flops | bytes accessed | tf_op | source)
XLA Modules:
  0.0 236.9 jit_solution(9844925212437538315)
XLA Ops:
  7.2 1.4 copy.77
  8.7 0.8 copy.74
  9.6 0.2 fusion.75
  9.9 0.2 copy-done.2
  10.2 37.6 %all_gather.12 = bf16[2,1024,128]{2,1,0:T(8,128)(2,1)S(1)} all-gather(bf16[2,64,128]{2,1,0:T(8,128)(2,1)S(1)} %slice.96), channel_id=1, replica_groups=mesh['depth'=32,'res'=16] {'res'}, dimensions={1}, use_global_device_ids=true | all-gather | bytes 557056 | tf_op jit(solution)/shard_map/all_gather | solution.py:39
  47.9 0.2 copy.80
  48.1 25.0 %all-gather.2.cloned.1.call-done = bf16[8,64,1024]{2,0,1:T(8,128)(2,1)} async-done(((bf16[8,2,1024]{2,0,1:T(8,128)(2,1)}), bf16[8,64,1024]{2,0,1:T(8,128)(2,1)}) %all-gather.2.cloned.1.call-update) | async-done | bytes 1048592 | tf_op jit(solution)/shard_map/all_gather | solution.py:38
  73.1 1.8 copy.81
  74.9 2.7 %while.62 = (s32[]{:T(128)}, f32[2,8,64]{2,1,0:T(8,128)S(1)}, f32[2,8,64]{2,1,0:T(8,128)S(1)}, bf16[2,1024,128]{1,2,0:T(8,128)(2,1)S(1)}, bf16[2,64,8,8]{1,3,2,0...) while((s32[]{:T(128)}, f32[2,8,64]{2,1,0:T(8,128)S(1)}, ...), condition=%wide.region_5.0_spmd.clone, body=%wide.region_2.0_spmd.clone.sunk | while | flops 11277319 | bytes 8081582 | solution.py:71
  75.0 0.6 fusion.106
  75.6 0.6 exponential_reduce_fusion.2
  76.4 0.6 fusion.106
  77.0 0.6 exponential_reduce_fusion.2
  77.7 1.8 while.63
  77.7 0.1 dynamic-slice_convert_fusion.9
  77.8 0.8 fusion.109
  78.7 0.8 fusion.109
  79.6 0.8 multiply_convert_fusion.3
  80.5 4.2 %copy.87 = bf16[8,64,1024]{1,0,2:T(8,128)(2,1)} copy(bf16[8,64,1024]{2,0,1:T(8,128)(2,1)} %all-gather.2.cloned.1.call-done) | data formatting | bytes 2097152 | tf_op jit(solution)/shard_map/all_gather | solution.py:38
  84.7 4.6 %reshape.128 = bf16[16,2,16384]{2,1,0:T(2,128)(2,1)} reshape(bf16[1024,8,64]{2,1,0:T(8,128)(2,1)} %bitcast.179) | data formatting | bytes 2097152
  89.4 7.2 %all-to-all-start = ((bf16[16,2,16384]{2,1,0:T(2,128)(2,1)}), bf16[16,2,16384]{2,1,0:T(2,128)(2,1)}, u32[]{:S(2)}, u32[]{:S(2)}) async-start(bf16[16,2,16384]{2,1,0:T(2,128)(2,1)} %reshape.128), calls=%async_computation | async-start | bytes 2097152 | tf_op jit(solution)/shard_map/all_to_all | solution.py:122
  96.6 0.1 broadcast_in_dim.45.clone
  96.7 4.3 %while.64 = (s32[]{:T(128)}, f32[2,64,8,8]{1,3,2,0:T(8,128)S(1)}, bf16[8,64,1024]{2,0,1:T(8,128)(2,1)S(1)}, bf16[2,1024,128]{1,2,0:T(8,128)(2,1)S(1)}, bf16[2,64...) while((s32[]{:T(128)}, f32[2,64,8,8]{1,3,2,0:T(8,128)S(1)}, ...), condition=%wide.region_11.0_spmd.clone, body=%wide.region_9.0_spmd.clone.sunk | while | flops 28327944 | bytes 11059433 | solution.py:121
  96.8 0.5 fusion.113
  97.3 0.8 fusion.114
  98.2 0.4 fusion.115
  98.5 0.3 copy_dynamic-update-slice_fusion.2
  99.0 0.5 fusion.113
  99.5 0.8 fusion.114
  100.3 0.4 fusion.115
  100.7 0.3 copy_dynamic-update-slice_fusion.2
  101.1 1.0 copy-done.1
  102.3 0.7 copy.86
  103.1 52.1 %all_gather.15 = f32[2,1024,16]{2,0,1:T(2,128)S(1)} all-gather(f32[2,64,16]{2,0,1:T(2,128)S(1)} %copy.89), channel_id=1, replica_groups=mesh['depth'=32,'res'=16] {'res'}, dimensions={1}, use_global_device_ids=true | all-gather | bytes 139264 | tf_op jit(solution)/shard_map/all_gather | solution.py:124
  155.3 1.1 copy.92
  156.3 0.7 copy.94
  157.1 0.8 convolution_convert_fusion
  158.0 36.2 %all_gather.14 = bf16[2,1024,128]{2,1,0:T(8,128)(2,1)} all-gather(bf16[2,64,128]{2,1,0:T(8,128)(2,1)S(1)} %pad_maximum_fusion), channel_id=1, replica_groups=mesh['depth'=32,'res'=16] {'res'}, dimensions={1}, use_global_device_ids=true | all-gather | bytes 557056 | tf_op jit(solution)/shard_map/all_gather | solution.py:133
  194.2 4.1 %reduce-scatter.2.cloned.1.call-done = bf16[8,2,1024]{2,0,1:T(8,128)(2,1)} async-done(((bf16[8,64,1024]{2,0,1:T(8,128)(2,1)}), bf16[8,2,1024]{2,0,1:T(8,128)(2,1)}) %reduce-scatter.2.cloned.1.call-update) | async-done | bytes 32784 | tf_op jit(solution)/shard_map/reduce_scatter | solution.py:174
  198.2 1.4 copy.99
  199.6 3.8 %reshape.129 = bf16[1024,8,64]{2,1,0:T(8,128)(2,1)S(1)} reshape(bf16[16,2,16384]{2,1,0:T(2,128)(2,1)} %all-to-all-done) | data formatting | bytes 2097152
  203.4 2.7 %copy.88 = bf16[8,16,64,64]{2,1,3,0:T(8,128)(2,1)} copy(bf16[8,16,64,64]{2,0,3,1:T(8,128)(2,1)S(1)} %bitcast.180) | data formatting | bytes 2097152 | tf_op jit(solution)/shard_map/all_to_all | solution.py:122
  206.1 4.1 %all_to_all.16 = bf16[8,1024,64]{1,2,0:T(8,128)(2,1)} reshape(bf16[8,16,64,64]{2,1,3,0:T(8,128)(2,1)} %copy.88) | data formatting | bytes 2097152 | tf_op jit(solution)/shard_map/all_to_all | solution.py:122
  210.2 16.2 %while.65 = (s32[]{:T(128)}, f32[2,64,8,8]{1,3,2,0:T(8,128)}, f32[2,64,8,8]{1,3,2,0:T(8,128)}, bf16[2,1024,128]{2,1,0:T(8,128)(2,1)}, bf16[2,64,8,8]{1,3,2,0:T(8...) while((s32[]{:T(128)}, f32[2,64,8,8]{1,3,2,0:T(8,128)}, ...), condition=%wide.region_13.0_spmd.clone, body=%wide.region_12.0_spmd.clone.sunk | while | flops 38043656 | bytes 11927794 | solution.py:171
  210.2 0.8 dynamic-slice_bitcast_fusion.23
  211.0 1.2 constant_dynamic-slice_fusion.3
  212.2 0.1 copy.116
  212.3 0.1 copy.117
  212.4 1.2 dynamic-slice_convert_fusion.11
  213.6 1.2 fusion.123
  214.9 1.5 fusion.124
  216.4 1.1 fusion.125
  217.4 0.8 dynamic-slice_bitcast_fusion.23
  218.2 1.2 constant_dynamic-slice_fusion.3
  219.4 0.1 copy.116
  219.5 0.1 copy.117
  219.7 1.2 dynamic-slice_convert_fusion.11
  220.9 1.2 fusion.123
  222.1 2.4 fusion.124
  224.5 1.9 fusion.125
  226.4 0.9 convert_bitcast_fusion
  227.5 1.1 fusion.72
  228.5 0.8 fusion.46
  229.3 0.7 copy.98
  (51 shorter events, 1.8 us)
Async XLA Ops:
  7.2 2.4 %copy-start = (bf16[64,256]{1,0:T(8,128)(2,1)S(1)}, bf16[64,256]{1,0:T(8,128)(2,1)}, u32[]{:S(2)}) copy-start(bf16[64,256]{1,0:T(8,128)(2,1)} %param.15) | copy-start | bytes 98308
  7.2 65.9 %all-gather.2.cloned.1.call-start = ((), (), s32[]{:S(2)}) async-start(), calls=%async_computation.2 | async-start | bytes 1081344 | tf_op jit(solution)/shard_map/all_gather | solution.py:38
  9.5 0.6 copy-start.2
  77.7 1.9 copy-start.3
  77.7 1.9 copy-start.4
  89.4 110.3 %all-to-all-start = ((bf16[16,2,16384]{2,1,0:T(2,128)(2,1)}), bf16[16,2,16384]{2,1,0:T(2,128)(2,1)}, u32[]{:S(2)}, u32[]{:S(2)}) async-start(bf16[16,2,16384]{2,1,0:T(2,128)(2,1)} %reshape.128), calls=%async_computation | async-start | bytes 2097152 | tf_op jit(solution)/shard_map/all_to_all | solution.py:122
  96.5 101.7 %reduce-scatter.2.cloned.1.call-start = ((), (), s32[]{:S(2)}) async-start(), calls=%async_computation.3 | async-start | bytes 1081344 | tf_op jit(solution)/shard_map/reduce_scatter | solution.py:174
  101.1 1.0 copy-start.1
Sparse Core Ops, SparseCore 0:
  11.7 61.3 all-gather.1
  102.2 95.9 reduce-scatter.1
where the time goes:
time: 239 us; the launch traced here: 237 us
  blocking collectives  126 us (53%)
  local copies, waits for them, and re-layouts  35.5 us (15%)
  waiting for transfers between devices  29.1 us (12%)
  matrix products  18.2 us (8%)
  between operations  14.3 us (6%)
  starting transfers between devices  7.26 us (3%)
  other arithmetic  6.12 us (3%)
    all_gather x1, blocking collectives, per_device(): all_stats = lax.all_gather(stats, 'res', axis=1, tiled=True)  52.1 us
    all_gather x1, blocking collectives, per_device(): keys_all = lax.all_gather(keyval, 'res', axis=1, tiled=True)  37.6 us
    all_gather x1, blocking collectives, per_device(): piece = lax.all_gather(packed_rows, 'res', axis=1, tiled=True)  36.2 us
    all_gather x1, waiting for transfers between devices, per_device(): panel = lax.all_gather(couple_offset, 'depth', axis=1, tiled=True)  25 us
    unnamed x19, local copies, waits for them, and re-layouts  17.1 us
    all_to_all x1, starting transfers between devices, per_device(): lax.all_to_all(panel, 'res', split_axis=2, concat_axis=1, tiled=True)  7.18 us
    all_to_all x2, local copies, waits for them, and re-layouts, per_device(): lax.all_to_all(panel, 'res', split_axis=2, concat_axis=1, tiled=True)  6.8 us
  transfers between devices with their start and end apart: 3, of which 2 were waited for; matrix products, arithmetic and copies ran while one was open for 5% of the time, Pallas kernels for 0%

commit v1 on v0

v1 whole, which is shorter than its diff:
```python
import math

import jax
import jax.numpy as jnp
from jax import lax
from jax.experimental import pallas as pl
from jax.experimental.pallas import tpu as pltpu
from jax.sharding import Mesh, PartitionSpec as P

HEADS = 8
HEAD_DIM = 8
EPS = 1e-05
SCALE = 1.0 / math.sqrt(HEAD_DIM)

DEPTH = ("x", "zh", "core")
RES = ("zl", "y")
HEAD_AXES = ("zl", "zh")
KEY_AXES = ("y",)
ROW_AXES = ("x", "core")


def tdot(a, b, ca, cb):
    return lax.dot_general(a, b, (((ca,), (cb,)), ((), ())), preferred_element_type=jnp.float32)


def project_kernel(x_hbm, rc_hbm, wm_hbm, wf_hbm, bias_hbm, pack_ref, xhat_ref, rstd_ref, g_ref, dg_ref,
                   x_ref, rc_ref, wm_ref, wf_ref, bias_ref, sems):
    pairs = [(x_hbm, x_ref), (wm_hbm, wm_ref), (rc_hbm, rc_ref), (wf_hbm, wf_ref), (bias_hbm, bias_ref)]
    copies = [pltpu.make_async_copy(a, b, sems.at[i]) for i, (a, b) in enumerate(pairs)]
    for copy in copies:
        copy.start()
    for copy in copies:
        copy.wait()
    x = x_ref[...].astype(jnp.float32).T
    cent = x - jnp.mean(x, 0, keepdims=True)
    rstd = lax.rsqrt(jnp.mean(cent * cent, 0, keepdims=True) + EPS)
    xhat = cent * rstd
    proj = tdot(wm_ref[...], xhat.astype(jnp.bfloat16), 0, 0)
    g = jax.nn.sigmoid(proj[192:256])
    d_gated = tdot(wf_ref[...], rc_ref[...], 1, 1)
    d_attn = d_gated * g
    xhat_ref[...] = xhat
    rstd_ref[...] = jnp.broadcast_to(rstd, rstd_ref.shape)
    g_ref[...] = g
    dg_ref[...] = d_gated
    for h in range(HEADS):
        lo, hi = h * HEAD_DIM, (h + 1) * HEAD_DIM
        b = bias_ref[h].astype(jnp.float32)
        parts = [proj[lo:hi] * SCALE, d_attn[lo:hi], proj[64 + lo : 64 + hi], proj[128 + lo : 128 + hi]]
        parts += [b[r : r + 1, c * 128 : c * 128 + 128] for r in range(2) for c in range(8)]
        pack_ref[h] = jnp.concatenate(parts, 0).astype(jnp.bfloat16)


def attend_kernel(pack_ref, kv_ref, bias_in_ref, dkv_ref, oq_ref, db_ref, bias_ref, acc_ref, tmp_ref):
    for zl in range(2):
        for x in range(4):
            for zh in range(4):
                for core in range(2):
                    at = (zh * 2 + core) * 16
                    tmp_ref[at : at + 16] = bias_in_ref[x * 2 + core, zl * 4 + zh].astype(jnp.float32)
            for c in range(8):
                at = (zl * 4 + x) * 16
                bias_ref[at : at + 16, c * 128 : c * 128 + 128] = tmp_ref[pl.ds(c, 16, stride=8)]
    rows = lax.broadcasted_iota(jnp.int32, (16, 128), 0)
    first = rows < HEAD_DIM
    ones = jnp.ones((16, 1024), jnp.bfloat16)
    for dl in range(4):
        dkv_pair, out_pair = [], []
        for s in range(2):
            lanes = slice(s * 64, s * 64 + 64)
            kv = jnp.concatenate(
                [kv_ref[y, zl * 4 + dl][:, lanes] for zl in range(2) for y in range(8)], 1
            )
            qd = jnp.concatenate([pack_ref[zl * 4 + dl, 0:16][:, lanes] for zl in range(2)], 1)
            qd = qd.astype(jnp.float32)
            q = jnp.where(first, qd, 0.0).astype(jnp.bfloat16)
            d = jnp.where(first, 0.0, qd)
            d_bf = d.astype(jnp.bfloat16)
            scores = tdot(q, kv, 0, 0) + bias_ref[...]
            e = jnp.exp(scores - jnp.max(scores, 1, keepdims=True))
            p = e * (1.0 / jnp.sum(e, 1, keepdims=True))
            p_bf = p.astype(jnp.bfloat16)
            attn = tdot(kv, p_bf, 1, 1)
            delta = -jnp.sum(d * attn, 0, keepdims=True)
            hi = delta.astype(jnp.bfloat16).astype(jnp.float32)
            mid = (delta - hi).astype(jnp.bfloat16).astype(jnp.float32)
            low = delta - hi - mid
            tail = jnp.where(rows == 0, hi, jnp.where(rows == 1, mid, jnp.where(rows == 2, low, 0.0)))
            lhs = jnp.concatenate([d, tail], 0).astype(jnp.bfloat16)
            ds = p * tdot(lhs, jnp.concatenate([kv, ones], 0), 0, 0)
            ds_bf = ds.astype(jnp.bfloat16)
            if dl == 0 and s == 0:
                acc_ref[...] = ds
            else:
                acc_ref[...] += ds
            dq = tdot(kv, ds_bf, 1, 1)
            both = jnp.concatenate([ds_bf, p_bf], 0)
            dkv_pair.append(tdot(jnp.concatenate([q, d_bf], 1), both, 1, 0).astype(jnp.bfloat16))
            out_pair.append(jnp.where(first, dq, attn).astype(jnp.bfloat16))
        for zl in range(2):
            part = slice(zl * 64, zl * 64 + 64)
            oq_ref[zl * 4 + dl] = jnp.concatenate([o[:, part] for o in out_pair], 1)
            for y in range(8):
                r = zl * 8 + y
                part_y = slice(r * 64, r * 64 + 64)
                dkv_ref[y, zl * 4 + dl] = jnp.concatenate([o[:, part_y] for o in dkv_pair], 1)
    for zl in range(2):
        for x in range(4):
            for c in range(8):
                at = (zl * 4 + x) * 16
                tmp_ref[pl.ds(c, 16, stride=8)] = acc_ref[at : at + 16, c * 128 : c * 128 + 128]
            for zh in range(4):
                for core in range(2):
                    at = (zh * 2 + core) * 16
                    db_ref[x * 2 + core, zl * 4 + zh] = tmp_ref[at : at + 16].astype(jnp.bfloat16)


def total(ref, h):
    acc = ref[0, h].astype(jnp.float32)
    for i in range(1, 8):
        acc += ref[i, h].astype(jnp.float32)
    return acc.astype(jnp.bfloat16)


def sum_kernel(oq_ref, dkv_ref, db_ref, pack_ref):
    for h in range(HEADS):
        pack_ref[h, 0:16] = oq_ref[h]
        pack_ref[h, 16:32] = total(dkv_ref, h)
        pack_ref[h, 32:48] = total(db_ref, h)


def finish_kernel(pack_ref, xhat_ref, rstd_ref, g_ref, dg_ref, wm_ref, wf_ref, up_ref, dx_ref, db_ref):
    dq, dk, dv, attn = [], [], [], []
    for h in range(HEADS):
        own = pack_ref[h].astype(jnp.float32)
        dq.append(own[0:8] * SCALE)
        attn.append(own[8:16])
        dk.append(own[16:24])
        dv.append(own[24:32])
        for r in range(2):
            db_ref[h, r : r + 1] = jnp.concatenate(
                [own[32 + r * 8 + c : 33 + r * 8 + c] for c in range(8)], 1
            )
    attn = jnp.concatenate(attn, 0)
    g = g_ref[...]
    gated = (g * attn).astype(jnp.bfloat16)
    up_ref[...] = tdot(gated, wf_ref[...], 0, 0).astype(jnp.bfloat16)
    d_gate = dg_ref[...] * attn * g * (1.0 - g)
    d_proj = jnp.concatenate(dq + dk + dv + [d_gate], 0).astype(jnp.bfloat16)
    d_normed = tdot(wm_ref[...], d_proj, 1, 0)
    xhat = xhat_ref[...]
    dx = rstd_ref[0:1] * (
        d_normed
        - jnp.mean(d_normed, 0, keepdims=True)
        - xhat * jnp.mean(d_normed * xhat, 0, keepdims=True)
    )
    dx_ref[...] = dx.T.astype(jnp.bfloat16)


def call(kernel, outs, *args, scratch=(), space=pltpu.VMEM, limit=40):
    return pl.pallas_call(
        kernel,
        out_shape=outs,
        in_specs=[pl.BlockSpec(memory_space=space)] * len(args),
        out_specs=[pl.BlockSpec(memory_space=pltpu.VMEM)] * len(outs),
        scratch_shapes=list(scratch),
        compiler_params=pltpu.CompilerParams(vmem_limit_bytes=limit * 1024 * 1024),
    )(*args)


def shape(*dims, dtype=jnp.bfloat16):
    return jax.ShapeDtypeStruct(dims, dtype)


def exchange(a, axes):
    return lax.all_to_all(a, axes, 0, 0, tiled=True)


def spread(a):
    return jnp.broadcast_to(a[None], (8,) + a.shape)


def per_device(x, bias, wm, wf, rc):
    f32 = jnp.float32
    pack, xhat, rstd, g, d_gated = call(
        project_kernel,
        [shape(8, 48, 128), shape(64, 128, dtype=f32), shape(8, 128, dtype=f32),
         shape(64, 128, dtype=f32), shape(64, 128, dtype=f32)],
        x.reshape(128, 64), rc.reshape(128, 64), wm, wf, bias,
        scratch=[pltpu.VMEM((128, 64), jnp.bfloat16), pltpu.VMEM((128, 64), jnp.bfloat16),
                 pltpu.VMEM((64, 256), jnp.bfloat16), pltpu.VMEM((64, 64), jnp.bfloat16),
                 pltpu.VMEM((8, 2, 1024), jnp.bfloat16), pltpu.SemaphoreType.DMA((5,))],
        space=pltpu.HBM, limit=60,
    )
    pack = exchange(pack, HEAD_AXES)
    kv = exchange(spread(pack[:, 16:32]), KEY_AXES)
    bias_rows = exchange(spread(pack[:, 32:48]), ROW_AXES)
    dkv, oq, db = call(
        attend_kernel,
        [shape(8, 8, 16, 128), shape(8, 16, 128), shape(8, 8, 16, 128)],
        pack, kv, bias_rows,
        scratch=[pltpu.VMEM((128, 1024), f32), pltpu.VMEM((128, 1024), f32), pltpu.VMEM((128, 128), f32)],
    )
    dkv = exchange(dkv, KEY_AXES)
    db = exchange(db, ROW_AXES)
    (back,) = call(sum_kernel, [shape(8, 48, 128)], oq, dkv, db)
    back = exchange(back, HEAD_AXES)
    update, dx, d_bias = call(
        finish_kernel,
        [shape(128, 64), shape(128, 64), shape(8, 2, 1024, dtype=f32)],
        back, xhat, rstd, g, d_gated, wm, wf,
    )
    return update.reshape(2, 64, 64), dx.reshape(2, 64, 64), d_bias


def solution(mesh):
    fine = Mesh(mesh.devices.reshape(4, 4, 2, 2, 8), DEPTH + RES)
    tokens = P(DEPTH, RES, None)
    rows = P(None, RES + DEPTH, None)
    return jax.shard_map(
        per_device,
        mesh=fine,
        in_specs=(tokens, rows, P(), P(), tokens),
        out_specs=(tokens, tokens, rows),
        check_vma=False,
    )
```

time: 239 us -> 94.9 us (0.40)
  blocking collectives: 126 us -> 81.3 us
  local copies, waits for them, and re-layouts: 35.5 us -> 0.75 us
  waiting for transfers between devices: 29.1 us -> 0 us
  matrix products: 18.2 us -> 0 us
  between operations: 14.3 us -> 0.71 us
  Pallas kernels: 0 us -> 10.9 us
  starting transfers between devices: 7.26 us -> 0 us
  other arithmetic: 6.12 us -> 0 us
    all_gather x3 -> x0, blocking collectives: 126 us -> none  [the longest x1 52.1 us: per_device(): all_stats = lax.all_gather(stats, 'res', axis=1, tiled=True)]
    all_to_all x0 -> x6, blocking collectives: none -> 81.3 us  [exchange(): return lax.all_to_all(a, axes, 0, 0, tiled=True)]
    all_gather x1 -> x0, waiting for transfers between devices: 25 us -> none  [per_device(): panel = lax.all_gather(couple_offset, 'depth', axis=1, tiled=True)]
    dot_general x20 -> x0, matrix products: 18.2 us -> none  [the longest x2 3.88 us: inner(): jnp.einsum('shij,sihd->sjhd', cotangent_logits_brain, part_query, preferr...]
    unnamed x19 -> x12, local copies, waits for them, and re-layouts: 17.1 us -> 0.68 us
    pallas_call x0 -> x4, Pallas kernels: none -> 10.9 us  [call(): pl.pallas_call(kernel, out_shape=outs, in_specs=[pl.BlockSpec(memory_spac...]
    all_to_all x1 -> x0, starting transfers between devices: 7.18 us -> none  [per_device(): lax.all_to_all(panel, 'res', split_axis=2, concat_axis=1, tiled=True)]
    all_to_all x2 -> x0, local copies, waits for them, and re-layouts: 6.8 us -> none  [per_device(): lax.all_to_all(panel, 'res', split_axis=2, concat_axis=1, tiled=True)]
  transfers between devices with their start and end apart: 3 -> 0, of which waited for: 2 -> 0; matrix products, arithmetic and copies ran while one was open for 5% -> 0% of each run, Pallas kernels for 0% -> 0%
where the time goes in v1:
time: 94.9 us; the launch traced here: 93.7 us
  blocking collectives  81.3 us (86%)
  Pallas kernels  10.9 us (11%)
    all_to_all x6, blocking collectives, exchange(): return lax.all_to_all(a, axes, 0, 0, tiled=True)  81.3 us
    pallas_call x4, Pallas kernels, call(): pl.pallas_call(kernel, out_shape=outs, in_specs=[pl.BlockSpec(memory_spac...  10.9 us

profile of v1, /device:TPU:6, one launch (start us, length us, event | category | flops | bytes accessed | tf_op | source)
XLA Modules:
  0.0 93.7 jit_solution(15606219538922547002)
XLA Ops:
  0.6 1.8 %shard_map.76 = (bf16[8,48,128]{2,1,0:T(8,128)(2,1)}, f32[64,128]{1,0:T(8,128)}, f32[8,128]{1,0:T(8,128)}, f32[64,128]{1,0:T(8,128)}, f32[64,128]{1,0:T(8,128)}) custom-call(bf16[128,64]{1,0:T(8,128)(2,1)} %bitcast.4, bf16[128,64]{1,0:T(8,128)(2,1)} %bitcast.5, bf16[64,256]{1,0:T(8,128)(2,1)} %wm_ref.1, bf16[64,64]{1,0:T(8,128)(2,1)} %wf_ref.1, ...), custom_call_target="tpu_custom_call" | custom-call | tf_op jit(solution)/shard_map/pallas_call | solution.py:161
  2.4 18.1 %all_to_all.30.pack_ref = bf16[8,48,128]{2,1,0:T(8,128)(2,1)S(1)} all-to-all(bf16[8,48,128]{2,1,0:T(8,128)(2,1)} %get-tuple-element.14), channel_id=1, replica_groups=mesh['x'=4,'zh'=4,'core'=2,'zl'=2,'y'=8] {'zl','zh'}, dimensions={0} | all-to-all | bytes 196608 | tf_op jit(solution)/shard_map/all_to_all | solution.py:176
  20.6 10.0 %all_to_all.31.bias_in_ref = bf16[8,8,16,128]{3,2,1,0:T(8,128)(2,1)S(1)} all-to-all(bf16[8,8,16,128]{3,2,1,0:T(8,128)(2,1)S(1)} %broadcast_in_dim.5), channel_id=1, replica_groups=mesh['x'=4,'zh'=4,'core'=2,'zl'=2,'y'=8] {'x','core'}, dimensions={0} | all-to-all | bytes 524288 | tf_op jit(solution)/shard_map/all_to_all | solution.py:176
  30.7 18.4 %all_to_all.32.kv_ref = bf16[8,8,16,128]{3,2,1,0:T(8,128)(2,1)S(1)} all-to-all(bf16[8,8,16,128]{3,2,1,0:T(8,128)(2,1)S(1)} %broadcast_in_dim.4), channel_id=1, replica_groups=mesh['x'=4,'zh'=4,'core'=2,'zl'=2,'y'=8] {'y'}, dimensions={0} | all-to-all | bytes 524288 | tf_op jit(solution)/shard_map/all_to_all | solution.py:176
  49.1 8.1 %shard_map.77 = (bf16[8,8,16,128]{3,2,1,0:T(8,128)(2,1)S(1)}, bf16[8,16,128]{2,1,0:T(8,128)(2,1)S(1)}, bf16[8,8,16,128]{3,2,1,0:T(8,128)(2,1)S(1)}) custom-call(bf16[8,48,128]{2,1,0:T(8,128)(2,1)S(1)} %all_to_all.30.pack_ref, bf16[8,8,16,128]{3,2,1,0:T(8,128)(2,1)S(1)} %all_to_all.32.kv_ref, bf16[8,8,16,128]{3,2,1,0:T(8,128)(2,1)S(1)} %all_to_all.31.bias_in_ref), custom_call_target="tpu_custom_call" | custom-call | tf_op jit(solution)/shard_map/pallas_call | solution.py:161
  57.2 9.9 %all_to_all.33.db_ref = bf16[8,8,16,128]{3,2,1,0:T(8,128)(2,1)S(1)} all-to-all(bf16[8,8,16,128]{3,2,1,0:T(8,128)(2,1)S(1)} %get-tuple-element.17), channel_id=1, replica_groups=mesh['x'=4,'zh'=4,'core'=2,'zl'=2,'y'=8] {'x','core'}, dimensions={0} | all-to-all | bytes 524288 | tf_op jit(solution)/shard_map/all_to_all | solution.py:176
  67.2 14.2 %all_to_all.34.dkv_ref = bf16[8,8,16,128]{3,2,1,0:T(8,128)(2,1)S(1)} all-to-all(bf16[8,8,16,128]{3,2,1,0:T(8,128)(2,1)S(1)} %get-tuple-element.16), channel_id=1, replica_groups=mesh['x'=4,'zh'=4,'core'=2,'zl'=2,'y'=8] {'y'}, dimensions={0} | all-to-all | bytes 524288 | tf_op jit(solution)/shard_map/all_to_all | solution.py:176
  81.4 0.1 shard_map.78
  81.4 0.0 copy-start
  81.4 0.0 copy-start.1
  81.5 0.0 copy-start.2
  81.5 0.0 copy-start.3
  81.5 0.0 copy-start.4
  81.5 10.6 %all_to_all.35.pack_ref = bf16[8,48,128]{2,1,0:T(8,128)(2,1)S(1)} all-to-all(bf16[8,48,128]{2,1,0:T(8,128)(2,1)S(1)} %shard_map.78), channel_id=1, replica_groups=mesh['x'=4,'zh'=4,'core'=2,'zl'=2,'y'=8] {'zl','zh'}, dimensions={0} | all-to-all | bytes 196608 | tf_op jit(solution)/shard_map/all_to_all | solution.py:176
  92.1 0.0 copy-start.5
  92.1 0.0 copy-done
  92.1 0.0 copy-done.1
  92.1 0.0 copy-done.2
  92.1 0.0 copy-done.3
  92.1 0.0 copy-done.4
  92.1 0.6 copy-done.5
  92.8 1.0 %shard_map.79 = (bf16[128,64]{1,0:T(8,128)(2,1)}, bf16[128,64]{1,0:T(8,128)(2,1)}, f32[8,2,1024]{2,1,0:T(2,128)}) custom-call(bf16[8,48,128]{2,1,0:T(8,128)(2,1)S(1)} %all_to_all.35.pack_ref, f32[64,128]{1,0:T(8,128)S(1)} %copy-done.2, f32[8,128]{1,0:T(8,128)S(1)} %copy-done.5, f32[64,128]{1,0:T(8,128)S(1)} %copy-done.3, f32[64,128]{1,0:T(8,128)S(1)} %copy-done.4, ...), custom_call_target="tpu_custom_call" | custom-call | tf_op jit(solution)/shard_map/pallas_call | solution.py:161
  (3 shorter events, 0.1 us)
Async XLA Ops:
  81.4 10.7 %copy-start = (bf16[64,256]{1,0:T(8,128)(2,1)S(1)}, bf16[64,256]{1,0:T(8,128)(2,1)}, u32[]{:S(2)}) copy-start(bf16[64,256]{1,0:T(8,128)(2,1)} %wm_ref.1) | copy-start | bytes 98308
  81.4 10.7 %copy-start.1 = (bf16[64,64]{1,0:T(8,128)(2,1)S(1)}, bf16[64,64]{1,0:T(8,128)(2,1)}, u32[]{:S(2)}) copy-start(bf16[64,64]{1,0:T(8,128)(2,1)} %wf_ref.1) | copy-start | bytes 24580
  81.5 10.7 %copy-start.2 = (f32[64,128]{1,0:T(8,128)S(1)}, f32[64,128]{1,0:T(8,128)}, u32[]{:S(2)}) copy-start(f32[64,128]{1,0:T(8,128)} %get-tuple-element.18.xhat_ref) | copy-start | bytes 98308
  81.5 10.7 %copy-start.3 = (f32[64,128]{1,0:T(8,128)S(1)}, f32[64,128]{1,0:T(8,128)}, u32[]{:S(2)}) copy-start(f32[64,128]{1,0:T(8,128)} %get-tuple-element.20.g_ref) | copy-start | bytes 98308
  81.5 10.7 %copy-start.4 = (f32[64,128]{1,0:T(8,128)S(1)}, f32[64,128]{1,0:T(8,128)}, u32[]{:S(2)}) copy-start(f32[64,128]{1,0:T(8,128)} %get-tuple-element.21.dg_ref) | copy-start | bytes 98308
  92.1 0.7 copy-start.5

commit v2 on v1

--- a/solution.py
+++ b/solution.py
@@ -16,7 +16,6 @@
 RES = ("zl", "y")
 HEAD_AXES = ("zl", "zh")
 KEY_AXES = ("y",)
-ROW_AXES = ("x", "core")
 
 
 def tdot(a, b, ca, cb):
@@ -51,13 +50,22 @@
         pack_ref[h] = jnp.concatenate(parts, 0).astype(jnp.bfloat16)
 
 
-def attend_kernel(pack_ref, kv_ref, bias_in_ref, dkv_ref, oq_ref, db_ref, bias_ref, acc_ref, tmp_ref):
+def attend_kernel(*refs):
+    pack_ref, kv_ref, own_bias, swap_bias = refs[:4]
+    oq_ref, dkv_ref, keep_ref, give_ref = refs[4:8]
+    wide_ref, bias_ref, acc_ref, tmp_ref = refs[8:]
+    me_x, core = lax.axis_index("x"), lax.axis_index("core")
+    for k in range(4):
+        at = lax.rem(me_x + 4 - k, 4) * 2
+        for h in range(8):
+            wide_ref[at + core, h] = own_bias[k, h].astype(jnp.float32)
+            wide_ref[at + 1 - core, h] = swap_bias[k, h].astype(jnp.float32)
     for zl in range(2):
         for x in range(4):
             for zh in range(4):
-                for core in range(2):
-                    at = (zh * 2 + core) * 16
-                    tmp_ref[at : at + 16] = bias_in_ref[x * 2 + core, zl * 4 + zh].astype(jnp.float32)
+                for half in range(2):
+                    at = (zh * 2 + half) * 16
+                    tmp_ref[at : at + 16] = wide_ref[x * 2 + half, zl * 4 + zh]
             for c in range(8):
                 at = (zl * 4 + x) * 16
                 bias_ref[at : at + 16, c * 128 : c * 128 + 128] = tmp_ref[pl.ds(c, 16, stride=8)]
@@ -110,23 +118,36 @@
                 at = (zl * 4 + x) * 16
                 tmp_ref[pl.ds(c, 16, stride=8)] = acc_ref[at : at + 16, c * 128 : c * 128 + 128]
             for zh in range(4):
-                for core in range(2):
-                    at = (zh * 2 + core) * 16
-                    db_ref[x * 2 + core, zl * 4 + zh] = tmp_ref[at : at + 16].astype(jnp.bfloat16)
-
-
-def total(ref, h):
-    acc = ref[0, h].astype(jnp.float32)
-    for i in range(1, 8):
-        acc += ref[i, h].astype(jnp.float32)
+                for half in range(2):
+                    at = (zh * 2 + half) * 16
+                    wide_ref[x * 2 + half, zl * 4 + zh] = tmp_ref[at : at + 16]
+    for k in range(4):
+        to = lax.rem(me_x + k, 4) * 2
+        for h in range(8):
+            keep_ref[k, h] = wide_ref[to + core, h].astype(jnp.bfloat16)
+            give_ref[k, h] = wide_ref[to + 1 - core, h].astype(jnp.bfloat16)
+
+
+def join_kernel(keep_ref, got_ref, *out_refs):
+    for k in range(4):
+        for h in range(HEADS):
+            both = keep_ref[k, h].astype(jnp.float32) + got_ref[k, h].astype(jnp.float32)
+            out_refs[k][h] = both.astype(jnp.bfloat16)
+
+
+def total(blocks):
+    acc = blocks[0].astype(jnp.float32)
+    for block in blocks[1:]:
+        acc += block.astype(jnp.float32)
     return acc.astype(jnp.bfloat16)
 
 
-def sum_kernel(oq_ref, dkv_ref, db_ref, pack_ref):
+def sum_kernel(*refs):
+    oq_ref, dkv_ref, db_refs, pack_ref = refs[0], refs[1], refs[2:6], refs[6]
     for h in range(HEADS):
         pack_ref[h, 0:16] = oq_ref[h]
-        pack_ref[h, 16:32] = total(dkv_ref, h)
-        pack_ref[h, 32:48] = total(db_ref, h)
+        pack_ref[h, 16:32] = total([dkv_ref[y, h] for y in range(8)])
+        pack_ref[h, 32:48] = total([ref[h] for ref in db_refs])
 
 
 def finish_kernel(pack_ref, xhat_ref, rstd_ref, g_ref, dg_ref, wm_ref, wf_ref, up_ref, dx_ref, db_ref):
@@ -176,8 +197,12 @@
     return lax.all_to_all(a, axes, 0, 0, tiled=True)
 
 
-def spread(a):
-    return jnp.broadcast_to(a[None], (8,) + a.shape)
+def shift_x(a, k):
+    return lax.ppermute(a, "x", [(i, (i + k) % 4) for i in range(4)])
+
+
+def swap_core(a):
+    return lax.ppermute(a, "core", [(0, 1), (1, 0)])
 
 
 def per_device(x, bias, wm, wf, rc):
@@ -193,17 +218,23 @@
         space=pltpu.HBM, limit=60,
     )
     pack = exchange(pack, HEAD_AXES)
-    kv = exchange(spread(pack[:, 16:32]), KEY_AXES)
-    bias_rows = exchange(spread(pack[:, 32:48]), ROW_AXES)
-    dkv, oq, db = call(
+    own = pack[:, 16:32]
+    kv = exchange(jnp.broadcast_to(own[None], (8,) + own.shape), KEY_AXES)
+    own = pack[:, 32:48]
+    own_bias = jnp.stack([own] + [shift_x(own, k) for k in range(1, 4)])
+    swap_bias = swap_core(own_bias)
+    block, quad, octet = shape(8, 16, 128), shape(4, 8, 16, 128), shape(8, 8, 16, 128)
+    oq, dkv, keep, give = call(
         attend_kernel,
-        [shape(8, 8, 16, 128), shape(8, 16, 128), shape(8, 8, 16, 128)],
-        pack, kv, bias_rows,
-        scratch=[pltpu.VMEM((128, 1024), f32), pltpu.VMEM((128, 1024), f32), pltpu.VMEM((128, 128), f32)],
+        [block, octet, quad, quad],
+        pack, kv, own_bias, swap_bias,
+        scratch=[pltpu.VMEM((8, 8, 16, 128), f32), pltpu.VMEM((128, 1024), f32),
+                 pltpu.VMEM((128, 1024), f32), pltpu.VMEM((128, 128), f32)],
     )
     dkv = exchange(dkv, KEY_AXES)
-    db = exchange(db, ROW_AXES)
-    (back,) = call(sum_kernel, [shape(8, 48, 128)], oq, dkv, db)
+    db = call(join_kernel, [block] * 4, keep, swap_core(give))
+    db = [db[0]] + [shift_x(db[k], k) for k in range(1, 4)]
+    (back,) = call(sum_kernel, [shape(8, 48, 128)], oq, dkv, *db)
     back = exchange(back, HEAD_AXES)
     update, dx, d_bias = call(
         finish_kernel,

time: 94.9 us -> 92.9 us (0.979)
  the two profiles are of different devices: /device:TPU:6 before, /device:TPU:8 now
where the time goes in v2:
time: 92.9 us; the launch traced here: 92.1 us
  starting transfers between devices  41.3 us (44%)
  blocking collectives  28.8 us (31%)
  Pallas kernels  11.7 us (13%)
  waiting for transfers between devices  8.06 us (9%)
  local copies, waits for them, and re-layouts  1.42 us (2%)
    all_to_all x2, blocking collectives, exchange(): return lax.all_to_all(a, axes, 0, 0, tiled=True)  28.8 us
    ppermute x6, starting transfers between devices, shift_x(): return lax.ppermute(a, 'x', [(i, (i + k) % 4) for i in range(4)])  22.7 us
    all_to_all x2, starting transfers between devices, exchange(): return lax.all_to_all(a, axes, 0, 0, tiled=True)  14.8 us
    pallas_call x5, Pallas kernels, call(): pl.pallas_call(kernel, out_shape=outs, in_specs=[pl.BlockSpec(memory_spac...  11.7 us
    ppermute x6, waiting for transfers between devices, shift_x(): return lax.ppermute(a, 'x', [(i, (i + k) % 4) for i in range(4)])  5.42 us
    ppermute x2, starting transfers between devices, swap_core(): return lax.ppermute(a, 'core', [(0, 1), (1, 0)])  3.83 us
    ppermute x2, waiting for transfers between devices, swap_core(): return lax.ppermute(a, 'core', [(0, 1), (1, 0)])  2.63 us
  transfers between devices with their start and end apart: 10, of which 4 were waited for; matrix products, arithmetic and copies ran while one was open for 0% of the time, Pallas kernels for 0%

profile of v2, /device:TPU:8, one launch (start us, length us, event | category | flops | bytes accessed | tf_op | source)
XLA Modules:
  0.0 92.1 jit_solution(18009407192023341364)
XLA Ops:
  0.6 1.8 %shard_map.76 = (bf16[8,48,128]{2,1,0:T(8,128)(2,1)}, f32[64,128]{1,0:T(8,128)}, f32[8,128]{1,0:T(8,128)}, f32[64,128]{1,0:T(8,128)}, f32[64,128]{1,0:T(8,128)}) custom-call(bf16[128,64]{1,0:T(8,128)(2,1)} %bitcast.9, bf16[128,64]{1,0:T(8,128)(2,1)} %bitcast.10, bf16[64,256]{1,0:T(8,128)(2,1)} %wm_ref.1, bf16[64,64]{1,0:T(8,128)(2,1)} %wf_ref.1, ...), custom_call_target="tpu_custom_call" | custom-call | tf_op jit(solution)/shard_map/pallas_call | solution.py:182
  2.5 18.1 %all_to_all.20.refs_0_ = bf16[8,48,128]{2,1,0:T(8,128)(2,1)S(1)} all-to-all(bf16[8,48,128]{2,1,0:T(8,128)(2,1)} %get-tuple-element.19), channel_id=1, replica_groups=mesh['x'=4,'zh'=4,'core'=2,'zl'=2,'y'=8] {'zl','zh'}, dimensions={0} | all-to-all | bytes 196608 | tf_op jit(solution)/shard_map/all_to_all | solution.py:197
  20.6 0.7 broadcast_in_dim.2
  21.3 7.5 %all-to-all-start.1 = ((bf16[8,8,16,128]{3,2,1,0:T(8,128)(2,1)}), bf16[8,8,16,128]{3,2,1,0:T(8,128)(2,1)S(1)}, u32[]{:S(2)}, u32[]{:S(2)}) async-start(bf16[8,8,16,128]{3,2,1,0:T(8,128)(2,1)} %broadcast_in_dim.2), calls=%async_computation.1 | async-start | bytes 524288 | tf_op jit(solution)/shard_map/all_to_all | solution.py:197
  28.9 4.9 %collective-permute-start.1 = (bf16[8,16,128]{2,1,0:T(8,128)(2,1)S(1)}, bf16[8,16,128]{2,1,0:T(8,128)(2,1)S(1)}, u32[]{:S(2)}, u32[]{:S(2)}) collective-permute-start(bf16[8,16,128]{2,1,0:T(8,128)(2,1)S(1)} %get-tuple-element.36), channel_id=1, source_target_pairs={{0,256},{128,384},{256,0},{384,128},{1,257},{129,385},{257,1},{385... | collective-permute-start | bytes 98312 | tf_op jit(solution)/shard_map/ppermute | solution.py:201
  33.8 2.5 %collective-permute-start = (bf16[8,16,128]{2,1,0:T(8,128)(2,1)S(1)}, bf16[8,16,128]{2,1,0:T(8,128)(2,1)S(1)}, u32[]{:S(2)}, u32[]{:S(2)}) collective-permute-start(bf16[8,16,128]{2,1,0:T(8,128)(2,1)S(1)} %get-tuple-element.36), channel_id=1, source_target_pairs={{0,128},{128,256},{256,384},{384,0},{1,129},{129,257},{257,385},{3... | collective-permute-start | bytes 98312 | tf_op jit(solution)/shard_map/ppermute | solution.py:201
  36.3 4.6 %collective-permute-start.2 = (bf16[8,16,128]{2,1,0:T(8,128)(2,1)S(1)}, bf16[8,16,128]{2,1,0:T(8,128)(2,1)S(1)}, u32[]{:S(2)}, u32[]{:S(2)}) collective-permute-start(bf16[8,16,128]{2,1,0:T(8,128)(2,1)S(1)} %get-tuple-element.36), channel_id=1, source_target_pairs={{0,384},{128,0},{256,128},{384,256},{1,385},{129,1},{257,129},{385... | collective-permute-start | bytes 98312 | tf_op jit(solution)/shard_map/ppermute | solution.py:201
  40.9 0.0 collective-permute-done.1
  40.9 0.0 collective-permute-done
  40.9 1.6 %collective-permute-done.2 = bf16[8,16,128]{2,1,0:T(8,128)(2,1)S(1)} collective-permute-done((bf16[8,16,128]{2,1,0:T(8,128)(2,1)S(1)}, bf16[8,16,128]{2,1,0:T(8,128)(2,1)S(1)}, u32[]{:S(2)}, u32[]{:S(2)}) %collective-permute-start.2) | collective-permute-done | bytes 32800 | tf_op jit(solution)/shard_map/ppermute | solution.py:201
  42.5 1.9 %collective-permute-start.3 = (bf16[4,8,16,128]{3,2,1,0:T(8,128)(2,1)S(1)}, bf16[4,8,16,128]{3,2,1,0:T(8,128)(2,1)S(1)}, u32[]{:S(2)}, u32[]{:S(2)}) collective-permute-start(bf16[4,8,16,128]{3,2,1,0:T(8,128)(2,1)S(1)} %pad_maximum_fusion.refs_2_), channel_id=1, source_target_pairs={{0,16},{16,0},{1,17},{17,1},{2,18},{18,2},{3,19},{19,3},{4,20},{20... | collective-permute-start | bytes 393224 | tf_op jit(solution)/shard_map/ppermute | solution.py:205
  44.4 1.3 %collective-permute-done.3.refs_3_ = bf16[4,8,16,128]{3,2,1,0:T(8,128)(2,1)S(1)} collective-permute-done((bf16[4,8,16,128]{3,2,1,0:T(8,128)(2,1)S(1)}, bf16[4,8,16,128]{3,2,1,0:T(8,128)(2,1)S(1)}, u32[]{:S(2)}, u32[]{:S(2)}) %collective-permute-start.3) | collective-permute-done | bytes 131104 | tf_op jit(solution)/shard_map/ppermute | solution.py:205
  45.7 0.0 all-to-all-done.1.refs_1_
  45.7 8.8 %shard_map.77 = (bf16[8,16,128]{2,1,0:T(8,128)(2,1)S(1)}, bf16[8,8,16,128]{3,2,1,0:T(8,128)(2,1)}, bf16[4,8,16,128]{3,2,1,0:T(8,128)(2,1)S(1)}, bf16[4,8,16,128]{3,2,1,0:T(8,128)(2,1)S(1)}) custom-call(bf16[8,48,128]{2,1,0:T(8,128)(2,1)S(1)} %all_to_all.20.refs_0_, bf16[8,8,16,128]{3,2,1,0:T(8,128)(2,1)S(1)} %all-to-all-done.1.refs_1_, ...), custom_call_target="tpu_custom_call" | custom-call | tf_op jit(solution)/shard_map/pallas_call | solution.py:182
  54.6 7.2 %all-to-all-start.2 = ((bf16[8,8,16,128]{3,2,1,0:T(8,128)(2,1)}), bf16[8,8,16,128]{3,2,1,0:T(8,128)(2,1)S(1)}, u32[]{:S(2)}, u32[]{:S(2)}) async-start(bf16[8,8,16,128]{3,2,1,0:T(8,128)(2,1)} %get-tuple-element.21), calls=%async_computation.2 | async-start | bytes 524288 | tf_op jit(solution)/shard_map/all_to_all | solution.py:197
  61.8 1.9 %collective-permute-start.4 = (bf16[4,8,16,128]{3,2,1,0:T(8,128)(2,1)S(1)}, bf16[4,8,16,128]{3,2,1,0:T(8,128)(2,1)S(1)}, u32[]{:S(2)}, u32[]{:S(2)}) collective-permute-start(bf16[4,8,16,128]{3,2,1,0:T(8,128)(2,1)S(1)} %get-tuple-element.23), channel_id=1, source_target_pairs={{0,16},{16,0},{1,17},{17,1},{2,18},{18,2},{3,19},{19,3},{4,20},{20... | collective-permute-start | bytes 393224 | tf_op jit(solution)/shard_map/ppermute | solution.py:205
  63.7 1.3 %collective-permute-done.4.got_ref = bf16[4,8,16,128]{3,2,1,0:T(8,128)(2,1)S(1)} collective-permute-done((bf16[4,8,16,128]{3,2,1,0:T(8,128)(2,1)S(1)}, bf16[4,8,16,128]{3,2,1,0:T(8,128)(2,1)S(1)}, u32[]{:S(2)}, u32[]{:S(2)}) %collective-permute-start.4) | collective-permute-done | bytes 131104 | tf_op jit(solution)/shard_map/ppermute | solution.py:205
  65.0 1.9 %collective-permute-start.5 = (bf16[8,16,128]{2,1,0:T(8,128)(2,1)S(1)}, bf16[8,16,128]{2,1,0:T(8,128)(2,1)S(1)}, u32[]{:S(2)}, u32[]{:S(2)}) collective-permute-start(bf16[8,16,128]{2,1,0:T(8,128)(2,1)S(1)} %get-tuple-element.25), channel_id=1, source_target_pairs={{0,128},{128,256},{256,384},{384,0},{1,129},{129,257},{257,385},{3... | collective-permute-start | bytes 98312 | tf_op jit(solution)/shard_map/ppermute | solution.py:201
  67.0 6.9 %collective-permute-start.6 = (bf16[8,16,128]{2,1,0:T(8,128)(2,1)S(1)}, bf16[8,16,128]{2,1,0:T(8,128)(2,1)S(1)}, u32[]{:S(2)}, u32[]{:S(2)}) collective-permute-start(bf16[8,16,128]{2,1,0:T(8,128)(2,1)S(1)} %get-tuple-element.26), channel_id=1, source_target_pairs={{0,256},{128,384},{256,0},{384,128},{1,257},{129,385},{257,1},{385... | collective-permute-start | bytes 98312 | tf_op jit(solution)/shard_map/ppermute | solution.py:201
  73.9 1.9 %collective-permute-start.7 = (bf16[8,16,128]{2,1,0:T(8,128)(2,1)S(1)}, bf16[8,16,128]{2,1,0:T(8,128)(2,1)S(1)}, u32[]{:S(2)}, u32[]{:S(2)}) collective-permute-start(bf16[8,16,128]{2,1,0:T(8,128)(2,1)S(1)} %get-tuple-element.27), channel_id=1, source_target_pairs={{0,384},{128,0},{256,128},{384,256},{1,385},{129,1},{257,129},{385... | collective-permute-start | bytes 98312 | tf_op jit(solution)/shard_map/ppermute | solution.py:201
  75.8 0.0 collective-permute-done.5.refs_3_
  75.8 0.0 collective-permute-done.6.refs_4_
  75.8 3.9 %collective-permute-done.7.refs_5_ = bf16[8,16,128]{2,1,0:T(8,128)(2,1)S(1)} collective-permute-done((bf16[8,16,128]{2,1,0:T(8,128)(2,1)S(1)}, bf16[8,16,128]{2,1,0:T(8,128)(2,1)S(1)}, u32[]{:S(2)}, u32[]{:S(2)}) %collective-permute-start.7) | collective-permute-done | bytes 32800 | tf_op jit(solution)/shard_map/ppermute | solution.py:201
  79.7 0.0 all-to-all-done.2.refs_1_
  79.7 0.1 shard_map.79
  79.7 0.0 copy-start
  79.7 0.0 copy-start.1
  79.8 0.0 copy-start.2
  79.8 0.0 copy-start.3
  79.8 0.0 copy-start.4
  79.8 10.7 %all_to_all.21.pack_ref = bf16[8,48,128]{2,1,0:T(8,128)(2,1)S(1)} all-to-all(bf16[8,48,128]{2,1,0:T(8,128)(2,1)S(1)} %shard_map.79), channel_id=1, replica_groups=mesh['x'=4,'zh'=4,'core'=2,'zl'=2,'y'=8] {'zl','zh'}, dimensions={0} | all-to-all | bytes 196608 | tf_op jit(solution)/shard_map/all_to_all | solution.py:197
  90.5 0.0 copy-start.5
  90.5 0.0 copy-done
  90.5 0.0 copy-done.1
  90.5 0.0 copy-done.2
  90.5 0.0 copy-done.3
  90.5 0.0 copy-done.4
  90.5 0.6 copy-done.5
  91.2 1.0 %shard_map.80 = (bf16[128,64]{1,0:T(8,128)(2,1)}, bf16[128,64]{1,0:T(8,128)(2,1)}, f32[8,2,1024]{2,1,0:T(2,128)}) custom-call(bf16[8,48,128]{2,1,0:T(8,128)(2,1)S(1)} %all_to_all.21.pack_ref, f32[64,128]{1,0:T(8,128)S(1)} %copy-done.2, f32[8,128]{1,0:T(8,128)S(1)} %copy-done.5, f32[64,128]{1,0:T(8,128)S(1)} %copy-done.3, f32[64,128]{1,0:T(8,128)S(1)} %copy-done.4, ...), custom_call_target="tpu_custom_call" | custom-call | tf_op jit(solution)/shard_map/pallas_call | solution.py:182
  (3 shorter events, 0.1 us)
Async XLA Ops:
  21.3 24.4 %all-to-all-start.1 = ((bf16[8,8,16,128]{3,2,1,0:T(8,128)(2,1)}), bf16[8,8,16,128]{3,2,1,0:T(8,128)(2,1)S(1)}, u32[]{:S(2)}, u32[]{:S(2)}) async-start(bf16[8,8,16,128]{3,2,1,0:T(8,128)(2,1)} %broadcast_in_dim.2), calls=%async_computation.1 | async-start | bytes 524288 | tf_op jit(solution)/shard_map/all_to_all | solution.py:197
  28.9 12.0 %collective-permute-start.1 = (bf16[8,16,128]{2,1,0:T(8,128)(2,1)S(1)}, bf16[8,16,128]{2,1,0:T(8,128)(2,1)S(1)}, u32[]{:S(2)}, u32[]{:S(2)}) collective-permute-start(bf16[8,16,128]{2,1,0:T(8,128)(2,1)S(1)} %get-tuple-element.36), channel_id=1, source_target_pairs={{0,256},{128,384},{256,0},{384,128},{1,257},{129,385},{257,1},{385... | collective-permute-start | bytes 98312 | tf_op jit(solution)/shard_map/ppermute | solution.py:201
  33.8 7.1 %collective-permute-start = (bf16[8,16,128]{2,1,0:T(8,128)(2,1)S(1)}, bf16[8,16,128]{2,1,0:T(8,128)(2,1)S(1)}, u32[]{:S(2)}, u32[]{:S(2)}) collective-permute-start(bf16[8,16,128]{2,1,0:T(8,128)(2,1)S(1)} %get-tuple-element.36), channel_id=1, source_target_pairs={{0,128},{128,256},{256,384},{384,0},{1,129},{129,257},{257,385},{3... | collective-permute-start | bytes 98312 | tf_op jit(solution)/shard_map/ppermute | solution.py:201
  36.3 6.1 %collective-permute-start.2 = (bf16[8,16,128]{2,1,0:T(8,128)(2,1)S(1)}, bf16[8,16,128]{2,1,0:T(8,128)(2,1)S(1)}, u32[]{:S(2)}, u32[]{:S(2)}) collective-permute-start(bf16[8,16,128]{2,1,0:T(8,128)(2,1)S(1)} %get-tuple-element.36), channel_id=1, source_target_pairs={{0,384},{128,0},{256,128},{384,256},{1,385},{129,1},{257,129},{385... | collective-permute-start | bytes 98312 | tf_op jit(solution)/shard_map/ppermute | solution.py:201
  42.5 3.2 %collective-permute-start.3 = (bf16[4,8,16,128]{3,2,1,0:T(8,128)(2,1)S(1)}, bf16[4,8,16,128]{3,2,1,0:T(8,128)(2,1)S(1)}, u32[]{:S(2)}, u32[]{:S(2)}) collective-permute-start(bf16[4,8,16,128]{3,2,1,0:T(8,128)(2,1)S(1)} %pad_maximum_fusion.refs_2_), channel_id=1, source_target_pairs={{0,16},{16,0},{1,17},{17,1},{2,18},{18,2},{3,19},{19,3},{4,20},{20... | collective-permute-start | bytes 393224 | tf_op jit(solution)/shard_map/ppermute | solution.py:205
  54.6 25.1 %all-to-all-start.2 = ((bf16[8,8,16,128]{3,2,1,0:T(8,128)(2,1)}), bf16[8,8,16,128]{3,2,1,0:T(8,128)(2,1)S(1)}, u32[]{:S(2)}, u32[]{:S(2)}) async-start(bf16[8,8,16,128]{3,2,1,0:T(8,128)(2,1)} %get-tuple-element.21), calls=%async_computation.2 | async-start | bytes 524288 | tf_op jit(solution)/shard_map/all_to_all | solution.py:197
  61.8 3.2 %collective-permute-start.4 = (bf16[4,8,16,128]{3,2,1,0:T(8,128)(2,1)S(1)}, bf16[4,8,16,128]{3,2,1,0:T(8,128)(2,1)S(1)}, u32[]{:S(2)}, u32[]{:S(2)}) collective-permute-start(bf16[4,8,16,128]{3,2,1,0:T(8,128)(2,1)S(1)} %get-tuple-element.23), channel_id=1, source_target_pairs={{0,16},{16,0},{1,17},{17,1},{2,18},{18,2},{3,19},{19,3},{4,20},{20... | collective-permute-start | bytes 393224 | tf_op jit(solution)/shard_map/ppermute | solution.py:205
  65.0 10.8 %collective-permute-start.5 = (bf16[8,16,128]{2,1,0:T(8,128)(2,1)S(1)}, bf16[8,16,128]{2,1,0:T(8,128)(2,1)S(1)}, u32[]{:S(2)}, u32[]{:S(2)}) collective-permute-start(bf16[8,16,128]{2,1,0:T(8,128)(2,1)S(1)} %get-tuple-element.25), channel_id=1, source_target_pairs={{0,128},{128,256},{256,384},{384,0},{1,129},{129,257},{257,385},{3... | collective-permute-start | bytes 98312 | tf_op jit(solution)/shard_map/ppermute | solution.py:201
  67.0 8.8 %collective-permute-start.6 = (bf16[8,16,128]{2,1,0:T(8,128)(2,1)S(1)}, bf16[8,16,128]{2,1,0:T(8,128)(2,1)S(1)}, u32[]{:S(2)}, u32[]{:S(2)}) collective-permute-start(bf16[8,16,128]{2,1,0:T(8,128)(2,1)S(1)} %get-tuple-element.26), channel_id=1, source_target_pairs={{0,256},{128,384},{256,0},{384,128},{1,257},{129,385},{257,1},{385... | collective-permute-start | bytes 98312 | tf_op jit(solution)/shard_map/ppermute | solution.py:201
  73.9 5.8 %collective-permute-start.7 = (bf16[8,16,128]{2,1,0:T(8,128)(2,1)S(1)}, bf16[8,16,128]{2,1,0:T(8,128)(2,1)S(1)}, u32[]{:S(2)}, u32[]{:S(2)}) collective-permute-start(bf16[8,16,128]{2,1,0:T(8,128)(2,1)S(1)} %get-tuple-element.27), channel_id=1, source_target_pairs={{0,384},{128,0},{256,128},{384,256},{1,385},{129,1},{257,129},{385... | collective-permute-start | bytes 98312 | tf_op jit(solution)/shard_map/ppermute | solution.py:201
  79.7 10.8 %copy-start = (bf16[64,256]{1,0:T(8,128)(2,1)S(1)}, bf16[64,256]{1,0:T(8,128)(2,1)}, u32[]{:S(2)}) copy-start(bf16[64,256]{1,0:T(8,128)(2,1)} %wm_ref.1) | copy-start | bytes 98308
  79.7 10.7 %copy-start.1 = (bf16[64,64]{1,0:T(8,128)(2,1)S(1)}, bf16[64,64]{1,0:T(8,128)(2,1)}, u32[]{:S(2)}) copy-start(bf16[64,64]{1,0:T(8,128)(2,1)} %wf_ref.1) | copy-start | bytes 24580
  79.8 10.7 %copy-start.2 = (f32[64,128]{1,0:T(8,128)S(1)}, f32[64,128]{1,0:T(8,128)}, u32[]{:S(2)}) copy-start(f32[64,128]{1,0:T(8,128)} %get-tuple-element.28.xhat_ref) | copy-start | bytes 98308
  79.8 10.7 %copy-start.3 = (f32[64,128]{1,0:T(8,128)S(1)}, f32[64,128]{1,0:T(8,128)}, u32[]{:S(2)}) copy-start(f32[64,128]{1,0:T(8,128)} %get-tuple-element.30.g_ref) | copy-start | bytes 98308
  79.8 10.7 %copy-start.4 = (f32[64,128]{1,0:T(8,128)S(1)}, f32[64,128]{1,0:T(8,128)}, u32[]{:S(2)}) copy-start(f32[64,128]{1,0:T(8,128)} %get-tuple-element.31.dg_ref) | copy-start | bytes 98308
  90.5 0.7 copy-start.5

commit v3 on v2

--- a/solution.py
+++ b/solution.py
@@ -15,14 +15,14 @@
 DEPTH = ("x", "zh", "core")
 RES = ("zl", "y")
 HEAD_AXES = ("zl", "zh")
-KEY_AXES = ("y",)
+KEY_AXES = ("zl", "zh", "y")
 
 
 def tdot(a, b, ca, cb):
     return lax.dot_general(a, b, (((ca,), (cb,)), ((), ())), preferred_element_type=jnp.float32)
 
 
-def project_kernel(x_hbm, rc_hbm, wm_hbm, wf_hbm, bias_hbm, pack_ref, xhat_ref, rstd_ref, g_ref, dg_ref,
+def project_kernel(x_hbm, rc_hbm, wm_hbm, wf_hbm, bias_hbm, kv_ref, pack_ref, save_ref,
                    x_ref, rc_ref, wm_ref, wf_ref, bias_ref, sems):
     pairs = [(x_hbm, x_ref), (wm_hbm, wm_ref), (rc_hbm, rc_ref), (wf_hbm, wf_ref), (bias_hbm, bias_ref)]
     copies = [pltpu.make_async_copy(a, b, sems.at[i]) for i, (a, b) in enumerate(pairs)]
@@ -38,14 +38,15 @@
     g = jax.nn.sigmoid(proj[192:256])
     d_gated = tdot(wf_ref[...], rc_ref[...], 1, 1)
     d_attn = d_gated * g
-    xhat_ref[...] = xhat
-    rstd_ref[...] = jnp.broadcast_to(rstd, rstd_ref.shape)
-    g_ref[...] = g
-    dg_ref[...] = d_gated
+    save_ref[...] = jnp.concatenate([xhat, g, d_gated, jnp.broadcast_to(rstd, (8, 128))], 0)
     for h in range(HEADS):
         lo, hi = h * HEAD_DIM, (h + 1) * HEAD_DIM
         b = bias_ref[h].astype(jnp.float32)
-        parts = [proj[lo:hi] * SCALE, d_attn[lo:hi], proj[64 + lo : 64 + hi], proj[128 + lo : 128 + hi]]
+        kv = jnp.concatenate([proj[64 + lo : 64 + hi], proj[128 + lo : 128 + hi]], 0)
+        kv = kv.astype(jnp.bfloat16)
+        for y in range(8):
+            kv_ref[h, y] = kv
+        parts = [proj[lo:hi] * SCALE, d_attn[lo:hi]]
         parts += [b[r : r + 1, c * 128 : c * 128 + 128] for r in range(2) for c in range(8)]
         pack_ref[h] = jnp.concatenate(parts, 0).astype(jnp.bfloat16)
 
@@ -55,8 +56,10 @@
     oq_ref, dkv_ref, keep_ref, give_ref = refs[4:8]
     wide_ref, bias_ref, acc_ref, tmp_ref = refs[8:]
     me_x, core = lax.axis_index("x"), lax.axis_index("core")
+    flip = me_x + 1 - 2 * lax.rem(me_x, 2)
+    order = [me_x, flip, 3 - me_x, 3 - flip]
     for k in range(4):
-        at = lax.rem(me_x + 4 - k, 4) * 2
+        at = order[k] * 2
         for h in range(8):
             wide_ref[at + core, h] = own_bias[k, h].astype(jnp.float32)
             wide_ref[at + 1 - core, h] = swap_bias[k, h].astype(jnp.float32)
@@ -77,7 +80,7 @@
         for s in range(2):
             lanes = slice(s * 64, s * 64 + 64)
             kv = jnp.concatenate(
-                [kv_ref[y, zl * 4 + dl][:, lanes] for zl in range(2) for y in range(8)], 1
+                [kv_ref[zl * 4 + dl, y][:, lanes] for zl in range(2) for y in range(8)], 1
             )
             qd = jnp.concatenate([pack_ref[zl * 4 + dl, 0:16][:, lanes] for zl in range(2)], 1)
             qd = qd.astype(jnp.float32)
@@ -111,7 +114,7 @@
             for y in range(8):
                 r = zl * 8 + y
                 part_y = slice(r * 64, r * 64 + 64)
-                dkv_ref[y, zl * 4 + dl] = jnp.concatenate([o[:, part_y] for o in dkv_pair], 1)
+                dkv_ref[zl * 4 + dl, y] = jnp.concatenate([o[:, part_y] for o in dkv_pair], 1)
     for zl in range(2):
         for x in range(4):
             for c in range(8):
@@ -122,55 +125,51 @@
                     at = (zh * 2 + half) * 16
                     wide_ref[x * 2 + half, zl * 4 + zh] = tmp_ref[at : at + 16]
     for k in range(4):
-        to = lax.rem(me_x + k, 4) * 2
+        to = order[k] * 2
         for h in range(8):
             keep_ref[k, h] = wide_ref[to + core, h].astype(jnp.bfloat16)
             give_ref[k, h] = wide_ref[to + 1 - core, h].astype(jnp.bfloat16)
 
 
-def join_kernel(keep_ref, got_ref, *out_refs):
-    for k in range(4):
+def join_kernel(keep_ref, got_ref, stay_ref, go_ref):
+    half = stay_ref.shape[0]
+    for k in range(2 * half):
         for h in range(HEADS):
             both = keep_ref[k, h].astype(jnp.float32) + got_ref[k, h].astype(jnp.float32)
-            out_refs[k][h] = both.astype(jnp.bfloat16)
-
-
-def total(blocks):
-    acc = blocks[0].astype(jnp.float32)
-    for block in blocks[1:]:
-        acc += block.astype(jnp.float32)
-    return acc.astype(jnp.bfloat16)
-
-
-def sum_kernel(*refs):
-    oq_ref, dkv_ref, db_refs, pack_ref = refs[0], refs[1], refs[2:6], refs[6]
+            out_ref = stay_ref if k < half else go_ref
+            out_ref[k % half, h] = both.astype(jnp.bfloat16)
+
+
+def pack_kernel(oq_ref, stay_ref, got_ref, pack_ref):
     for h in range(HEADS):
         pack_ref[h, 0:16] = oq_ref[h]
-        pack_ref[h, 16:32] = total([dkv_ref[y, h] for y in range(8)])
-        pack_ref[h, 32:48] = total([ref[h] for ref in db_refs])
-
-
-def finish_kernel(pack_ref, xhat_ref, rstd_ref, g_ref, dg_ref, wm_ref, wf_ref, up_ref, dx_ref, db_ref):
+        both = stay_ref[0, h].astype(jnp.float32) + got_ref[0, h].astype(jnp.float32)
+        pack_ref[h, 16:32] = both.astype(jnp.bfloat16)
+
+
+def finish_kernel(pack_ref, dkv_ref, save_ref, wm_ref, wf_ref, up_ref, dx_ref, db_ref):
     dq, dk, dv, attn = [], [], [], []
     for h in range(HEADS):
         own = pack_ref[h].astype(jnp.float32)
         dq.append(own[0:8] * SCALE)
         attn.append(own[8:16])
-        dk.append(own[16:24])
-        dv.append(own[24:32])
+        total = dkv_ref[h, 0].astype(jnp.float32)
+        for y in range(1, 8):
+            total += dkv_ref[h, y].astype(jnp.float32)
+        dk.append(total[0:8])
+        dv.append(total[8:16])
         for r in range(2):
             db_ref[h, r : r + 1] = jnp.concatenate(
-                [own[32 + r * 8 + c : 33 + r * 8 + c] for c in range(8)], 1
+                [own[16 + r * 8 + c : 17 + r * 8 + c] for c in range(8)], 1
             )
     attn = jnp.concatenate(attn, 0)
-    g = g_ref[...]
+    xhat, g, d_gated, rstd = save_ref[0:64], save_ref[64:128], save_ref[128:192], save_ref[192:193]
     gated = (g * attn).astype(jnp.bfloat16)
     up_ref[...] = tdot(gated, wf_ref[...], 0, 0).astype(jnp.bfloat16)
-    d_gate = dg_ref[...] * attn * g * (1.0 - g)
+    d_gate = d_gated * attn * g * (1.0 - g)
     d_proj = jnp.concatenate(dq + dk + dv + [d_gate], 0).astype(jnp.bfloat16)
     d_normed = tdot(wm_ref[...], d_proj, 1, 0)
-    xhat = xhat_ref[...]
-    dx = rstd_ref[0:1] * (
+    dx = rstd * (
         d_normed
         - jnp.mean(d_normed, 0, keepdims=True)
         - xhat * jnp.mean(d_normed * xhat, 0, keepdims=True)
@@ -197,20 +196,27 @@
     return lax.all_to_all(a, axes, 0, 0, tiled=True)
 
 
-def shift_x(a, k):
-    return lax.ppermute(a, "x", [(i, (i + k) % 4) for i in range(4)])
+def swap(a, axis, pairs):
+    return lax.ppermute(a, axis, pairs + [(j, i) for i, j in pairs])
+
+
+def swap_near(a):
+    return swap(a, "x", [(0, 1), (2, 3)])
+
+
+def swap_far(a):
+    return swap(a, "x", [(0, 3), (1, 2)])
 
 
 def swap_core(a):
-    return lax.ppermute(a, "core", [(0, 1), (1, 0)])
+    return swap(a, "core", [(0, 1)])
 
 
 def per_device(x, bias, wm, wf, rc):
     f32 = jnp.float32
-    pack, xhat, rstd, g, d_gated = call(
+    kv, pack, saved = call(
         project_kernel,
-        [shape(8, 48, 128), shape(64, 128, dtype=f32), shape(8, 128, dtype=f32),
-         shape(64, 128, dtype=f32), shape(64, 128, dtype=f32)],
+        [shape(8, 8, 16, 128), shape(8, 32, 128), shape(200, 128, dtype=f32)],
         x.reshape(128, 64), rc.reshape(128, 64), wm, wf, bias,
         scratch=[pltpu.VMEM((128, 64), jnp.bfloat16), pltpu.VMEM((128, 64), jnp.bfloat16),
                  pltpu.VMEM((64, 256), jnp.bfloat16), pltpu.VMEM((64, 64), jnp.bfloat16),
@@ -218,28 +224,29 @@
         space=pltpu.HBM, limit=60,
     )
     pack = exchange(pack, HEAD_AXES)
-    own = pack[:, 16:32]
-    kv = exchange(jnp.broadcast_to(own[None], (8,) + own.shape), KEY_AXES)
-    own = pack[:, 32:48]
-    own_bias = jnp.stack([own] + [shift_x(own, k) for k in range(1, 4)])
-    swap_bias = swap_core(own_bias)
-    block, quad, octet = shape(8, 16, 128), shape(4, 8, 16, 128), shape(8, 8, 16, 128)
+    kv, pack = lax.optimization_barrier((kv, pack))
+    kv = exchange(kv.reshape(64, 16, 128), KEY_AXES).reshape(8, 8, 16, 128)
+    own = pack[None, :, 16:32]
+    own = jnp.concatenate([own, swap_near(own)])
+    own = jnp.concatenate([own, swap_far(own)])
+    sibling = swap_core(own)
+    pair, quad, octet = shape(2, 8, 16, 128), shape(4, 8, 16, 128), shape(8, 8, 16, 128)
     oq, dkv, keep, give = call(
         attend_kernel,
-        [block, octet, quad, quad],
-        pack, kv, own_bias, swap_bias,
+        [shape(8, 16, 128), octet, quad, quad],
+        pack, kv, own, sibling,
         scratch=[pltpu.VMEM((8, 8, 16, 128), f32), pltpu.VMEM((128, 1024), f32),
                  pltpu.VMEM((128, 1024), f32), pltpu.VMEM((128, 128), f32)],
     )
-    dkv = exchange(dkv, KEY_AXES)
-    db = call(join_kernel, [block] * 4, keep, swap_core(give))
-    db = [db[0]] + [shift_x(db[k], k) for k in range(1, 4)]
-    (back,) = call(sum_kernel, [shape(8, 48, 128)], oq, dkv, *db)
+    dkv = exchange(dkv.reshape(64, 16, 128), KEY_AXES).reshape(8, 8, 16, 128)
+    stay, go = call(join_kernel, [pair] * 2, keep, swap_core(give))
+    stay, go = call(join_kernel, [shape(1, 8, 16, 128)] * 2, stay, swap_far(go))
+    (back,) = call(pack_kernel, [shape(8, 32, 128)], oq, stay, swap_near(go))
     back = exchange(back, HEAD_AXES)
     update, dx, d_bias = call(
         finish_kernel,
         [shape(128, 64), shape(128, 64), shape(8, 2, 1024, dtype=f32)],
-        back, xhat, rstd, g, d_gated, wm, wf,
+        back, dkv, saved, wm, wf,
     )
     return update.reshape(2, 64, 64), dx.reshape(2, 64, 64), d_bias
 

time: 92.9 us -> 109 us (1.17)
  the two profiles are of different devices: /device:TPU:8 before, /device:TPU:6 now
where the time goes in v3:
time: 109 us; the launch traced here: 108 us
  blocking collectives  54.9 us (50%)
  starting transfers between devices  22.1 us (20%)
  waiting for transfers between devices  19.4 us (18%)
  Pallas kernels  11.1 us (10%)
    all_to_all x3, blocking collectives, exchange(): return lax.all_to_all(a, axes, 0, 0, tiled=True)  54.9 us
    ppermute x6, waiting for transfers between devices, swap(): return lax.ppermute(a, axis, pairs + [(j, i) for i, j in pairs])  19.4 us
    ppermute x6, starting transfers between devices, swap(): return lax.ppermute(a, axis, pairs + [(j, i) for i, j in pairs])  13.4 us
    pallas_call x6, Pallas kernels, call(): pl.pallas_call(kernel, out_shape=outs, in_specs=[pl.BlockSpec(memory_spac...  11.1 us
    all_to_all x1, starting transfers between devices, exchange(): return lax.all_to_all(a, axes, 0, 0, tiled=True)  8.71 us
  transfers between devices with their start and end apart: 7, of which 6 were waited for; matrix products, arithmetic and copies ran while one was open for 0% of the time, Pallas kernels for 0%

profile of v3, /device:TPU:6, one launch (start us, length us, event | category | flops | bytes accessed | tf_op | source)
XLA Modules:
  0.0 108.3 jit_solution(4562992928385222896)
XLA Ops:
  0.6 1.9 %shard_map.76 = (bf16[8,8,16,128]{3,2,1,0:T(8,128)(2,1)}, bf16[8,32,128]{2,1,0:T(8,128)(2,1)}, f32[200,128]{1,0:T(8,128)}) custom-call(bf16[128,64]{1,0:T(8,128)(2,1)} %bitcast.14, bf16[128,64]{1,0:T(8,128)(2,1)} %bitcast.15, bf16[64,256]{1,0:T(8,128)(2,1)} %wm_ref.1, bf16[64,64]{1,0:T(8,128)(2,1)} %wf_ref.1, bf16[8,2,1024]{2,1,0:T(2,128)(2,1)} %bias_hbm.1), custom_call_target="tpu_custom_call" | custom-call | tf_op jit(solution)/shard_map/pallas_call | solution.py:181
  2.5 18.1 %all_to_all.20.refs_0_ = bf16[8,32,128]{2,1,0:T(8,128)(2,1)S(1)} all-to-all(bf16[8,32,128]{2,1,0:T(8,128)(2,1)} %get-tuple-element.20), channel_id=1, replica_groups=mesh['x'=4,'zh'=4,'core'=2,'zl'=2,'y'=8] {'zl','zh'}, dimensions={0} | all-to-all | bytes 131072 | tf_op jit(solution)/shard_map/all_to_all | solution.py:196
  20.6 8.7 %all-to-all-start.1 = ((bf16[64,16,128]{2,1,0:T(8,128)(2,1)}), bf16[64,16,128]{2,1,0:T(8,128)(2,1)S(1)}, u32[]{:S(2)}, u32[]{:S(2)}) async-start(bf16[64,16,128]{2,1,0:T(8,128)(2,1)} %bitcast.13), calls=%async_computation.1 | async-start | bytes 524288 | tf_op jit(solution)/shard_map/all_to_all | solution.py:196
  29.4 2.7 %collective-permute-start = (bf16[1,8,16,128]{3,2,1,0:T(8,128)(2,1)S(1)}, bf16[1,8,16,128]{3,2,1,0:T(8,128)(2,1)S(1)}, u32[]{:S(2)}, u32[]{:S(2)}) collective-permute-start(bf16[1,8,16,128]{3,2,1,0:T(8,128)(2,1)S(1)} %slice_bitcast_fusion), channel_id=1, source_target_pairs={{0,128},{256,384},{128,0},{384,256},{1,129},{257,385},{129,1},{385... | collective-permute-start | bytes 98312 | tf_op jit(solution)/shard_map/ppermute | solution.py:200
  32.1 3.1 %collective-permute-done = bf16[1,8,16,128]{3,2,1,0:T(8,128)(2,1)S(1)} collective-permute-done((bf16[1,8,16,128]{3,2,1,0:T(8,128)(2,1)S(1)}, bf16[1,8,16,128]{3,2,1,0:T(8,128)(2,1)S(1)}, u32[]{:S(2)}, u32[]{:S(2)}) %collective-permute-start) | collective-permute-done | bytes 32800 | tf_op jit(solution)/shard_map/ppermute | solution.py:200
  35.2 2.4 %collective-permute-start.1 = (bf16[2,8,16,128]{3,2,1,0:T(8,128)(2,1)S(1)}, bf16[2,8,16,128]{3,2,1,0:T(8,128)(2,1)S(1)}, u32[]{:S(2)}, u32[]{:S(2)}) collective-permute-start(bf16[2,8,16,128]{3,2,1,0:T(8,128)(2,1)S(1)} %pad_maximum_fusion.1), channel_id=1, source_target_pairs={{0,384},{128,256},{384,0},{256,128},{1,385},{129,257},{385,1},{257... | collective-permute-start | bytes 196616 | tf_op jit(solution)/shard_map/ppermute | solution.py:200
  37.6 5.0 %collective-permute-done.1 = bf16[2,8,16,128]{3,2,1,0:T(8,128)(2,1)S(1)} collective-permute-done((bf16[2,8,16,128]{3,2,1,0:T(8,128)(2,1)S(1)}, bf16[2,8,16,128]{3,2,1,0:T(8,128)(2,1)S(1)}, u32[]{:S(2)}, u32[]{:S(2)}) %collective-permute-start.1) | collective-permute-done | bytes 65568 | tf_op jit(solution)/shard_map/ppermute | solution.py:200
  42.6 1.9 %collective-permute-start.2 = (bf16[4,8,16,128]{3,2,1,0:T(8,128)(2,1)S(1)}, bf16[4,8,16,128]{3,2,1,0:T(8,128)(2,1)S(1)}, u32[]{:S(2)}, u32[]{:S(2)}) collective-permute-start(bf16[4,8,16,128]{3,2,1,0:T(8,128)(2,1)S(1)} %pad_maximum_fusion.refs_2_), channel_id=1, source_target_pairs={{0,16},{16,0},{1,17},{17,1},{2,18},{18,2},{3,19},{19,3},{4,20},{20... | collective-permute-start | bytes 393224 | tf_op jit(solution)/shard_map/ppermute | solution.py:200
  44.5 1.3 %collective-permute-done.2.refs_3_ = bf16[4,8,16,128]{3,2,1,0:T(8,128)(2,1)S(1)} collective-permute-done((bf16[4,8,16,128]{3,2,1,0:T(8,128)(2,1)S(1)}, bf16[4,8,16,128]{3,2,1,0:T(8,128)(2,1)S(1)}, u32[]{:S(2)}, u32[]{:S(2)}) %collective-permute-start.2) | collective-permute-done | bytes 131104 | tf_op jit(solution)/shard_map/ppermute | solution.py:200
  45.8 0.0 all-to-all-done.1
  45.8 8.1 %shard_map.77 = (bf16[8,16,128]{2,1,0:T(8,128)(2,1)S(1)}, bf16[8,8,16,128]{3,2,1,0:T(8,128)(2,1)S(1)}, bf16[4,8,16,128]{3,2,1,0:T(8,128)(2,1)S(1)}, bf16[4,8,16,128]{3,2,1,0:T(8,128)(2,1)S(1)}) custom-call(bf16[8,32,128]{2,1,0:T(8,128)(2,1)S(1)} %all_to_all.20.refs_0_, bf16[8,8,16,128]{3,2,1,0:T(8,128)(2,1)S(1)} %bitcast.10, ...), custom_call_target="tpu_custom_call" | custom-call | tf_op jit(solution)/shard_map/pallas_call | solution.py:181
  54.0 2.1 %collective-permute-start.3 = (bf16[4,8,16,128]{3,2,1,0:T(8,128)(2,1)S(1)}, bf16[4,8,16,128]{3,2,1,0:T(8,128)(2,1)S(1)}, u32[]{:S(2)}, u32[]{:S(2)}) collective-permute-start(bf16[4,8,16,128]{3,2,1,0:T(8,128)(2,1)S(1)} %get-tuple-element.25), channel_id=1, source_target_pairs={{0,16},{16,0},{1,17},{17,1},{2,18},{18,2},{3,19},{19,3},{4,20},{20... | collective-permute-start | bytes 393224 | tf_op jit(solution)/shard_map/ppermute | solution.py:200
  56.0 1.2 %collective-permute-done.3.got_ref = bf16[4,8,16,128]{3,2,1,0:T(8,128)(2,1)S(1)} collective-permute-done((bf16[4,8,16,128]{3,2,1,0:T(8,128)(2,1)S(1)}, bf16[4,8,16,128]{3,2,1,0:T(8,128)(2,1)S(1)}, u32[]{:S(2)}, u32[]{:S(2)}) %collective-permute-start.3) | collective-permute-done | bytes 131104 | tf_op jit(solution)/shard_map/ppermute | solution.py:200
  57.2 2.4 %collective-permute-start.4 = (bf16[2,8,16,128]{3,2,1,0:T(8,128)(2,1)S(1)}, bf16[2,8,16,128]{3,2,1,0:T(8,128)(2,1)S(1)}, u32[]{:S(2)}, u32[]{:S(2)}) collective-permute-start(bf16[2,8,16,128]{3,2,1,0:T(8,128)(2,1)S(1)} %get-tuple-element.27), channel_id=1, source_target_pairs={{0,384},{128,256},{384,0},{256,128},{1,385},{129,257},{385,1},{257... | collective-permute-start | bytes 196616 | tf_op jit(solution)/shard_map/ppermute | solution.py:200
  59.6 5.0 %collective-permute-done.4.got_ref = bf16[2,8,16,128]{3,2,1,0:T(8,128)(2,1)S(1)} collective-permute-done((bf16[2,8,16,128]{3,2,1,0:T(8,128)(2,1)S(1)}, bf16[2,8,16,128]{3,2,1,0:T(8,128)(2,1)S(1)}, u32[]{:S(2)}, u32[]{:S(2)}) %collective-permute-start.4) | collective-permute-done | bytes 65568 | tf_op jit(solution)/shard_map/ppermute | solution.py:200
  64.6 1.9 %collective-permute-start.5 = (bf16[1,8,16,128]{3,2,1,0:T(8,128)(2,1)S(1)}, bf16[1,8,16,128]{3,2,1,0:T(8,128)(2,1)S(1)}, u32[]{:S(2)}, u32[]{:S(2)}) collective-permute-start(bf16[1,8,16,128]{3,2,1,0:T(8,128)(2,1)S(1)} %get-tuple-element.29), channel_id=1, source_target_pairs={{0,128},{256,384},{128,0},{384,256},{1,129},{257,385},{129,1},{385... | collective-permute-start | bytes 98312 | tf_op jit(solution)/shard_map/ppermute | solution.py:200
  66.6 3.9 %collective-permute-done.5.got_ref = bf16[1,8,16,128]{3,2,1,0:T(8,128)(2,1)S(1)} collective-permute-done((bf16[1,8,16,128]{3,2,1,0:T(8,128)(2,1)S(1)}, bf16[1,8,16,128]{3,2,1,0:T(8,128)(2,1)S(1)}, u32[]{:S(2)}, u32[]{:S(2)}) %collective-permute-start.5) | collective-permute-done | bytes 32800 | tf_op jit(solution)/shard_map/ppermute | solution.py:200
  70.4 14.3 %all_to_all.21.pack_ref = bf16[8,32,128]{2,1,0:T(8,128)(2,1)S(1)} all-to-all(bf16[8,32,128]{2,1,0:T(8,128)(2,1)S(1)} %shard_map.80), channel_id=1, replica_groups=mesh['x'=4,'zh'=4,'core'=2,'zl'=2,'y'=8] {'zl','zh'}, dimensions={0} | all-to-all | bytes 131072 | tf_op jit(solution)/shard_map/all_to_all | solution.py:196
  84.8 0.0 copy-start
  84.8 0.0 copy-start.1
  84.8 0.0 copy-start.2
  84.8 22.5 %all_to_all.22 = bf16[64,16,128]{2,1,0:T(8,128)(2,1)S(1)} all-to-all(bf16[64,16,128]{2,1,0:T(8,128)(2,1)S(1)} %bitcast.12), channel_id=1, replica_groups=mesh['x'=4,'zh'=4,'core'=2,'zl'=2,'y'=8] {'zl','zh','y'}, dimensions={0} | all-to-all | bytes 524288 | tf_op jit(solution)/shard_map/all_to_all | solution.py:196
  107.3 0.0 copy-done
  107.3 0.0 copy-done.1
  107.3 0.0 copy-done.2
  107.3 1.0 shard_map.81
  (6 shorter events, 0.1 us)
Async XLA Ops:
  20.6 25.2 %all-to-all-start.1 = ((bf16[64,16,128]{2,1,0:T(8,128)(2,1)}), bf16[64,16,128]{2,1,0:T(8,128)(2,1)S(1)}, u32[]{:S(2)}, u32[]{:S(2)}) async-start(bf16[64,16,128]{2,1,0:T(8,128)(2,1)} %bitcast.13), calls=%async_computation.1 | async-start | bytes 524288 | tf_op jit(solution)/shard_map/all_to_all | solution.py:196
  29.4 5.8 %collective-permute-start = (bf16[1,8,16,128]{3,2,1,0:T(8,128)(2,1)S(1)}, bf16[1,8,16,128]{3,2,1,0:T(8,128)(2,1)S(1)}, u32[]{:S(2)}, u32[]{:S(2)}) collective-permute-start(bf16[1,8,16,128]{3,2,1,0:T(8,128)(2,1)S(1)} %slice_bitcast_fusion), channel_id=1, source_target_pairs={{0,128},{256,384},{128,0},{384,256},{1,129},{257,385},{129,1},{385... | collective-permute-start | bytes 98312 | tf_op jit(solution)/shard_map/ppermute | solution.py:200
  35.2 7.4 %collective-permute-start.1 = (bf16[2,8,16,128]{3,2,1,0:T(8,128)(2,1)S(1)}, bf16[2,8,16,128]{3,2,1,0:T(8,128)(2,1)S(1)}, u32[]{:S(2)}, u32[]{:S(2)}) collective-permute-start(bf16[2,8,16,128]{3,2,1,0:T(8,128)(2,1)S(1)} %pad_maximum_fusion.1), channel_id=1, source_target_pairs={{0,384},{128,256},{384,0},{256,128},{1,385},{129,257},{385,1},{257... | collective-permute-start | bytes 196616 | tf_op jit(solution)/shard_map/ppermute | solution.py:200
  42.6 3.2 %collective-permute-start.2 = (bf16[4,8,16,128]{3,2,1,0:T(8,128)(2,1)S(1)}, bf16[4,8,16,128]{3,2,1,0:T(8,128)(2,1)S(1)}, u32[]{:S(2)}, u32[]{:S(2)}) collective-permute-start(bf16[4,8,16,128]{3,2,1,0:T(8,128)(2,1)S(1)} %pad_maximum_fusion.refs_2_), channel_id=1, source_target_pairs={{0,16},{16,0},{1,17},{17,1},{2,18},{18,2},{3,19},{19,3},{4,20},{20... | collective-permute-start | bytes 393224 | tf_op jit(solution)/shard_map/ppermute | solution.py:200
  54.0 3.2 %collective-permute-start.3 = (bf16[4,8,16,128]{3,2,1,0:T(8,128)(2,1)S(1)}, bf16[4,8,16,128]{3,2,1,0:T(8,128)(2,1)S(1)}, u32[]{:S(2)}, u32[]{:S(2)}) collective-permute-start(bf16[4,8,16,128]{3,2,1,0:T(8,128)(2,1)S(1)} %get-tuple-element.25), channel_id=1, source_target_pairs={{0,16},{16,0},{1,17},{17,1},{2,18},{18,2},{3,19},{19,3},{4,20},{20... | collective-permute-start | bytes 393224 | tf_op jit(solution)/shard_map/ppermute | solution.py:200
  57.2 7.4 %collective-permute-start.4 = (bf16[2,8,16,128]{3,2,1,0:T(8,128)(2,1)S(1)}, bf16[2,8,16,128]{3,2,1,0:T(8,128)(2,1)S(1)}, u32[]{:S(2)}, u32[]{:S(2)}) collective-permute-start(bf16[2,8,16,128]{3,2,1,0:T(8,128)(2,1)S(1)} %get-tuple-element.27), channel_id=1, source_target_pairs={{0,384},{128,256},{384,0},{256,128},{1,385},{129,257},{385,1},{257... | collective-permute-start | bytes 196616 | tf_op jit(solution)/shard_map/ppermute | solution.py:200
  64.6 5.8 %collective-permute-start.5 = (bf16[1,8,16,128]{3,2,1,0:T(8,128)(2,1)S(1)}, bf16[1,8,16,128]{3,2,1,0:T(8,128)(2,1)S(1)}, u32[]{:S(2)}, u32[]{:S(2)}) collective-permute-start(bf16[1,8,16,128]{3,2,1,0:T(8,128)(2,1)S(1)} %get-tuple-element.29), channel_id=1, source_target_pairs={{0,128},{256,384},{128,0},{384,256},{1,129},{257,385},{129,1},{385... | collective-permute-start | bytes 98312 | tf_op jit(solution)/shard_map/ppermute | solution.py:200
  84.8 22.5 %copy-start = (bf16[64,256]{1,0:T(8,128)(2,1)S(1)}, bf16[64,256]{1,0:T(8,128)(2,1)}, u32[]{:S(2)}) copy-start(bf16[64,256]{1,0:T(8,128)(2,1)} %wm_ref.1) | copy-start | bytes 98308
  84.8 22.5 %copy-start.1 = (f32[200,128]{1,0:T(8,128)S(1)}, f32[200,128]{1,0:T(8,128)}, u32[]{:S(2)}) copy-start(f32[200,128]{1,0:T(8,128)} %get-tuple-element.31.save_ref) | copy-start | bytes 307204
  84.8 22.5 %copy-start.2 = (bf16[64,64]{1,0:T(8,128)(2,1)S(1)}, bf16[64,64]{1,0:T(8,128)(2,1)}, u32[]{:S(2)}) copy-start(bf16[64,64]{1,0:T(8,128)(2,1)} %wf_ref.1) | copy-start | bytes 24580

commit v4 on v1

v4 whole, which is shorter than its diff:
```python
import math

import jax
import jax.numpy as jnp
from jax import lax
from jax.experimental import pallas as pl
from jax.experimental.pallas import tpu as pltpu
from jax.sharding import Mesh, PartitionSpec as P

HEADS = 8
HEAD_DIM = 8
EPS = 1e-05
SCALE = 1.0 / math.sqrt(HEAD_DIM)

DEPTH = ("x", "zh", "core")
RES = ("zl", "y")
HEAD_AXES = ("zl", "zh")
KEY_AXES = ("y",)
ROW_AXES = ("x", "core")


def tdot(a, b, ca, cb):
    return lax.dot_general(a, b, (((ca,), (cb,)), ((), ())), preferred_element_type=jnp.float32)


def project_kernel(x_hbm, rc_hbm, wm_hbm, wf_hbm, bias_hbm, pack_ref, save_ref,
                   x_ref, rc_ref, wm_ref, wf_ref, bias_ref, sems):
    pairs = [(x_hbm, x_ref), (wm_hbm, wm_ref), (rc_hbm, rc_ref), (wf_hbm, wf_ref), (bias_hbm, bias_ref)]
    copies = [pltpu.make_async_copy(a, b, sems.at[i]) for i, (a, b) in enumerate(pairs)]
    for copy in copies:
        copy.start()
    for copy in copies:
        copy.wait()
    x = x_ref[...].astype(jnp.float32).T
    cent = x - jnp.mean(x, 0, keepdims=True)
    rstd = lax.rsqrt(jnp.mean(cent * cent, 0, keepdims=True) + EPS)
    xhat = cent * rstd
    proj = tdot(wm_ref[...], xhat.astype(jnp.bfloat16), 0, 0)
    g = jax.nn.sigmoid(proj[192:256])
    d_gated = tdot(wf_ref[...], rc_ref[...], 1, 1)
    d_attn = d_gated * g
    save_ref[...] = jnp.concatenate([xhat, g, d_gated, jnp.broadcast_to(rstd, (8, 128))], 0)
    for h in range(HEADS):
        lo, hi = h * HEAD_DIM, (h + 1) * HEAD_DIM
        b = bias_ref[h].astype(jnp.float32)
        parts = [proj[lo:hi] * SCALE, d_attn[lo:hi], proj[64 + lo : 64 + hi], proj[128 + lo : 128 + hi]]
        parts += [b[r : r + 1, c * 128 : c * 128 + 128] for r in range(2) for c in range(8)]
        pack_ref[h] = jnp.concatenate(parts, 0).astype(jnp.bfloat16)


def sequence_operands(pack_ref, kv_ref, dl, s):
    lanes = slice(s * 64, s * 64 + 64)
    kv = jnp.concatenate([kv_ref[y, zl * 4 + dl][:, lanes] for zl in range(2) for y in range(8)], 1)
    qd = jnp.concatenate([pack_ref[zl * 4 + dl, 0:16][:, lanes] for zl in range(2)], 1)
    qd = qd.astype(jnp.float32)
    first = lax.broadcasted_iota(jnp.int32, (16, 128), 0) < HEAD_DIM
    return kv, jnp.where(first, qd, 0.0), jnp.where(first, 0.0, qd), first


def score_kernel(pack_ref, kv_ref, own_ref, sibling_ref, p_ref, ds_ref, attn_ref, db_ref,
                 wide_ref, bias_ref, acc_ref, tmp_ref):
    core = lax.axis_index("core")
    for x in range(4):
        for h in range(8):
            wide_ref[x * 2 + core, h] = own_ref[x, h].astype(jnp.float32)
            wide_ref[x * 2 + 1 - core, h] = sibling_ref[x, h].astype(jnp.float32)
    for zl in range(2):
        for x in range(4):
            for zh in range(4):
                for half in range(2):
                    at = (zh * 2 + half) * 16
                    tmp_ref[at : at + 16] = wide_ref[x * 2 + half, zl * 4 + zh]
            for c in range(8):
                at = (zl * 4 + x) * 16
                bias_ref[at : at + 16, c * 128 : c * 128 + 128] = tmp_ref[pl.ds(c, 16, stride=8)]
    rows = lax.broadcasted_iota(jnp.int32, (16, 128), 0)
    ones = jnp.ones((16, 1024), jnp.bfloat16)
    for dl in range(4):
        for s in range(2):
            kv, q, d, first = sequence_operands(pack_ref, kv_ref, dl, s)
            scores = tdot(q.astype(jnp.bfloat16), kv, 0, 0) + bias_ref[...]
            e = jnp.exp(scores - jnp.max(scores, 1, keepdims=True))
            p = e * (1.0 / jnp.sum(e, 1, keepdims=True))
            p_bf = p.astype(jnp.bfloat16)
            attn = tdot(kv, p_bf, 1, 1)
            delta = -jnp.sum(d * attn, 0, keepdims=True)
            hi = delta.astype(jnp.bfloat16).astype(jnp.float32)
            mid = (delta - hi).astype(jnp.bfloat16).astype(jnp.float32)
            low = delta - hi - mid
            tail = jnp.where(rows == 0, hi, jnp.where(rows == 1, mid, jnp.where(rows == 2, low, 0.0)))
            lhs = jnp.concatenate([d, tail], 0).astype(jnp.bfloat16)
            ds = p * tdot(lhs, jnp.concatenate([kv, ones], 0), 0, 0)
            n = dl * 2 + s
            p_ref[n] = p_bf
            ds_ref[n] = ds.astype(jnp.bfloat16)
            attn_ref[n] = attn
            if n == 0:
                acc_ref[...] = ds
            else:
                acc_ref[...] += ds
    for zl in range(2):
        for x in range(4):
            for c in range(8):
                at = (zl * 4 + x) * 16
                tmp_ref[pl.ds(c, 16, stride=8)] = acc_ref[at : at + 16, c * 128 : c * 128 + 128]
            for zh in range(4):
                for half in range(2):
                    at = (zh * 2 + half) * 16
                    db_ref[x * 2 + half, zl * 4 + zh] = tmp_ref[at : at + 16].astype(jnp.bfloat16)


def gradient_kernel(pack_ref, kv_ref, p_ref, ds_ref, attn_ref, oq_ref, dkv_ref):
    for dl in range(4):
        dkv_pair, out_pair = [], []
        for s in range(2):
            kv, q, d, first = sequence_operands(pack_ref, kv_ref, dl, s)
            n = dl * 2 + s
            ds, p = ds_ref[n], p_ref[n]
            dq = tdot(kv, ds, 1, 1)
            lhs = jnp.concatenate([q, d], 1).astype(jnp.bfloat16)
            dkv = tdot(lhs, jnp.concatenate([ds, p], 0), 1, 0)
            dkv_pair.append(dkv.astype(jnp.bfloat16))
            out_pair.append(jnp.where(first, dq, attn_ref[n]).astype(jnp.bfloat16))
        for zl in range(2):
            part = slice(zl * 64, zl * 64 + 64)
            oq_ref[zl * 4 + dl] = jnp.concatenate([o[:, part] for o in out_pair], 1)
            for y in range(8):
                r = zl * 8 + y
                part_y = slice(r * 64, r * 64 + 64)
                dkv_ref[y, zl * 4 + dl] = jnp.concatenate([o[:, part_y] for o in dkv_pair], 1)


def total(ref, h):
    acc = ref[0, h].astype(jnp.float32)
    for i in range(1, 8):
        acc += ref[i, h].astype(jnp.float32)
    return acc.astype(jnp.bfloat16)


def sum_kernel(oq_ref, dkv_ref, db_ref, pack_ref):
    for h in range(HEADS):
        pack_ref[h, 0:16] = oq_ref[h]
        pack_ref[h, 16:32] = total(dkv_ref, h)
        pack_ref[h, 32:48] = total(db_ref, h)


def finish_kernel(pack_ref, save_ref, wm_ref, wf_ref, up_ref, dx_ref, db_ref):
    dq, dk, dv, attn = [], [], [], []
    for h in range(HEADS):
        own = pack_ref[h].astype(jnp.float32)
        dq.append(own[0:8] * SCALE)
        attn.append(own[8:16])
        dk.append(own[16:24])
        dv.append(own[24:32])
        for r in range(2):
            db_ref[h, r : r + 1] = jnp.concatenate(
                [own[32 + r * 8 + c : 33 + r * 8 + c] for c in range(8)], 1
            )
    attn = jnp.concatenate(attn, 0)
    xhat, g, d_gated, rstd = save_ref[0:64], save_ref[64:128], save_ref[128:192], save_ref[192:193]
    gated = (g * attn).astype(jnp.bfloat16)
    up_ref[...] = tdot(gated, wf_ref[...], 0, 0).astype(jnp.bfloat16)
    d_gate = d_gated * attn * g * (1.0 - g)
    d_proj = jnp.concatenate(dq + dk + dv + [d_gate], 0).astype(jnp.bfloat16)
    d_normed = tdot(wm_ref[...], d_proj, 1, 0)
    dx = rstd * (
        d_normed
        - jnp.mean(d_normed, 0, keepdims=True)
        - xhat * jnp.mean(d_normed * xhat, 0, keepdims=True)
    )
    dx_ref[...] = dx.T.astype(jnp.bfloat16)


def call(kernel, outs, *args, scratch=(), space=pltpu.VMEM, limit=40):
    return pl.pallas_call(
        kernel,
        out_shape=outs,
        in_specs=[pl.BlockSpec(memory_space=space)] * len(args),
        out_specs=[pl.BlockSpec(memory_space=pltpu.VMEM)] * len(outs),
        scratch_shapes=list(scratch),
        compiler_params=pltpu.CompilerParams(vmem_limit_bytes=limit * 1024 * 1024),
    )(*args)


def shape(*dims, dtype=jnp.bfloat16):
    return jax.ShapeDtypeStruct(dims, dtype)


def exchange(a, axes):
    return lax.all_to_all(a, axes, 0, 0, tiled=True)


def spread(a):
    return jnp.broadcast_to(a[None], (8,) + a.shape)


def per_device(x, bias, wm, wf, rc):
    f32 = jnp.float32
    pack, saved = call(
        project_kernel,
        [shape(8, 48, 128), shape(200, 128, dtype=f32)],
        x.reshape(128, 64), rc.reshape(128, 64), wm, wf, bias,
        scratch=[pltpu.VMEM((128, 64), jnp.bfloat16), pltpu.VMEM((128, 64), jnp.bfloat16),
                 pltpu.VMEM((64, 256), jnp.bfloat16), pltpu.VMEM((64, 64), jnp.bfloat16),
                 pltpu.VMEM((8, 2, 1024), jnp.bfloat16), pltpu.SemaphoreType.DMA((5,))],
        space=pltpu.HBM, limit=60,
    )
    pack = exchange(pack, HEAD_AXES)
    kv = exchange(spread(pack[:, 16:32]), KEY_AXES)
    own = lax.all_gather(pack[:, 32:48], "x")
    sibling = lax.ppermute(own, "core", [(0, 1), (1, 0)])
    octet, plane = shape(8, 8, 16, 128), pltpu.VMEM((128, 1024), f32)
    p, ds, attn, db = call(
        score_kernel,
        [shape(8, 128, 1024), shape(8, 128, 1024), shape(8, 16, 128, dtype=f32), octet],
        pack, kv, own, sibling,
        scratch=[pltpu.VMEM((8, 8, 16, 128), f32), plane, plane, pltpu.VMEM((128, 128), f32)],
    )
    db = exchange(db, ROW_AXES)
    oq, dkv = call(gradient_kernel, [shape(8, 16, 128), octet], pack, kv, p, ds, attn)
    dkv = exchange(dkv, KEY_AXES)
    (back,) = call(sum_kernel, [shape(8, 48, 128)], oq, dkv, db)
    back = exchange(back, HEAD_AXES)
    update, dx, d_bias = call(
        finish_kernel,
        [shape(128, 64), shape(128, 64), shape(8, 2, 1024, dtype=f32)],
        back, saved, wm, wf,
    )
    return update.reshape(2, 64, 64), dx.reshape(2, 64, 64), d_bias


def solution(mesh):
    fine = Mesh(mesh.devices.reshape(4, 4, 2, 2, 8), DEPTH + RES)
    tokens = P(DEPTH, RES, None)
    rows = P(None, RES + DEPTH, None)
    return jax.shard_map(
        per_device,
        mesh=fine,
        in_specs=(tokens, rows, P(), P(), tokens),
        out_specs=(tokens, tokens, rows),
        check_vma=False,
    )
```

time: 94.9 us -> 93.8 us (0.988)
  blocking collectives: 81.3 us -> 59.1 us
  starting transfers between devices: 0 us -> 13.5 us
  waiting for transfers between devices: 0 us -> 3.9 us
  local copies, waits for them, and re-layouts: 0.75 us -> 3.69 us
    all_to_all x6 -> x3, blocking collectives: 81.3 us -> 47.1 us  [exchange(): return lax.all_to_all(a, axes, 0, 0, tiled=True)]
    all_gather x0 -> x1, blocking collectives: none -> 12 us  [per_device(): own = lax.all_gather(pack[:, 32:48], 'x')]
    all_to_all x0 -> x2, starting transfers between devices: none -> 11.6 us  [exchange(): return lax.all_to_all(a, axes, 0, 0, tiled=True)]
    all_to_all x0 -> x2, waiting for transfers between devices: none -> 2.58 us  [exchange(): return lax.all_to_all(a, axes, 0, 0, tiled=True)]
    unnamed x12 -> x10, local copies, waits for them, and re-layouts: 0.68 us -> 2.94 us
    ppermute x0 -> x1, starting transfers between devices: none -> 1.91 us  [per_device(): sibling = lax.ppermute(own, 'core', [(0, 1), (1, 0)])]
    ppermute x0 -> x1, waiting for transfers between devices: none -> 1.31 us  [per_device(): sibling = lax.ppermute(own, 'core', [(0, 1), (1, 0)])]
    pallas_call x4 -> x5, Pallas kernels: 10.9 us -> 11.7 us  [call(): pl.pallas_call(kernel, out_shape=outs, in_specs=[pl.BlockSpec(memory_spac...]
  transfers between devices with their start and end apart: 0 -> 3, of which waited for: 0 -> 2; matrix products, arithmetic and copies ran while one was open for 0% -> 0% of each run, Pallas kernels for 0% -> 1%
where the time goes in v4:
time: 93.8 us; the launch traced here: 92.6 us
  blocking collectives  59.1 us (63%)
  starting transfers between devices  13.5 us (14%)
  Pallas kernels  11.7 us (12%)
  waiting for transfers between devices  3.9 us (4%)
  local copies, waits for them, and re-layouts  3.69 us (4%)
    all_to_all x3, blocking collectives, exchange(): return lax.all_to_all(a, axes, 0, 0, tiled=True)  47.1 us
    all_gather x1, blocking collectives, per_device(): own = lax.all_gather(pack[:, 32:48], 'x')  12 us
    pallas_call x5, Pallas kernels, call(): pl.pallas_call(kernel, out_shape=outs, in_specs=[pl.BlockSpec(memory_spac...  11.7 us
    all_to_all x2, starting transfers between devices, exchange(): return lax.all_to_all(a, axes, 0, 0, tiled=True)  11.6 us
    unnamed x10, local copies, waits for them, and re-layouts  2.94 us
    all_to_all x2, waiting for transfers between devices, exchange(): return lax.all_to_all(a, axes, 0, 0, tiled=True)  2.58 us
    ppermute x1, starting transfers between devices, per_device(): sibling = lax.ppermute(own, 'core', [(0, 1), (1, 0)])  1.91 us
  transfers between devices with their start and end apart: 3, of which 2 were waited for; matrix products, arithmetic and copies ran while one was open for 0% of the time, Pallas kernels for 1%

profile of v4, /device:TPU:6, one launch (start us, length us, event | category | flops | bytes accessed | tf_op | source)
XLA Modules:
  0.0 92.6 jit_solution(14131833643782167178)
XLA Ops:
  0.6 1.8 %shard_map.76 = (bf16[8,48,128]{2,1,0:T(8,128)(2,1)}, f32[200,128]{1,0:T(8,128)}) custom-call(bf16[128,64]{1,0:T(8,128)(2,1)} %bitcast.7, bf16[128,64]{1,0:T(8,128)(2,1)} %bitcast.8, bf16[64,256]{1,0:T(8,128)(2,1)} %wm_ref.1, bf16[64,64]{1,0:T(8,128)(2,1)} %wf_ref.1, bf16[8,2,1024]{2,1,0:T(2,128)(2,1)} %bias_hbm.1), custom_call_target="tpu_custom_call" | custom-call | tf_op jit(solution)/shard_map/pallas_call | solution.py:175
  2.5 18.1 %all_to_all.25.pack_ref = bf16[8,48,128]{2,1,0:T(8,128)(2,1)S(1)} all-to-all(bf16[8,48,128]{2,1,0:T(8,128)(2,1)} %get-tuple-element.14), channel_id=1, replica_groups=mesh['x'=4,'zh'=4,'core'=2,'zl'=2,'y'=8] {'zl','zh'}, dimensions={0} | all-to-all | bytes 196608 | tf_op jit(solution)/shard_map/all_to_all | solution.py:190
  20.6 0.7 broadcast_in_dim.2
  21.3 7.1 %all-to-all-start.1 = ((bf16[8,8,16,128]{3,2,1,0:T(8,128)(2,1)}), bf16[8,8,16,128]{3,2,1,0:T(8,128)(2,1)S(1)}, u32[]{:S(2)}, u32[]{:S(2)}) async-start(bf16[8,8,16,128]{3,2,1,0:T(8,128)(2,1)} %broadcast_in_dim.2), calls=%async_computation.1 | async-start | bytes 524288 | tf_op jit(solution)/shard_map/all_to_all | solution.py:190
  28.4 12.0 %all-gather = bf16[32,16,128]{2,1,0:T(8,128)(2,1)S(1)} all-gather(bf16[8,16,128]{2,1,0:T(8,128)(2,1)S(1)} %get-tuple-element.25), channel_id=2, replica_groups=mesh['x'=4,'zh'=4,'core'=2,'zl'=2,'y'=8] {'x'}, dimensions={0}, use_global_device_ids=true | all-gather | bytes 163840 | tf_op jit(solution)/shard_map/all_gather | solution.py:210
  40.4 1.9 %collective-permute-start = (bf16[4,8,16,128]{3,2,1,0:T(8,128)(2,1)S(1)}, bf16[4,8,16,128]{3,2,1,0:T(8,128)(2,1)S(1)}, u32[]{:S(2)}, u32[]{:S(2)}) collective-permute-start(bf16[4,8,16,128]{3,2,1,0:T(8,128)(2,1)S(1)} %bitcast.5), channel_id=1, source_target_pairs={{0,16},{16,0},{1,17},{17,1},{2,18},{18,2},{3,19},{19,3},{4,20},{20... | collective-permute-start | bytes 393224 | tf_op jit(solution)/shard_map/ppermute | solution.py:211
  42.3 1.3 %collective-permute-done.sibling_ref = bf16[4,8,16,128]{3,2,1,0:T(8,128)(2,1)S(1)} collective-permute-done((bf16[4,8,16,128]{3,2,1,0:T(8,128)(2,1)S(1)}, bf16[4,8,16,128]{3,2,1,0:T(8,128)(2,1)S(1)}, u32[]{:S(2)}, u32[]{:S(2)}) %collective-permute-start) | collective-permute-done | bytes 131104 | tf_op jit(solution)/shard_map/ppermute | solution.py:211
  43.7 0.0 all-to-all-done.1.kv_ref
  43.7 7.5 %shard_map.77 = (bf16[8,128,1024]{2,1,0:T(8,128)(2,1)S(1)}, bf16[8,128,1024]{2,1,0:T(8,128)(2,1)S(1)}, f32[8,16,128]{2,1,0:T(8,128)S(1)}, bf16[8,8,16,128]{3,2,1,0:T(8,128)(2,1)}) custom-call(bf16[8,48,128]{2,1,0:T(8,128)(2,1)S(1)} %all_to_all.25.pack_ref, bf16[8,8,16,128]{3,2,1,0:T(8,128)(2,1)S(1)} %all-to-all-done.1.kv_ref, ...), custom_call_target="tpu_custom_call" | custom-call | tf_op jit(solution)/shard_map/pallas_call | solution.py:175
  51.2 0.0 copy-start
  51.2 1.3 %copy-done = bf16[8,128,1024]{2,1,0:T(8,128)(2,1)} copy-done((bf16[8,128,1024]{2,1,0:T(8,128)(2,1)}, bf16[8,128,1024]{2,1,0:T(8,128)(2,1)S(1)}, u32[]{:S(2)}) %copy-start) | copy-done | bytes 2097176
  52.5 4.5 %all-to-all-start.3 = ((bf16[8,8,16,128]{3,2,1,0:T(8,128)(2,1)}), bf16[8,8,16,128]{3,2,1,0:T(8,128)(2,1)S(1)}, u32[]{:S(2)}, u32[]{:S(2)}) async-start(bf16[8,8,16,128]{3,2,1,0:T(8,128)(2,1)} %get-tuple-element.20), calls=%async_computation.3 | async-start | bytes 524288 | tf_op jit(solution)/shard_map/all_to_all | solution.py:190
  57.0 0.0 copy-start.1
  57.1 1.6 %copy-done.1 = bf16[8,128,1024]{2,1,0:T(8,128)(2,1)S(1)} copy-done((bf16[8,128,1024]{2,1,0:T(8,128)(2,1)S(1)}, bf16[8,128,1024]{2,1,0:T(8,128)(2,1)}, u32[]{:S(2)}) %copy-start.1) | copy-done | bytes 2097176
  58.6 0.0 copy-start.2
  58.6 0.0 copy-start.3
  58.6 0.0 copy-start.4
  58.6 1.3 %shard_map.78 = (bf16[8,16,128]{2,1,0:T(8,128)(2,1)S(1)}, bf16[8,8,16,128]{3,2,1,0:T(8,128)(2,1)S(1)}) custom-call(bf16[8,48,128]{2,1,0:T(8,128)(2,1)S(1)} %all_to_all.25.pack_ref, bf16[8,8,16,128]{3,2,1,0:T(8,128)(2,1)S(1)} %all-to-all-done.1.kv_ref, bf16[8,128,1024]{2,1,0:T(8,128)(2,1)S(1)} %get-tuple-element.15.p_ref, ...), custom_call_target="tpu_custom_call" | custom-call | tf_op jit(solution)/shard_map/pallas_call | solution.py:175
  59.9 2.6 %all-to-all-done.3.db_ref = bf16[8,8,16,128]{3,2,1,0:T(8,128)(2,1)S(1)} async-done(((bf16[8,8,16,128]{3,2,1,0:T(8,128)(2,1)}), bf16[8,8,16,128]{3,2,1,0:T(8,128)(2,1)S(1)}, u32[]{:S(2)}, u32[]{:S(2)}) %all-to-all-start.3) | async-done | bytes 262176 | tf_op jit(solution)/shard_map/all_to_all | solution.py:190
  62.5 18.5 %all_to_all.26.dkv_ref = bf16[8,8,16,128]{3,2,1,0:T(8,128)(2,1)S(1)} all-to-all(bf16[8,8,16,128]{3,2,1,0:T(8,128)(2,1)S(1)} %get-tuple-element.19), channel_id=1, replica_groups=mesh['x'=4,'zh'=4,'core'=2,'zl'=2,'y'=8] {'y'}, dimensions={0} | all-to-all | bytes 524288 | tf_op jit(solution)/shard_map/all_to_all | solution.py:190
  81.0 0.1 shard_map.79
  81.1 10.5 %all_to_all.27.pack_ref = bf16[8,48,128]{2,1,0:T(8,128)(2,1)S(1)} all-to-all(bf16[8,48,128]{2,1,0:T(8,128)(2,1)S(1)} %shard_map.79), channel_id=1, replica_groups=mesh['x'=4,'zh'=4,'core'=2,'zl'=2,'y'=8] {'zl','zh'}, dimensions={0} | all-to-all | bytes 196608 | tf_op jit(solution)/shard_map/all_to_all | solution.py:190
  91.6 0.0 copy-done.2
  91.6 0.0 copy-done.3
  91.6 0.0 copy-done.4
  91.6 1.0 %shard_map.80 = (bf16[128,64]{1,0:T(8,128)(2,1)}, bf16[128,64]{1,0:T(8,128)(2,1)}, f32[8,2,1024]{2,1,0:T(2,128)}) custom-call(bf16[8,48,128]{2,1,0:T(8,128)(2,1)S(1)} %all_to_all.27.pack_ref, f32[200,128]{1,0:T(8,128)S(1)} %copy-done.3, bf16[64,256]{1,0:T(8,128)(2,1)S(1)} %copy-done.2, bf16[64,64]{1,0:T(8,128)(2,1)S(1)} %copy-done.4), custom_call_target="tpu_custom_call" | custom-call | tf_op jit(solution)/shard_map/pallas_call | solution.py:175
  (1 shorter events, 0.0 us)
Async XLA Ops:
  21.3 22.3 %all-to-all-start.1 = ((bf16[8,8,16,128]{3,2,1,0:T(8,128)(2,1)}), bf16[8,8,16,128]{3,2,1,0:T(8,128)(2,1)S(1)}, u32[]{:S(2)}, u32[]{:S(2)}) async-start(bf16[8,8,16,128]{3,2,1,0:T(8,128)(2,1)} %broadcast_in_dim.2), calls=%async_computation.1 | async-start | bytes 524288 | tf_op jit(solution)/shard_map/all_to_all | solution.py:190
  40.4 3.2 %collective-permute-start = (bf16[4,8,16,128]{3,2,1,0:T(8,128)(2,1)S(1)}, bf16[4,8,16,128]{3,2,1,0:T(8,128)(2,1)S(1)}, u32[]{:S(2)}, u32[]{:S(2)}) collective-permute-start(bf16[4,8,16,128]{3,2,1,0:T(8,128)(2,1)S(1)} %bitcast.5), channel_id=1, source_target_pairs={{0,16},{16,0},{1,17},{17,1},{2,18},{18,2},{3,19},{19,3},{4,20},{20... | collective-permute-start | bytes 393224 | tf_op jit(solution)/shard_map/ppermute | solution.py:211
  51.2 1.3 %copy-start = (bf16[8,128,1024]{2,1,0:T(8,128)(2,1)}, bf16[8,128,1024]{2,1,0:T(8,128)(2,1)S(1)}, u32[]{:S(2)}) copy-start(bf16[8,128,1024]{2,1,0:T(8,128)(2,1)S(1)} %get-tuple-element.16.ds_ref) | copy-start | bytes 6291460
  52.5 10.0 %all-to-all-start.3 = ((bf16[8,8,16,128]{3,2,1,0:T(8,128)(2,1)}), bf16[8,8,16,128]{3,2,1,0:T(8,128)(2,1)S(1)}, u32[]{:S(2)}, u32[]{:S(2)}) async-start(bf16[8,8,16,128]{3,2,1,0:T(8,128)(2,1)} %get-tuple-element.20), calls=%async_computation.3 | async-start | bytes 524288 | tf_op jit(solution)/shard_map/all_to_all | solution.py:190
  57.0 1.6 %copy-start.1 = (bf16[8,128,1024]{2,1,0:T(8,128)(2,1)S(1)}, bf16[8,128,1024]{2,1,0:T(8,128)(2,1)}, u32[]{:S(2)}) copy-start(bf16[8,128,1024]{2,1,0:T(8,128)(2,1)} %copy-done) | copy-start | bytes 6291460
  58.6 33.0 %copy-start.2 = (bf16[64,256]{1,0:T(8,128)(2,1)S(1)}, bf16[64,256]{1,0:T(8,128)(2,1)}, u32[]{:S(2)}) copy-start(bf16[64,256]{1,0:T(8,128)(2,1)} %wm_ref.1) | copy-start | bytes 98308
  58.6 33.0 %copy-start.3 = (f32[200,128]{1,0:T(8,128)S(1)}, f32[200,128]{1,0:T(8,128)}, u32[]{:S(2)}) copy-start(f32[200,128]{1,0:T(8,128)} %get-tuple-element.21.save_ref) | copy-start | bytes 307204
  58.6 33.0 %copy-start.4 = (bf16[64,64]{1,0:T(8,128)(2,1)S(1)}, bf16[64,64]{1,0:T(8,128)(2,1)}, u32[]{:S(2)}) copy-start(bf16[64,64]{1,0:T(8,128)(2,1)} %wf_ref.1) | copy-start | bytes 24580

commit v5 on v2

v5 whole, which is shorter than its diff:
```python
import math

import jax
import jax.numpy as jnp
from jax import lax
from jax.experimental import pallas as pl
from jax.experimental.pallas import tpu as pltpu
from jax.sharding import Mesh, PartitionSpec as P

HEADS = 8
HEAD_DIM = 8
EPS = 1e-05
SCALE = 1.0 / math.sqrt(HEAD_DIM)

DEPTH = ("x", "zh", "core")
RES = ("zl", "y")
HEAD_AXES = ("zl", "zh")
KEY_AXES = ("y",)
ROW_AXES = ("x", "core")
BLOCK = 32


def tdot(a, b, ca, cb):
    return lax.dot_general(a, b, (((ca,), (cb,)), ((), ())), preferred_element_type=jnp.float32)


def project_kernel(x_hbm, rc_hbm, wm_hbm, wf_hbm, bias_hbm, pack_ref, save_ref,
                   x_ref, rc_ref, wm_ref, wf_ref, bias_ref, sems):
    pairs = [(x_hbm, x_ref), (wm_hbm, wm_ref), (rc_hbm, rc_ref), (wf_hbm, wf_ref), (bias_hbm, bias_ref)]
    copies = [pltpu.make_async_copy(a, b, sems.at[i]) for i, (a, b) in enumerate(pairs)]
    for copy in copies:
        copy.start()
    for copy in copies:
        copy.wait()
    x = x_ref[...].astype(jnp.float32).T
    cent = x - jnp.mean(x, 0, keepdims=True)
    rstd = lax.rsqrt(jnp.mean(cent * cent, 0, keepdims=True) + EPS)
    xhat = cent * rstd
    proj = tdot(wm_ref[...], xhat.astype(jnp.bfloat16), 0, 0)
    g = jax.nn.sigmoid(proj[192:256])
    d_gated = tdot(wf_ref[...], rc_ref[...], 1, 1)
    d_attn = d_gated * g
    save_ref[...] = jnp.concatenate([xhat, g, d_gated, jnp.broadcast_to(rstd, (8, 128))], 0)
    for h in range(HEADS):
        lo, hi = h * HEAD_DIM, (h + 1) * HEAD_DIM
        b = bias_ref[h].astype(jnp.float32)
        parts = [proj[lo:hi] * SCALE, d_attn[lo:hi], proj[64 + lo : 64 + hi], proj[128 + lo : 128 + hi]]
        parts += [b[r : r + 1, c * 128 : c * 128 + 128] for r in range(2) for c in range(8)]
        pack_ref[h] = jnp.concatenate(parts, 0).astype(jnp.bfloat16)


def attend_kernel(pack_ref, kv_ref, own_ref, sibling_ref, dkv_ref, oq_ref, db_ref,
                  wide_ref, bias_ref, acc_ref, tmp_ref, pair_ref):
    me_x, core = lax.axis_index("x"), lax.axis_index("core")
    for k in range(4):
        at = lax.rem(me_x + 4 - k, 4) * 2
        for h in range(8):
            wide_ref[at + core, h] = own_ref[k, h].astype(jnp.float32)
            wide_ref[at + 1 - core, h] = sibling_ref[k, h].astype(jnp.float32)
    for zl in range(2):
        for x in range(4):
            for zh in range(4):
                for half in range(2):
                    at = (zh * 2 + half) * 16
                    tmp_ref[at : at + 16] = wide_ref[x * 2 + half, zl * 4 + zh]
            for c in range(8):
                at = (zl * 4 + x) * 16
                bias_ref[at : at + 16, c * 128 : c * 128 + 128] = tmp_ref[pl.ds(c, 16, stride=8)]
    upper = lax.broadcasted_iota(jnp.int32, (16, 128), 0) < HEAD_DIM
    left = lax.broadcasted_iota(jnp.int32, (128, 16), 1) < HEAD_DIM
    for dl in range(4):
        dkv_pair, out_pair = [], []
        for s in range(2):
            n = dl * 2 + s
            lanes = slice(s * 64, s * 64 + 64)
            kv = jnp.concatenate(
                [kv_ref[y, zl * 4 + dl][:, lanes] for zl in range(2) for y in range(8)], 1
            )
            qd = jnp.concatenate([pack_ref[zl * 4 + dl, 0:16][:, lanes] for zl in range(2)], 1)
            qd = qd.astype(jnp.float32)
            qd_rows = qd.T
            q_rows = jnp.where(left, qd_rows, 0.0).astype(jnp.bfloat16)
            d_rows = jnp.where(left, 0.0, qd_rows)
            d_bf = d_rows.astype(jnp.bfloat16)
            out_rows = []
            for at in range(0, 128, BLOCK):
                block = slice(at, at + BLOCK)
                scores = tdot(q_rows[block], kv, 1, 0) + bias_ref[block]
                e = jnp.exp(scores - jnp.max(scores, 1, keepdims=True))
                p = e * (1.0 / jnp.sum(e, 1, keepdims=True))
                p_bf = p.astype(jnp.bfloat16)
                pair_ref[n % 2, 128 + at : 128 + at + BLOCK] = p_bf
                attn = tdot(p_bf, kv, 1, 1)
                delta = jnp.sum(d_rows[block] * attn, 1, keepdims=True)
                ds = p * (tdot(d_bf[block], kv, 1, 0) - delta)
                ds_bf = ds.astype(jnp.bfloat16)
                pair_ref[n % 2, block] = ds_bf
                if n == 0:
                    acc_ref[block] = ds
                else:
                    acc_ref[block] += ds
                dq = tdot(ds_bf, kv, 1, 1)
                out_rows.append(jnp.where(left[block], dq, attn))
            lhs = jnp.concatenate([jnp.where(upper, qd, 0.0), jnp.where(upper, 0.0, qd)], 1)
            dkv_pair.append(tdot(lhs.astype(jnp.bfloat16), pair_ref[n % 2], 1, 0).astype(jnp.bfloat16))
            out_pair.append(jnp.concatenate(out_rows, 0).T.astype(jnp.bfloat16))
        for zl in range(2):
            part = slice(zl * 64, zl * 64 + 64)
            oq_ref[zl * 4 + dl] = jnp.concatenate([o[:, part] for o in out_pair], 1)
            for y in range(8):
                r = zl * 8 + y
                part_y = slice(r * 64, r * 64 + 64)
                dkv_ref[y, zl * 4 + dl] = jnp.concatenate([o[:, part_y] for o in dkv_pair], 1)
    for zl in range(2):
        for x in range(4):
            for c in range(8):
                at = (zl * 4 + x) * 16
                tmp_ref[pl.ds(c, 16, stride=8)] = acc_ref[at : at + 16, c * 128 : c * 128 + 128]
            for zh in range(4):
                for half in range(2):
                    at = (zh * 2 + half) * 16
                    db_ref[x * 2 + half, zl * 4 + zh] = tmp_ref[at : at + 16].astype(jnp.bfloat16)


def total(blocks):
    acc = blocks[0].astype(jnp.float32)
    for block in blocks[1:]:
        acc += block.astype(jnp.float32)
    return acc.astype(jnp.bfloat16)


def sum_kernel(oq_ref, dkv_ref, db_ref, pack_ref):
    for h in range(HEADS):
        pack_ref[h, 0:16] = oq_ref[h]
        pack_ref[h, 16:32] = total([dkv_ref[i, h] for i in range(8)])
        pack_ref[h, 32:48] = total([db_ref[i, h] for i in range(8)])


def finish_kernel(pack_ref, save_ref, wm_ref, wf_ref, up_ref, dx_ref, db_ref):
    dq, dk, dv, attn = [], [], [], []
    for h in range(HEADS):
        own = pack_ref[h].astype(jnp.float32)
        dq.append(own[0:8] * SCALE)
        attn.append(own[8:16])
        dk.append(own[16:24])
        dv.append(own[24:32])
        for r in range(2):
            db_ref[h, r : r + 1] = jnp.concatenate(
                [own[32 + r * 8 + c : 33 + r * 8 + c] for c in range(8)], 1
            )
    attn = jnp.concatenate(attn, 0)
    xhat, g, d_gated, rstd = save_ref[0:64], save_ref[64:128], save_ref[128:192], save_ref[192:193]
    gated = (g * attn).astype(jnp.bfloat16)
    up_ref[...] = tdot(gated, wf_ref[...], 0, 0).astype(jnp.bfloat16)
    d_gate = d_gated * attn * g * (1.0 - g)
    d_proj = jnp.concatenate(dq + dk + dv + [d_gate], 0).astype(jnp.bfloat16)
    d_normed = tdot(wm_ref[...], d_proj, 1, 0)
    dx = rstd * (
        d_normed
        - jnp.mean(d_normed, 0, keepdims=True)
        - xhat * jnp.mean(d_normed * xhat, 0, keepdims=True)
    )
    dx_ref[...] = dx.T.astype(jnp.bfloat16)


def call(kernel, outs, *args, scratch=(), space=pltpu.VMEM, limit=40):
    return pl.pallas_call(
        kernel,
        out_shape=outs,
        in_specs=[pl.BlockSpec(memory_space=space)] * len(args),
        out_specs=[pl.BlockSpec(memory_space=pltpu.VMEM)] * len(outs),
        scratch_shapes=list(scratch),
        compiler_params=pltpu.CompilerParams(vmem_limit_bytes=limit * 1024 * 1024),
    )(*args)


def shape(*dims, dtype=jnp.bfloat16):
    return jax.ShapeDtypeStruct(dims, dtype)


def exchange(a, axes):
    return lax.all_to_all(a, axes, 0, 0, tiled=True)


def shift_x(a, k):
    return lax.ppermute(a, "x", [(i, (i + k) % 4) for i in range(4)])


def swap_core(a):
    return lax.ppermute(a, "core", [(0, 1), (1, 0)])


def per_device(x, bias, wm, wf, rc):
    f32 = jnp.float32
    pack, saved = call(
        project_kernel,
        [shape(8, 48, 128), shape(200, 128, dtype=f32)],
        x.reshape(128, 64), rc.reshape(128, 64), wm, wf, bias,
        scratch=[pltpu.VMEM((128, 64), jnp.bfloat16), pltpu.VMEM((128, 64), jnp.bfloat16),
                 pltpu.VMEM((64, 256), jnp.bfloat16), pltpu.VMEM((64, 64), jnp.bfloat16),
                 pltpu.VMEM((8, 2, 1024), jnp.bfloat16), pltpu.SemaphoreType.DMA((5,))],
        space=pltpu.HBM, limit=60,
    )
    pack = exchange(pack, HEAD_AXES)
    own = pack[:, 16:32]
    kv = exchange(jnp.broadcast_to(own[None], (8,) + own.shape), KEY_AXES)
    own = pack[:, 32:48]
    own_bias = jnp.stack([own] + [shift_x(own, k) for k in range(1, 4)])
    swap_bias = swap_core(own_bias)
    octet, plane = shape(8, 8, 16, 128), pltpu.VMEM((128, 1024), f32)
    dkv, oq, db = call(
        attend_kernel,
        [octet, shape(8, 16, 128), octet],
        pack, kv, own_bias, swap_bias,
        scratch=[pltpu.VMEM((8, 8, 16, 128), f32), plane, plane, pltpu.VMEM((128, 128), f32),
                 pltpu.VMEM((2, 256, 1024), jnp.bfloat16)],
    )
    db = exchange(db, ROW_AXES)
    dkv = exchange(dkv, KEY_AXES)
    (back,) = call(sum_kernel, [shape(8, 48, 128)], oq, dkv, db)
    back = exchange(back, HEAD_AXES)
    update, dx, d_bias = call(
        finish_kernel,
        [shape(128, 64), shape(128, 64), shape(8, 2, 1024, dtype=f32)],
        back, saved, wm, wf,
    )
    return update.reshape(2, 64, 64), dx.reshape(2, 64, 64), d_bias


def solution(mesh):
    fine = Mesh(mesh.devices.reshape(4, 4, 2, 2, 8), DEPTH + RES)
    tokens = P(DEPTH, RES, None)
    rows = P(None, RES + DEPTH, None)
    return jax.shard_map(
        per_device,
        mesh=fine,
        in_specs=(tokens, rows, P(), P(), tokens),
        out_specs=(tokens, tokens, rows),
        check_vma=False,
    )
```

time: 92.9 us -> 99.3 us (1.069)
  the two profiles are of different devices: /device:TPU:8 before, /device:TPU:6 now
where the time goes in v5:
time: 99.3 us; the launch traced here: 98 us
  blocking collectives  57 us (57%)
  starting transfers between devices  18.2 us (18%)
  Pallas kernels  14.8 us (15%)
  waiting for transfers between devices  6.39 us (6%)
    all_to_all x4, blocking collectives, exchange(): return lax.all_to_all(a, axes, 0, 0, tiled=True)  57 us
    pallas_call x4, Pallas kernels, call(): pl.pallas_call(kernel, out_shape=outs, in_specs=[pl.BlockSpec(memory_spac...  14.8 us
    ppermute x3, starting transfers between devices, shift_x(): return lax.ppermute(a, 'x', [(i, (i + k) % 4) for i in range(4)])  9.23 us
    all_to_all x1, starting transfers between devices, exchange(): return lax.all_to_all(a, axes, 0, 0, tiled=True)  7.1 us
    ppermute x3, waiting for transfers between devices, shift_x(): return lax.ppermute(a, 'x', [(i, (i + k) % 4) for i in range(4)])  5.07 us
  transfers between devices with their start and end apart: 5, of which 2 were waited for; matrix products, arithmetic and copies ran while one was open for 0% of the time, Pallas kernels for 0%

profile of v5, /device:TPU:6, one launch (start us, length us, event | category | flops | bytes accessed | tf_op | source)
XLA Modules:
  0.0 98.0 jit_solution(21692165852419241)
XLA Ops:
  0.6 1.8 %shard_map.76 = (bf16[8,48,128]{2,1,0:T(8,128)(2,1)}, f32[200,128]{1,0:T(8,128)}) custom-call(bf16[128,64]{1,0:T(8,128)(2,1)} %bitcast.9, bf16[128,64]{1,0:T(8,128)(2,1)} %bitcast.10, bf16[64,256]{1,0:T(8,128)(2,1)} %wm_ref.1, bf16[64,64]{1,0:T(8,128)(2,1)} %wf_ref.1, bf16[8,2,1024]{2,1,0:T(2,128)(2,1)} %bias_hbm.1), custom_call_target="tpu_custom_call" | custom-call | tf_op jit(solution)/shard_map/pallas_call | solution.py:167
  2.5 18.1 %all_to_all.25.pack_ref = bf16[8,48,128]{2,1,0:T(8,128)(2,1)S(1)} all-to-all(bf16[8,48,128]{2,1,0:T(8,128)(2,1)} %get-tuple-element.11), channel_id=1, replica_groups=mesh['x'=4,'zh'=4,'core'=2,'zl'=2,'y'=8] {'zl','zh'}, dimensions={0} | all-to-all | bytes 196608 | tf_op jit(solution)/shard_map/all_to_all | solution.py:182
  20.6 0.7 broadcast_in_dim.2
  21.4 7.1 %all-to-all-start.1 = ((bf16[8,8,16,128]{3,2,1,0:T(8,128)(2,1)}), bf16[8,8,16,128]{3,2,1,0:T(8,128)(2,1)S(1)}, u32[]{:S(2)}, u32[]{:S(2)}) async-start(bf16[8,8,16,128]{3,2,1,0:T(8,128)(2,1)} %broadcast_in_dim.2), calls=%async_computation.1 | async-start | bytes 524288 | tf_op jit(solution)/shard_map/all_to_all | solution.py:182
  28.5 3.3 %collective-permute-start.1 = (bf16[8,16,128]{2,1,0:T(8,128)(2,1)S(1)}, bf16[8,16,128]{2,1,0:T(8,128)(2,1)S(1)}, u32[]{:S(2)}, u32[]{:S(2)}) collective-permute-start(bf16[8,16,128]{2,1,0:T(8,128)(2,1)S(1)} %get-tuple-element.20), channel_id=1, source_target_pairs={{0,256},{128,384},{256,0},{384,128},{1,257},{129,385},{257,1},{385... | collective-permute-start | bytes 98312 | tf_op jit(solution)/shard_map/ppermute | solution.py:186
  31.8 4.0 %collective-permute-start = (bf16[8,16,128]{2,1,0:T(8,128)(2,1)S(1)}, bf16[8,16,128]{2,1,0:T(8,128)(2,1)S(1)}, u32[]{:S(2)}, u32[]{:S(2)}) collective-permute-start(bf16[8,16,128]{2,1,0:T(8,128)(2,1)S(1)} %get-tuple-element.20), channel_id=1, source_target_pairs={{0,128},{128,256},{256,384},{384,0},{1,129},{129,257},{257,385},{3... | collective-permute-start | bytes 98312 | tf_op jit(solution)/shard_map/ppermute | solution.py:186
  35.8 1.9 %collective-permute-start.2 = (bf16[8,16,128]{2,1,0:T(8,128)(2,1)S(1)}, bf16[8,16,128]{2,1,0:T(8,128)(2,1)S(1)}, u32[]{:S(2)}, u32[]{:S(2)}) collective-permute-start(bf16[8,16,128]{2,1,0:T(8,128)(2,1)S(1)} %get-tuple-element.20), channel_id=1, source_target_pairs={{0,384},{128,0},{256,128},{384,256},{1,385},{129,1},{257,129},{385... | collective-permute-start | bytes 98312 | tf_op jit(solution)/shard_map/ppermute | solution.py:186
  37.7 0.0 collective-permute-done.1
  37.7 0.0 collective-permute-done
  37.7 5.1 %collective-permute-done.2 = bf16[8,16,128]{2,1,0:T(8,128)(2,1)S(1)} collective-permute-done((bf16[8,16,128]{2,1,0:T(8,128)(2,1)S(1)}, bf16[8,16,128]{2,1,0:T(8,128)(2,1)S(1)}, u32[]{:S(2)}, u32[]{:S(2)}) %collective-permute-start.2) | collective-permute-done | bytes 32800 | tf_op jit(solution)/shard_map/ppermute | solution.py:186
  42.8 1.9 %collective-permute-start.3 = (bf16[4,8,16,128]{3,2,1,0:T(8,128)(2,1)S(1)}, bf16[4,8,16,128]{3,2,1,0:T(8,128)(2,1)S(1)}, u32[]{:S(2)}, u32[]{:S(2)}) collective-permute-start(bf16[4,8,16,128]{3,2,1,0:T(8,128)(2,1)S(1)} %pad_maximum_fusion.own_ref), channel_id=1, source_target_pairs={{0,16},{16,0},{1,17},{17,1},{2,18},{18,2},{3,19},{19,3},{4,20},{20... | collective-permute-start | bytes 393224 | tf_op jit(solution)/shard_map/ppermute | solution.py:190
  44.8 1.3 %collective-permute-done.3.sibling_ref = bf16[4,8,16,128]{3,2,1,0:T(8,128)(2,1)S(1)} collective-permute-done((bf16[4,8,16,128]{3,2,1,0:T(8,128)(2,1)S(1)}, bf16[4,8,16,128]{3,2,1,0:T(8,128)(2,1)S(1)}, u32[]{:S(2)}, u32[]{:S(2)}) %collective-permute-start.3) | collective-permute-done | bytes 131104 | tf_op jit(solution)/shard_map/ppermute | solution.py:190
  46.1 0.0 all-to-all-done.1.kv_ref
  46.1 11.9 %shard_map.77 = (bf16[8,8,16,128]{3,2,1,0:T(8,128)(2,1)S(1)}, bf16[8,16,128]{2,1,0:T(8,128)(2,1)S(1)}, bf16[8,8,16,128]{3,2,1,0:T(8,128)(2,1)S(1)}) custom-call(bf16[8,48,128]{2,1,0:T(8,128)(2,1)S(1)} %all_to_all.25.pack_ref, bf16[8,8,16,128]{3,2,1,0:T(8,128)(2,1)S(1)} %all-to-all-done.1.kv_ref, bf16[4,8,16,128]{3,2,1,0:T(8,128)(2,1)S(1)} %pad_maximum_fusion.own_ref, ...), custom_call_target="tpu_custom_call" | custom-call | tf_op jit(solution)/shard_map/pallas_call | solution.py:167
  58.0 9.8 %all_to_all.26.db_ref = bf16[8,8,16,128]{3,2,1,0:T(8,128)(2,1)S(1)} all-to-all(bf16[8,8,16,128]{3,2,1,0:T(8,128)(2,1)S(1)} %get-tuple-element.14), channel_id=1, replica_groups=mesh['x'=4,'zh'=4,'core'=2,'zl'=2,'y'=8] {'x','core'}, dimensions={0} | all-to-all | bytes 524288 | tf_op jit(solution)/shard_map/all_to_all | solution.py:182
  67.8 18.5 %all_to_all.27.dkv_ref = bf16[8,8,16,128]{3,2,1,0:T(8,128)(2,1)S(1)} all-to-all(bf16[8,8,16,128]{3,2,1,0:T(8,128)(2,1)S(1)} %get-tuple-element.13), channel_id=1, replica_groups=mesh['x'=4,'zh'=4,'core'=2,'zl'=2,'y'=8] {'y'}, dimensions={0} | all-to-all | bytes 524288 | tf_op jit(solution)/shard_map/all_to_all | solution.py:182
  86.3 0.1 shard_map.78
  86.4 0.0 copy-start
  86.4 0.0 copy-start.1
  86.4 0.0 copy-start.2
  86.4 10.6 %all_to_all.28.pack_ref = bf16[8,48,128]{2,1,0:T(8,128)(2,1)S(1)} all-to-all(bf16[8,48,128]{2,1,0:T(8,128)(2,1)S(1)} %shard_map.78), channel_id=1, replica_groups=mesh['x'=4,'zh'=4,'core'=2,'zl'=2,'y'=8] {'zl','zh'}, dimensions={0} | all-to-all | bytes 196608 | tf_op jit(solution)/shard_map/all_to_all | solution.py:182
  97.0 0.0 copy-done
  97.0 0.0 copy-done.1
  97.0 0.0 copy-done.2
  97.0 1.0 shard_map.79
  (2 shorter events, 0.0 us)
Async XLA Ops:
  21.4 24.7 %all-to-all-start.1 = ((bf16[8,8,16,128]{3,2,1,0:T(8,128)(2,1)}), bf16[8,8,16,128]{3,2,1,0:T(8,128)(2,1)S(1)}, u32[]{:S(2)}, u32[]{:S(2)}) async-start(bf16[8,8,16,128]{3,2,1,0:T(8,128)(2,1)} %broadcast_in_dim.2), calls=%async_computation.1 | async-start | bytes 524288 | tf_op jit(solution)/shard_map/all_to_all | solution.py:182
  28.5 9.3 %collective-permute-start.1 = (bf16[8,16,128]{2,1,0:T(8,128)(2,1)S(1)}, bf16[8,16,128]{2,1,0:T(8,128)(2,1)S(1)}, u32[]{:S(2)}, u32[]{:S(2)}) collective-permute-start(bf16[8,16,128]{2,1,0:T(8,128)(2,1)S(1)} %get-tuple-element.20), channel_id=1, source_target_pairs={{0,256},{128,384},{256,0},{384,128},{1,257},{129,385},{257,1},{385... | collective-permute-start | bytes 98312 | tf_op jit(solution)/shard_map/ppermute | solution.py:186
  31.8 6.0 %collective-permute-start = (bf16[8,16,128]{2,1,0:T(8,128)(2,1)S(1)}, bf16[8,16,128]{2,1,0:T(8,128)(2,1)S(1)}, u32[]{:S(2)}, u32[]{:S(2)}) collective-permute-start(bf16[8,16,128]{2,1,0:T(8,128)(2,1)S(1)} %get-tuple-element.20), channel_id=1, source_target_pairs={{0,128},{128,256},{256,384},{384,0},{1,129},{129,257},{257,385},{3... | collective-permute-start | bytes 98312 | tf_op jit(solution)/shard_map/ppermute | solution.py:186
  35.8 7.0 %collective-permute-start.2 = (bf16[8,16,128]{2,1,0:T(8,128)(2,1)S(1)}, bf16[8,16,128]{2,1,0:T(8,128)(2,1)S(1)}, u32[]{:S(2)}, u32[]{:S(2)}) collective-permute-start(bf16[8,16,128]{2,1,0:T(8,128)(2,1)S(1)} %get-tuple-element.20), channel_id=1, source_target_pairs={{0,384},{128,0},{256,128},{384,256},{1,385},{129,1},{257,129},{385... | collective-permute-start | bytes 98312 | tf_op jit(solution)/shard_map/ppermute | solution.py:186
  42.8 3.2 %collective-permute-start.3 = (bf16[4,8,16,128]{3,2,1,0:T(8,128)(2,1)S(1)}, bf16[4,8,16,128]{3,2,1,0:T(8,128)(2,1)S(1)}, u32[]{:S(2)}, u32[]{:S(2)}) collective-permute-start(bf16[4,8,16,128]{3,2,1,0:T(8,128)(2,1)S(1)} %pad_maximum_fusion.own_ref), channel_id=1, source_target_pairs={{0,16},{16,0},{1,17},{17,1},{2,18},{18,2},{3,19},{19,3},{4,20},{20... | collective-permute-start | bytes 393224 | tf_op jit(solution)/shard_map/ppermute | solution.py:190
  86.4 10.7 %copy-start = (bf16[64,256]{1,0:T(8,128)(2,1)S(1)}, bf16[64,256]{1,0:T(8,128)(2,1)}, u32[]{:S(2)}) copy-start(bf16[64,256]{1,0:T(8,128)(2,1)} %wm_ref.1) | copy-start | bytes 98308
  86.4 10.6 %copy-start.1 = (f32[200,128]{1,0:T(8,128)S(1)}, f32[200,128]{1,0:T(8,128)}, u32[]{:S(2)}) copy-start(f32[200,128]{1,0:T(8,128)} %get-tuple-element.15.save_ref) | copy-start | bytes 307204
  86.4 10.6 %copy-start.2 = (bf16[64,64]{1,0:T(8,128)(2,1)S(1)}, bf16[64,64]{1,0:T(8,128)(2,1)}, u32[]{:S(2)}) copy-start(bf16[64,64]{1,0:T(8,128)(2,1)} %wf_ref.1) | copy-start | bytes 24580

commit v6 on v2

v6 whole, which is shorter than its diff:
```python
import math

import jax
import jax.numpy as jnp
from jax import lax
from jax.experimental import pallas as pl
from jax.experimental.pallas import tpu as pltpu
from jax.sharding import Mesh, PartitionSpec as P

HEADS = 8
HEAD_DIM = 8
EPS = 1e-05
SCALE = 1.0 / math.sqrt(HEAD_DIM)

DEPTH = ("x", "zh", "core")
RES = ("zl", "y")
HEAD_AXES = ("zl", "zh")
KEY_AXES = ("y",)


def tdot(a, b, ca, cb):
    return lax.dot_general(a, b, (((ca,), (cb,)), ((), ())), preferred_element_type=jnp.float32)


def project_kernel(x_hbm, rc_hbm, wm_hbm, wf_hbm, bias_hbm, pack_ref, save_ref,
                   x_ref, rc_ref, wm_ref, wf_ref, bias_ref, sems):
    pairs = [(x_hbm, x_ref), (wm_hbm, wm_ref), (rc_hbm, rc_ref), (wf_hbm, wf_ref), (bias_hbm, bias_ref)]
    copies = [pltpu.make_async_copy(a, b, sems.at[i]) for i, (a, b) in enumerate(pairs)]
    for copy in copies:
        copy.start()
    for copy in copies:
        copy.wait()
    x = x_ref[...].astype(jnp.float32).T
    cent = x - jnp.mean(x, 0, keepdims=True)
    rstd = lax.rsqrt(jnp.mean(cent * cent, 0, keepdims=True) + EPS)
    xhat = cent * rstd
    proj = tdot(wm_ref[...], xhat.astype(jnp.bfloat16), 0, 0)
    g = jax.nn.sigmoid(proj[192:256])
    d_gated = tdot(wf_ref[...], rc_ref[...], 1, 1)
    d_attn = d_gated * g
    save_ref[...] = jnp.concatenate([xhat, g, d_gated, jnp.broadcast_to(rstd, (8, 128))], 0)
    for h in range(HEADS):
        lo, hi = h * HEAD_DIM, (h + 1) * HEAD_DIM
        b = bias_ref[h].astype(jnp.float32)
        parts = [proj[lo:hi] * SCALE, d_attn[lo:hi], proj[64 + lo : 64 + hi], proj[128 + lo : 128 + hi]]
        parts += [b[r : r + 1, c * 128 : c * 128 + 128] for r in range(2) for c in range(8)]
        pack_ref[h] = jnp.concatenate(parts, 0).astype(jnp.bfloat16)


def attend_kernel(pack_ref, kv_in_ref, own_ref, sibling_ref, oq_ref, dkv_ref, keep_ref, give_ref,
                  wide_ref, bias_ref, acc_ref, tmp_ref, kv_ref, t_ref, pair_ref):
    me_x, core = lax.axis_index("x"), lax.axis_index("core")
    for k in range(4):
        at = lax.rem(me_x + 4 - k, 4) * 2
        for h in range(8):
            wide_ref[at + core, h] = own_ref[k, h].astype(jnp.float32)
            wide_ref[at + 1 - core, h] = sibling_ref[k, h].astype(jnp.float32)
    groups = [(zl, x) for zl in range(2) for x in range(4)]
    for i, (zl, x) in enumerate(groups):
        for zh in range(4):
            for half in range(2):
                at = (zh * 2 + half) * 16
                tmp_ref[i, at : at + 16] = wide_ref[x * 2 + half, zl * 4 + zh]
    for i in range(8):
        for c in range(8):
            bias_ref[i * 16 : i * 16 + 16, c * 128 : c * 128 + 128] = tmp_ref[i, pl.ds(c, 16, stride=8)]
    left = lax.broadcasted_iota(jnp.int32, (128, 16), 1) < HEAD_DIM
    blocks = [slice(at, at + 16) for at in range(0, 128, 16)]
    queries, cots, tops, sums, deltas, scaled, attns = [], [], [], [], [], [], []
    for n in range(8):
        dl, lanes = n // 2, slice(n % 2 * 64, n % 2 * 64 + 64)
        kv_ref[n] = jnp.concatenate(
            [kv_in_ref[y, zl * 4 + dl][:, lanes] for zl in range(2) for y in range(8)], 1
        )
        qd = jnp.concatenate([pack_ref[zl * 4 + dl, 0:16][:, lanes] for zl in range(2)], 1)
        rows = qd.astype(jnp.float32).T
        queries.append(jnp.where(left, rows, 0.0))
        cots.append(jnp.where(left, 0.0, rows))
    for n in range(8):
        scores = tdot(queries[n].astype(jnp.bfloat16), kv_ref[n], 1, 0)
        top = []
        for b in blocks:
            t = scores[b] + bias_ref[b]
            t_ref[n, b] = t
            top.append(jnp.max(t, 1, keepdims=True))
        tops.append(top)
    for n in range(8):
        total = []
        for i, b in enumerate(blocks):
            e = jnp.exp(t_ref[n, b] - tops[n][i])
            total.append(jnp.sum(e, 1, keepdims=True))
            pair_ref[n, 128 + i * 16 : 144 + i * 16] = e.astype(jnp.bfloat16)
        sums.append(jnp.concatenate(total, 0))
    for n in range(8):
        inverse = 1.0 / sums[n]
        attn = tdot(pair_ref[n, 128:256], kv_ref[n], 1, 1) * inverse
        d = (cots[n] * inverse).astype(jnp.bfloat16)
        scaled.append(d)
        attns.append(attn)
        deltas.append(jnp.sum(d.astype(jnp.float32) * attn, 1, keepdims=True))
    for n in range(8):
        dp = tdot(scaled[n], kv_ref[n], 1, 0)
        for i, b in enumerate(blocks):
            e = pair_ref[n, 128 + i * 16 : 144 + i * 16].astype(jnp.float32)
            ds = e * (dp[b] - deltas[n][b])
            pair_ref[n, b] = ds.astype(jnp.bfloat16)
            if n == 0:
                acc_ref[b] = ds
            else:
                acc_ref[b] += ds
    outs, grads = [], []
    for n in range(8):
        dq = tdot(pair_ref[n, 0:128], kv_ref[n], 1, 1)
        outs.append(jnp.where(left, dq, attns[n]).T.astype(jnp.bfloat16))
        lhs = jnp.concatenate([queries[n].T, scaled[n].astype(jnp.float32).T], 1)
        grads.append(tdot(lhs.astype(jnp.bfloat16), pair_ref[n], 1, 0).astype(jnp.bfloat16))
    for dl in range(4):
        for zl in range(2):
            part = slice(zl * 64, zl * 64 + 64)
            oq_ref[zl * 4 + dl] = jnp.concatenate([outs[dl * 2 + s][:, part] for s in range(2)], 1)
            for y in range(8):
                r = zl * 8 + y
                part_y = slice(r * 64, r * 64 + 64)
                dkv_ref[y, zl * 4 + dl] = jnp.concatenate(
                    [grads[dl * 2 + s][:, part_y] for s in range(2)], 1
                )
    for i in range(8):
        for c in range(8):
            tmp_ref[i, pl.ds(c, 16, stride=8)] = acc_ref[i * 16 : i * 16 + 16, c * 128 : c * 128 + 128]
    for i, (zl, x) in enumerate(groups):
        for zh in range(4):
            for half in range(2):
                at = (zh * 2 + half) * 16
                wide_ref[x * 2 + half, zl * 4 + zh] = tmp_ref[i, at : at + 16]
    for k in range(4):
        to = lax.rem(me_x + k, 4) * 2
        for h in range(8):
            keep_ref[k, h] = wide_ref[to + core, h].astype(jnp.bfloat16)
            give_ref[k, h] = wide_ref[to + 1 - core, h].astype(jnp.bfloat16)


def join_kernel(keep_ref, got_ref, *out_refs):
    for k in range(4):
        for h in range(HEADS):
            both = keep_ref[k, h].astype(jnp.float32) + got_ref[k, h].astype(jnp.float32)
            out_refs[k][h] = both.astype(jnp.bfloat16)


def total(blocks):
    acc = blocks[0].astype(jnp.float32)
    for block in blocks[1:]:
        acc += block.astype(jnp.float32)
    return acc.astype(jnp.bfloat16)


def sum_kernel(*refs):
    oq_ref, dkv_ref, db_refs, pack_ref = refs[0], refs[1], refs[2:6], refs[6]
    for h in range(HEADS):
        pack_ref[h, 0:16] = oq_ref[h]
        pack_ref[h, 16:32] = total([dkv_ref[y, h] for y in range(8)])
        pack_ref[h, 32:48] = total([ref[h] for ref in db_refs])


def finish_kernel(pack_ref, save_ref, wm_ref, wf_ref, up_ref, dx_ref, db_ref):
    dq, dk, dv, attn = [], [], [], []
    for h in range(HEADS):
        own = pack_ref[h].astype(jnp.float32)
        dq.append(own[0:8] * SCALE)
        attn.append(own[8:16])
        dk.append(own[16:24])
        dv.append(own[24:32])
        for r in range(2):
            db_ref[h, r : r + 1] = jnp.concatenate(
                [own[32 + r * 8 + c : 33 + r * 8 + c] for c in range(8)], 1
            )
    attn = jnp.concatenate(attn, 0)
    xhat, g, d_gated, rstd = save_ref[0:64], save_ref[64:128], save_ref[128:192], save_ref[192:193]
    gated = (g * attn).astype(jnp.bfloat16)
    up_ref[...] = tdot(gated, wf_ref[...], 0, 0).astype(jnp.bfloat16)
    d_gate = d_gated * attn * g * (1.0 - g)
    d_proj = jnp.concatenate(dq + dk + dv + [d_gate], 0).astype(jnp.bfloat16)
    d_normed = tdot(wm_ref[...], d_proj, 1, 0)
    dx = rstd * (
        d_normed
        - jnp.mean(d_normed, 0, keepdims=True)
        - xhat * jnp.mean(d_normed * xhat, 0, keepdims=True)
    )
    dx_ref[...] = dx.T.astype(jnp.bfloat16)


def call(kernel, outs, *args, scratch=(), space=pltpu.VMEM, limit=40):
    return pl.pallas_call(
        kernel,
        out_shape=outs,
        in_specs=[pl.BlockSpec(memory_space=space)] * len(args),
        out_specs=[pl.BlockSpec(memory_space=pltpu.VMEM)] * len(outs),
        scratch_shapes=list(scratch),
        compiler_params=pltpu.CompilerParams(vmem_limit_bytes=limit * 1024 * 1024),
    )(*args)


def shape(*dims, dtype=jnp.bfloat16):
    return jax.ShapeDtypeStruct(dims, dtype)


def exchange(a, axes):
    return lax.all_to_all(a, axes, 0, 0, tiled=True)


def shift_x(a, k):
    return lax.ppermute(a, "x", [(i, (i + k) % 4) for i in range(4)])


def swap_core(a):
    return lax.ppermute(a, "core", [(0, 1), (1, 0)])


def per_device(x, bias, wm, wf, rc):
    f32 = jnp.float32
    pack, saved = call(
        project_kernel,
        [shape(8, 48, 128), shape(200, 128, dtype=f32)],
        x.reshape(128, 64), rc.reshape(128, 64), wm, wf, bias,
        scratch=[pltpu.VMEM((128, 64), jnp.bfloat16), pltpu.VMEM((128, 64), jnp.bfloat16),
                 pltpu.VMEM((64, 256), jnp.bfloat16), pltpu.VMEM((64, 64), jnp.bfloat16),
                 pltpu.VMEM((8, 2, 1024), jnp.bfloat16), pltpu.SemaphoreType.DMA((5,))],
        space=pltpu.HBM, limit=60,
    )
    pack = exchange(pack, HEAD_AXES)
    own = pack[:, 16:32]
    kv = exchange(jnp.broadcast_to(own[None], (8,) + own.shape), KEY_AXES)
    own = pack[:, 32:48]
    own_bias = jnp.stack([own] + [shift_x(own, k) for k in range(1, 4)])
    swap_bias = swap_core(own_bias)
    block, quad, octet = shape(8, 16, 128), shape(4, 8, 16, 128), shape(8, 8, 16, 128)
    oq, dkv, keep, give = call(
        attend_kernel,
        [block, octet, quad, quad],
        pack, kv, own_bias, swap_bias,
        scratch=[pltpu.VMEM((8, 8, 16, 128), f32), pltpu.VMEM((128, 1024), f32),
                 pltpu.VMEM((128, 1024), f32), pltpu.VMEM((8, 128, 128), f32),
                 pltpu.VMEM((8, 16, 1024), jnp.bfloat16), pltpu.VMEM((8, 128, 1024), f32),
                 pltpu.VMEM((8, 256, 1024), jnp.bfloat16)],
    )
    dkv = exchange(dkv, KEY_AXES)
    db = call(join_kernel, [block] * 4, keep, swap_core(give))
    db = [db[0]] + [shift_x(db[k], k) for k in range(1, 4)]
    (back,) = call(sum_kernel, [shape(8, 48, 128)], oq, dkv, *db)
    back = exchange(back, HEAD_AXES)
    update, dx, d_bias = call(
        finish_kernel,
        [shape(128, 64), shape(128, 64), shape(8, 2, 1024, dtype=f32)],
        back, saved, wm, wf,
    )
    return update.reshape(2, 64, 64), dx.reshape(2, 64, 64), d_bias


def solution(mesh):
    fine = Mesh(mesh.devices.reshape(4, 4, 2, 2, 8), DEPTH + RES)
    tokens = P(DEPTH, RES, None)
    rows = P(None, RES + DEPTH, None)
    return jax.shard_map(
        per_device,
        mesh=fine,
        in_specs=(tokens, rows, P(), P(), tokens),
        out_specs=(tokens, tokens, rows),
        check_vma=False,
    )
```

time: 92.9 us -> 88.4 us (0.952)
  Pallas kernels: 11.7 us -> 7.97 us
    pallas_call x5, Pallas kernels: 11.7 us -> 7.97 us  [call(): pl.pallas_call(kernel, out_shape=outs, in_specs=[pl.BlockSpec(memory_spac...]
where the time goes in v6:
time: 88.4 us; the launch traced here: 87.7 us
  starting transfers between devices  41.3 us (47%)
  blocking collectives  28.8 us (33%)
  waiting for transfers between devices  8.06 us (9%)
  Pallas kernels  7.97 us (9%)
    all_to_all x2, blocking collectives, exchange(): return lax.all_to_all(a, axes, 0, 0, tiled=True)  28.8 us
    ppermute x6, starting transfers between devices, shift_x(): return lax.ppermute(a, 'x', [(i, (i + k) % 4) for i in range(4)])  22.7 us
    all_to_all x2, starting transfers between devices, exchange(): return lax.all_to_all(a, axes, 0, 0, tiled=True)  14.7 us
    pallas_call x5, Pallas kernels, call(): pl.pallas_call(kernel, out_shape=outs, in_specs=[pl.BlockSpec(memory_spac...  7.97 us
    ppermute x6, waiting for transfers between devices, shift_x(): return lax.ppermute(a, 'x', [(i, (i + k) % 4) for i in range(4)])  5.42 us
    ppermute x2, starting transfers between devices, swap_core(): return lax.ppermute(a, 'core', [(0, 1), (1, 0)])  3.83 us
    ppermute x2, waiting for transfers between devices, swap_core(): return lax.ppermute(a, 'core', [(0, 1), (1, 0)])  2.63 us
  transfers between devices with their start and end apart: 10, of which 4 were waited for; matrix products, arithmetic and copies ran while one was open for 0% of the time, Pallas kernels for 0%

profile of v6, /device:TPU:8, one launch (start us, length us, event | category | flops | bytes accessed | tf_op | source)
XLA Modules:
  0.0 87.7 jit_solution(483710475833750018)
XLA Ops:
  0.6 1.8 %shard_map.76 = (bf16[8,48,128]{2,1,0:T(8,128)(2,1)}, f32[200,128]{1,0:T(8,128)}) custom-call(bf16[128,64]{1,0:T(8,128)(2,1)} %bitcast.9, bf16[128,64]{1,0:T(8,128)(2,1)} %bitcast.10, bf16[64,256]{1,0:T(8,128)(2,1)} %wm_ref.1, bf16[64,64]{1,0:T(8,128)(2,1)} %wf_ref.1, bf16[8,2,1024]{2,1,0:T(2,128)(2,1)} %bias_hbm.1), custom_call_target="tpu_custom_call" | custom-call | tf_op jit(solution)/shard_map/pallas_call | solution.py:192
  2.5 18.1 %all_to_all.20.pack_ref = bf16[8,48,128]{2,1,0:T(8,128)(2,1)S(1)} all-to-all(bf16[8,48,128]{2,1,0:T(8,128)(2,1)} %get-tuple-element.16), channel_id=1, replica_groups=mesh['x'=4,'zh'=4,'core'=2,'zl'=2,'y'=8] {'zl','zh'}, dimensions={0} | all-to-all | bytes 196608 | tf_op jit(solution)/shard_map/all_to_all | solution.py:207
  20.6 0.7 broadcast_in_dim.2
  21.3 7.5 %all-to-all-start.1 = ((bf16[8,8,16,128]{3,2,1,0:T(8,128)(2,1)}), bf16[8,8,16,128]{3,2,1,0:T(8,128)(2,1)S(1)}, u32[]{:S(2)}, u32[]{:S(2)}) async-start(bf16[8,8,16,128]{3,2,1,0:T(8,128)(2,1)} %broadcast_in_dim.2), calls=%async_computation.1 | async-start | bytes 524288 | tf_op jit(solution)/shard_map/all_to_all | solution.py:207
  28.9 4.9 %collective-permute-start.1 = (bf16[8,16,128]{2,1,0:T(8,128)(2,1)S(1)}, bf16[8,16,128]{2,1,0:T(8,128)(2,1)S(1)}, u32[]{:S(2)}, u32[]{:S(2)}) collective-permute-start(bf16[8,16,128]{2,1,0:T(8,128)(2,1)S(1)} %get-tuple-element.30), channel_id=1, source_target_pairs={{0,256},{128,384},{256,0},{384,128},{1,257},{129,385},{257,1},{385... | collective-permute-start | bytes 98312 | tf_op jit(solution)/shard_map/ppermute | solution.py:211
  33.8 2.5 %collective-permute-start = (bf16[8,16,128]{2,1,0:T(8,128)(2,1)S(1)}, bf16[8,16,128]{2,1,0:T(8,128)(2,1)S(1)}, u32[]{:S(2)}, u32[]{:S(2)}) collective-permute-start(bf16[8,16,128]{2,1,0:T(8,128)(2,1)S(1)} %get-tuple-element.30), channel_id=1, source_target_pairs={{0,128},{128,256},{256,384},{384,0},{1,129},{129,257},{257,385},{3... | collective-permute-start | bytes 98312 | tf_op jit(solution)/shard_map/ppermute | solution.py:211
  36.3 4.6 %collective-permute-start.2 = (bf16[8,16,128]{2,1,0:T(8,128)(2,1)S(1)}, bf16[8,16,128]{2,1,0:T(8,128)(2,1)S(1)}, u32[]{:S(2)}, u32[]{:S(2)}) collective-permute-start(bf16[8,16,128]{2,1,0:T(8,128)(2,1)S(1)} %get-tuple-element.30), channel_id=1, source_target_pairs={{0,384},{128,0},{256,128},{384,256},{1,385},{129,1},{257,129},{385... | collective-permute-start | bytes 98312 | tf_op jit(solution)/shard_map/ppermute | solution.py:211
  40.9 0.0 collective-permute-done.1
  40.9 0.0 collective-permute-done
  40.9 1.6 %collective-permute-done.2 = bf16[8,16,128]{2,1,0:T(8,128)(2,1)S(1)} collective-permute-done((bf16[8,16,128]{2,1,0:T(8,128)(2,1)S(1)}, bf16[8,16,128]{2,1,0:T(8,128)(2,1)S(1)}, u32[]{:S(2)}, u32[]{:S(2)}) %collective-permute-start.2) | collective-permute-done | bytes 32800 | tf_op jit(solution)/shard_map/ppermute | solution.py:211
  42.5 1.9 %collective-permute-start.3 = (bf16[4,8,16,128]{3,2,1,0:T(8,128)(2,1)S(1)}, bf16[4,8,16,128]{3,2,1,0:T(8,128)(2,1)S(1)}, u32[]{:S(2)}, u32[]{:S(2)}) collective-permute-start(bf16[4,8,16,128]{3,2,1,0:T(8,128)(2,1)S(1)} %pad_maximum_fusion.own_ref), channel_id=1, source_target_pairs={{0,16},{16,0},{1,17},{17,1},{2,18},{18,2},{3,19},{19,3},{4,20},{20... | collective-permute-start | bytes 393224 | tf_op jit(solution)/shard_map/ppermute | solution.py:215
  44.4 1.3 %collective-permute-done.3.sibling_ref = bf16[4,8,16,128]{3,2,1,0:T(8,128)(2,1)S(1)} collective-permute-done((bf16[4,8,16,128]{3,2,1,0:T(8,128)(2,1)S(1)}, bf16[4,8,16,128]{3,2,1,0:T(8,128)(2,1)S(1)}, u32[]{:S(2)}, u32[]{:S(2)}) %collective-permute-start.3) | collective-permute-done | bytes 131104 | tf_op jit(solution)/shard_map/ppermute | solution.py:215
  45.7 0.0 all-to-all-done.1.kv_in_ref
  45.7 5.1 %shard_map.77 = (bf16[8,16,128]{2,1,0:T(8,128)(2,1)S(1)}, bf16[8,8,16,128]{3,2,1,0:T(8,128)(2,1)}, bf16[4,8,16,128]{3,2,1,0:T(8,128)(2,1)S(1)}, bf16[4,8,16,128]{3,2,1,0:T(8,128)(2,1)S(1)}) custom-call(bf16[8,48,128]{2,1,0:T(8,128)(2,1)S(1)} %all_to_all.20.pack_ref, bf16[8,8,16,128]{3,2,1,0:T(8,128)(2,1)S(1)} %all-to-all-done.1.kv_in_ref, ...), custom_call_target="tpu_custom_call" | custom-call | tf_op jit(solution)/shard_map/pallas_call | solution.py:192
  50.8 7.2 %all-to-all-start.2 = ((bf16[8,8,16,128]{3,2,1,0:T(8,128)(2,1)}), bf16[8,8,16,128]{3,2,1,0:T(8,128)(2,1)S(1)}, u32[]{:S(2)}, u32[]{:S(2)}) async-start(bf16[8,8,16,128]{3,2,1,0:T(8,128)(2,1)} %get-tuple-element.18), calls=%async_computation.2 | async-start | bytes 524288 | tf_op jit(solution)/shard_map/all_to_all | solution.py:207
  58.0 1.9 %collective-permute-start.4 = (bf16[4,8,16,128]{3,2,1,0:T(8,128)(2,1)S(1)}, bf16[4,8,16,128]{3,2,1,0:T(8,128)(2,1)S(1)}, u32[]{:S(2)}, u32[]{:S(2)}) collective-permute-start(bf16[4,8,16,128]{3,2,1,0:T(8,128)(2,1)S(1)} %get-tuple-element.20), channel_id=1, source_target_pairs={{0,16},{16,0},{1,17},{17,1},{2,18},{18,2},{3,19},{19,3},{4,20},{20... | collective-permute-start | bytes 393224 | tf_op jit(solution)/shard_map/ppermute | solution.py:215
  59.9 1.3 %collective-permute-done.4.got_ref = bf16[4,8,16,128]{3,2,1,0:T(8,128)(2,1)S(1)} collective-permute-done((bf16[4,8,16,128]{3,2,1,0:T(8,128)(2,1)S(1)}, bf16[4,8,16,128]{3,2,1,0:T(8,128)(2,1)S(1)}, u32[]{:S(2)}, u32[]{:S(2)}) %collective-permute-start.4) | collective-permute-done | bytes 131104 | tf_op jit(solution)/shard_map/ppermute | solution.py:215
  61.3 1.9 %collective-permute-start.5 = (bf16[8,16,128]{2,1,0:T(8,128)(2,1)S(1)}, bf16[8,16,128]{2,1,0:T(8,128)(2,1)S(1)}, u32[]{:S(2)}, u32[]{:S(2)}) collective-permute-start(bf16[8,16,128]{2,1,0:T(8,128)(2,1)S(1)} %get-tuple-element.22), channel_id=1, source_target_pairs={{0,128},{128,256},{256,384},{384,0},{1,129},{129,257},{257,385},{3... | collective-permute-start | bytes 98312 | tf_op jit(solution)/shard_map/ppermute | solution.py:211
  63.2 6.9 %collective-permute-start.6 = (bf16[8,16,128]{2,1,0:T(8,128)(2,1)S(1)}, bf16[8,16,128]{2,1,0:T(8,128)(2,1)S(1)}, u32[]{:S(2)}, u32[]{:S(2)}) collective-permute-start(bf16[8,16,128]{2,1,0:T(8,128)(2,1)S(1)} %get-tuple-element.23), channel_id=1, source_target_pairs={{0,256},{128,384},{256,0},{384,128},{1,257},{129,385},{257,1},{385... | collective-permute-start | bytes 98312 | tf_op jit(solution)/shard_map/ppermute | solution.py:211
  70.1 1.9 %collective-permute-start.7 = (bf16[8,16,128]{2,1,0:T(8,128)(2,1)S(1)}, bf16[8,16,128]{2,1,0:T(8,128)(2,1)S(1)}, u32[]{:S(2)}, u32[]{:S(2)}) collective-permute-start(bf16[8,16,128]{2,1,0:T(8,128)(2,1)S(1)} %get-tuple-element.24), channel_id=1, source_target_pairs={{0,384},{128,0},{256,128},{384,256},{1,385},{129,1},{257,129},{385... | collective-permute-start | bytes 98312 | tf_op jit(solution)/shard_map/ppermute | solution.py:211
  72.0 0.0 collective-permute-done.5.refs_3_
  72.0 0.0 collective-permute-done.6.refs_4_
  72.1 3.9 %collective-permute-done.7.refs_5_ = bf16[8,16,128]{2,1,0:T(8,128)(2,1)S(1)} collective-permute-done((bf16[8,16,128]{2,1,0:T(8,128)(2,1)S(1)}, bf16[8,16,128]{2,1,0:T(8,128)(2,1)S(1)}, u32[]{:S(2)}, u32[]{:S(2)}) %collective-permute-start.7) | collective-permute-done | bytes 32800 | tf_op jit(solution)/shard_map/ppermute | solution.py:211
  75.9 0.0 all-to-all-done.2.refs_1_
  75.9 0.1 shard_map.79
  76.0 0.0 copy-start
  76.0 0.0 copy-start.1
  76.0 0.0 copy-start.2
  76.0 10.7 %all_to_all.21.pack_ref = bf16[8,48,128]{2,1,0:T(8,128)(2,1)S(1)} all-to-all(bf16[8,48,128]{2,1,0:T(8,128)(2,1)S(1)} %shard_map.79), channel_id=1, replica_groups=mesh['x'=4,'zh'=4,'core'=2,'zl'=2,'y'=8] {'zl','zh'}, dimensions={0} | all-to-all | bytes 196608 | tf_op jit(solution)/shard_map/all_to_all | solution.py:207
  86.7 0.0 copy-done
  86.7 0.0 copy-done.1
  86.7 0.0 copy-done.2
  86.7 1.0 %shard_map.80 = (bf16[128,64]{1,0:T(8,128)(2,1)}, bf16[128,64]{1,0:T(8,128)(2,1)}, f32[8,2,1024]{2,1,0:T(2,128)}) custom-call(bf16[8,48,128]{2,1,0:T(8,128)(2,1)S(1)} %all_to_all.21.pack_ref, f32[200,128]{1,0:T(8,128)S(1)} %copy-done.1, bf16[64,256]{1,0:T(8,128)(2,1)S(1)} %copy-done, bf16[64,64]{1,0:T(8,128)(2,1)S(1)} %copy-done.2), custom_call_target="tpu_custom_call" | custom-call | tf_op jit(solution)/shard_map/pallas_call | solution.py:192
  (3 shorter events, 0.1 us)
Async XLA Ops:
  21.3 24.4 %all-to-all-start.1 = ((bf16[8,8,16,128]{3,2,1,0:T(8,128)(2,1)}), bf16[8,8,16,128]{3,2,1,0:T(8,128)(2,1)S(1)}, u32[]{:S(2)}, u32[]{:S(2)}) async-start(bf16[8,8,16,128]{3,2,1,0:T(8,128)(2,1)} %broadcast_in_dim.2), calls=%async_computation.1 | async-start | bytes 524288 | tf_op jit(solution)/shard_map/all_to_all | solution.py:207
  28.9 12.0 %collective-permute-start.1 = (bf16[8,16,128]{2,1,0:T(8,128)(2,1)S(1)}, bf16[8,16,128]{2,1,0:T(8,128)(2,1)S(1)}, u32[]{:S(2)}, u32[]{:S(2)}) collective-permute-start(bf16[8,16,128]{2,1,0:T(8,128)(2,1)S(1)} %get-tuple-element.30), channel_id=1, source_target_pairs={{0,256},{128,384},{256,0},{384,128},{1,257},{129,385},{257,1},{385... | collective-permute-start | bytes 98312 | tf_op jit(solution)/shard_map/ppermute | solution.py:211
  33.8 7.1 %collective-permute-start = (bf16[8,16,128]{2,1,0:T(8,128)(2,1)S(1)}, bf16[8,16,128]{2,1,0:T(8,128)(2,1)S(1)}, u32[]{:S(2)}, u32[]{:S(2)}) collective-permute-start(bf16[8,16,128]{2,1,0:T(8,128)(2,1)S(1)} %get-tuple-element.30), channel_id=1, source_target_pairs={{0,128},{128,256},{256,384},{384,0},{1,129},{129,257},{257,385},{3... | collective-permute-start | bytes 98312 | tf_op jit(solution)/shard_map/ppermute | solution.py:211
  36.3 6.1 %collective-permute-start.2 = (bf16[8,16,128]{2,1,0:T(8,128)(2,1)S(1)}, bf16[8,16,128]{2,1,0:T(8,128)(2,1)S(1)}, u32[]{:S(2)}, u32[]{:S(2)}) collective-permute-start(bf16[8,16,128]{2,1,0:T(8,128)(2,1)S(1)} %get-tuple-element.30), channel_id=1, source_target_pairs={{0,384},{128,0},{256,128},{384,256},{1,385},{129,1},{257,129},{385... | collective-permute-start | bytes 98312 | tf_op jit(solution)/shard_map/ppermute | solution.py:211
  42.5 3.2 %collective-permute-start.3 = (bf16[4,8,16,128]{3,2,1,0:T(8,128)(2,1)S(1)}, bf16[4,8,16,128]{3,2,1,0:T(8,128)(2,1)S(1)}, u32[]{:S(2)}, u32[]{:S(2)}) collective-permute-start(bf16[4,8,16,128]{3,2,1,0:T(8,128)(2,1)S(1)} %pad_maximum_fusion.own_ref), channel_id=1, source_target_pairs={{0,16},{16,0},{1,17},{17,1},{2,18},{18,2},{3,19},{19,3},{4,20},{20... | collective-permute-start | bytes 393224 | tf_op jit(solution)/shard_map/ppermute | solution.py:215
  50.8 25.1 %all-to-all-start.2 = ((bf16[8,8,16,128]{3,2,1,0:T(8,128)(2,1)}), bf16[8,8,16,128]{3,2,1,0:T(8,128)(2,1)S(1)}, u32[]{:S(2)}, u32[]{:S(2)}) async-start(bf16[8,8,16,128]{3,2,1,0:T(8,128)(2,1)} %get-tuple-element.18), calls=%async_computation.2 | async-start | bytes 524288 | tf_op jit(solution)/shard_map/all_to_all | solution.py:207
  58.0 3.2 %collective-permute-start.4 = (bf16[4,8,16,128]{3,2,1,0:T(8,128)(2,1)S(1)}, bf16[4,8,16,128]{3,2,1,0:T(8,128)(2,1)S(1)}, u32[]{:S(2)}, u32[]{:S(2)}) collective-permute-start(bf16[4,8,16,128]{3,2,1,0:T(8,128)(2,1)S(1)} %get-tuple-element.20), channel_id=1, source_target_pairs={{0,16},{16,0},{1,17},{17,1},{2,18},{18,2},{3,19},{19,3},{4,20},{20... | collective-permute-start | bytes 393224 | tf_op jit(solution)/shard_map/ppermute | solution.py:215
  61.3 10.8 %collective-permute-start.5 = (bf16[8,16,128]{2,1,0:T(8,128)(2,1)S(1)}, bf16[8,16,128]{2,1,0:T(8,128)(2,1)S(1)}, u32[]{:S(2)}, u32[]{:S(2)}) collective-permute-start(bf16[8,16,128]{2,1,0:T(8,128)(2,1)S(1)} %get-tuple-element.22), channel_id=1, source_target_pairs={{0,128},{128,256},{256,384},{384,0},{1,129},{129,257},{257,385},{3... | collective-permute-start | bytes 98312 | tf_op jit(solution)/shard_map/ppermute | solution.py:211
  63.2 8.8 %collective-permute-start.6 = (bf16[8,16,128]{2,1,0:T(8,128)(2,1)S(1)}, bf16[8,16,128]{2,1,0:T(8,128)(2,1)S(1)}, u32[]{:S(2)}, u32[]{:S(2)}) collective-permute-start(bf16[8,16,128]{2,1,0:T(8,128)(2,1)S(1)} %get-tuple-element.23), channel_id=1, source_target_pairs={{0,256},{128,384},{256,0},{384,128},{1,257},{129,385},{257,1},{385... | collective-permute-start | bytes 98312 | tf_op jit(solution)/shard_map/ppermute | solution.py:211
  70.1 5.8 %collective-permute-start.7 = (bf16[8,16,128]{2,1,0:T(8,128)(2,1)S(1)}, bf16[8,16,128]{2,1,0:T(8,128)(2,1)S(1)}, u32[]{:S(2)}, u32[]{:S(2)}) collective-permute-start(bf16[8,16,128]{2,1,0:T(8,128)(2,1)S(1)} %get-tuple-element.24), channel_id=1, source_target_pairs={{0,384},{128,0},{256,128},{384,256},{1,385},{129,1},{257,129},{385... | collective-permute-start | bytes 98312 | tf_op jit(solution)/shard_map/ppermute | solution.py:211
  76.0 10.7 %copy-start = (bf16[64,256]{1,0:T(8,128)(2,1)S(1)}, bf16[64,256]{1,0:T(8,128)(2,1)}, u32[]{:S(2)}) copy-start(bf16[64,256]{1,0:T(8,128)(2,1)} %wm_ref.1) | copy-start | bytes 98308
  76.0 10.7 %copy-start.1 = (f32[200,128]{1,0:T(8,128)S(1)}, f32[200,128]{1,0:T(8,128)}, u32[]{:S(2)}) copy-start(f32[200,128]{1,0:T(8,128)} %get-tuple-element.25.save_ref) | copy-start | bytes 307204
  76.0 10.7 %copy-start.2 = (bf16[64,64]{1,0:T(8,128)(2,1)S(1)}, bf16[64,64]{1,0:T(8,128)(2,1)}, u32[]{:S(2)}) copy-start(bf16[64,64]{1,0:T(8,128)(2,1)} %wf_ref.1) | copy-start | bytes 24580

commit v7 on v6

--- a/solution.py
+++ b/solution.py
@@ -47,14 +47,13 @@
         pack_ref[h] = jnp.concatenate(parts, 0).astype(jnp.bfloat16)
 
 
-def attend_kernel(pack_ref, kv_in_ref, own_ref, sibling_ref, oq_ref, dkv_ref, keep_ref, give_ref,
+def attend_kernel(pack_ref, kv_in_ref, bias_in_ref, oq_ref, dkv_ref, keep_ref, give_ref,
                   wide_ref, bias_ref, acc_ref, tmp_ref, kv_ref, t_ref, pair_ref):
-    me_x, core = lax.axis_index("x"), lax.axis_index("core")
-    for k in range(4):
-        at = lax.rem(me_x + 4 - k, 4) * 2
+    core = lax.axis_index("core")
+    for x in range(4):
         for h in range(8):
-            wide_ref[at + core, h] = own_ref[k, h].astype(jnp.float32)
-            wide_ref[at + 1 - core, h] = sibling_ref[k, h].astype(jnp.float32)
+            wide_ref[x * 2 + core, h] = bias_in_ref[x, 0, h].astype(jnp.float32)
+            wide_ref[x * 2 + 1 - core, h] = bias_in_ref[x, 1, h].astype(jnp.float32)
     groups = [(zl, x) for zl in range(2) for x in range(4)]
     for i, (zl, x) in enumerate(groups):
         for zh in range(4):
@@ -132,18 +131,17 @@
             for half in range(2):
                 at = (zh * 2 + half) * 16
                 wide_ref[x * 2 + half, zl * 4 + zh] = tmp_ref[i, at : at + 16]
-    for k in range(4):
-        to = lax.rem(me_x + k, 4) * 2
+    for x in range(4):
         for h in range(8):
-            keep_ref[k, h] = wide_ref[to + core, h].astype(jnp.bfloat16)
-            give_ref[k, h] = wide_ref[to + 1 - core, h].astype(jnp.bfloat16)
-
-
-def join_kernel(keep_ref, got_ref, *out_refs):
-    for k in range(4):
+            keep_ref[x, h] = wide_ref[x * 2 + core, h].astype(jnp.bfloat16)
+            give_ref[x, h] = wide_ref[x * 2 + 1 - core, h].astype(jnp.bfloat16)
+
+
+def join_kernel(keep_ref, got_ref, out_ref):
+    for x in range(4):
         for h in range(HEADS):
-            both = keep_ref[k, h].astype(jnp.float32) + got_ref[k, h].astype(jnp.float32)
-            out_refs[k][h] = both.astype(jnp.bfloat16)
+            both = keep_ref[x, h].astype(jnp.float32) + got_ref[x, h].astype(jnp.float32)
+            out_ref[x, h] = both.astype(jnp.bfloat16)
 
 
 def total(blocks):
@@ -153,12 +151,11 @@
     return acc.astype(jnp.bfloat16)
 
 
-def sum_kernel(*refs):
-    oq_ref, dkv_ref, db_refs, pack_ref = refs[0], refs[1], refs[2:6], refs[6]
+def sum_kernel(oq_ref, dkv_ref, db_ref, pack_ref):
     for h in range(HEADS):
         pack_ref[h, 0:16] = oq_ref[h]
         pack_ref[h, 16:32] = total([dkv_ref[y, h] for y in range(8)])
-        pack_ref[h, 32:48] = total([ref[h] for ref in db_refs])
+        pack_ref[h, 32:48] = total([db_ref[x, h] for x in range(4)])
 
 
 def finish_kernel(pack_ref, save_ref, wm_ref, wf_ref, up_ref, dx_ref, db_ref):
@@ -207,10 +204,6 @@
     return lax.all_to_all(a, axes, 0, 0, tiled=True)
 
 
-def shift_x(a, k):
-    return lax.ppermute(a, "x", [(i, (i + k) % 4) for i in range(4)])
-
-
 def swap_core(a):
     return lax.ppermute(a, "core", [(0, 1), (1, 0)])
 
@@ -230,22 +223,24 @@
     own = pack[:, 16:32]
     kv = exchange(jnp.broadcast_to(own[None], (8,) + own.shape), KEY_AXES)
     own = pack[:, 32:48]
-    own_bias = jnp.stack([own] + [shift_x(own, k) for k in range(1, 4)])
-    swap_bias = swap_core(own_bias)
+    pair = jnp.stack([own, swap_core(own)])
+    kv, pair = lax.optimization_barrier((kv, pair))
+    bias_rows = exchange(jnp.broadcast_to(pair[None], (4,) + pair.shape), ("x",))
     block, quad, octet = shape(8, 16, 128), shape(4, 8, 16, 128), shape(8, 8, 16, 128)
     oq, dkv, keep, give = call(
         attend_kernel,
         [block, octet, quad, quad],
-        pack, kv, own_bias, swap_bias,
+        pack, kv, bias_rows,
         scratch=[pltpu.VMEM((8, 8, 16, 128), f32), pltpu.VMEM((128, 1024), f32),
                  pltpu.VMEM((128, 1024), f32), pltpu.VMEM((8, 128, 128), f32),
                  pltpu.VMEM((8, 16, 1024), jnp.bfloat16), pltpu.VMEM((8, 128, 1024), f32),
                  pltpu.VMEM((8, 256, 1024), jnp.bfloat16)],
     )
     dkv = exchange(dkv, KEY_AXES)
-    db = call(join_kernel, [block] * 4, keep, swap_core(give))
-    db = [db[0]] + [shift_x(db[k], k) for k in range(1, 4)]
-    (back,) = call(sum_kernel, [shape(8, 48, 128)], oq, dkv, *db)
+    (db,) = call(join_kernel, [quad], keep, swap_core(give))
+    dkv, db = lax.optimization_barrier((dkv, db))
+    db = exchange(db, ("x",))
+    (back,) = call(sum_kernel, [shape(8, 48, 128)], oq, dkv, db)
     back = exchange(back, HEAD_AXES)
     update, dx, d_bias = call(
         finish_kernel,

time: 88.4 us -> 88.6 us (level)
  the two profiles are of different devices: /device:TPU:8 before, /device:TPU:6 now
where the time goes in v7:
time: 88.6 us; the launch traced here: 87.3 us
  blocking collectives  46.3 us (52%)
  waiting for transfers between devices  17.2 us (19%)
  starting transfers between devices  14.3 us (16%)
  Pallas kernels  7.88 us (9%)
    all_to_all x4, blocking collectives, exchange(): return lax.all_to_all(a, axes, 0, 0, tiled=True)  46.3 us
    all_to_all x2, waiting for transfers between devices, exchange(): return lax.all_to_all(a, axes, 0, 0, tiled=True)  14.7 us
    all_to_all x2, starting transfers between devices, exchange(): return lax.all_to_all(a, axes, 0, 0, tiled=True)  10.5 us
    pallas_call x5, Pallas kernels, call(): pl.pallas_call(kernel, out_shape=outs, in_specs=[pl.BlockSpec(memory_spac...  7.88 us
    ppermute x2, starting transfers between devices, swap_core(): return lax.ppermute(a, 'core', [(0, 1), (1, 0)])  3.83 us
    ppermute x2, waiting for transfers between devices, swap_core(): return lax.ppermute(a, 'core', [(0, 1), (1, 0)])  2.49 us
  transfers between devices with their start and end apart: 4, of which 4 were waited for; matrix products, arithmetic and copies ran while one was open for 0% of the time, Pallas kernels for 0%

profile of v7, /device:TPU:6, one launch (start us, length us, event | category | flops | bytes accessed | tf_op | source)
XLA Modules:
  0.0 87.3 jit_solution(1136395439181483067)
XLA Ops:
  0.6 1.8 %shard_map.76 = (bf16[8,48,128]{2,1,0:T(8,128)(2,1)}, f32[200,128]{1,0:T(8,128)}) custom-call(bf16[128,64]{1,0:T(8,128)(2,1)} %bitcast.7, bf16[128,64]{1,0:T(8,128)(2,1)} %bitcast.8, bf16[64,256]{1,0:T(8,128)(2,1)} %wm_ref.1, bf16[64,64]{1,0:T(8,128)(2,1)} %wf_ref.1, bf16[8,2,1024]{2,1,0:T(2,128)(2,1)} %bias_hbm.1), custom_call_target="tpu_custom_call" | custom-call | tf_op jit(solution)/shard_map/pallas_call | solution.py:189
  2.5 18.1 %all_to_all.30.pack_ref = bf16[8,48,128]{2,1,0:T(8,128)(2,1)S(1)} all-to-all(bf16[8,48,128]{2,1,0:T(8,128)(2,1)} %get-tuple-element.16), channel_id=1, replica_groups=mesh['x'=4,'zh'=4,'core'=2,'zl'=2,'y'=8] {'zl','zh'}, dimensions={0} | all-to-all | bytes 196608 | tf_op jit(solution)/shard_map/all_to_all | solution.py:204
  20.6 0.7 broadcast_in_dim.4
  21.4 7.1 %all-to-all-start.1 = ((bf16[8,8,16,128]{3,2,1,0:T(8,128)(2,1)}), bf16[8,8,16,128]{3,2,1,0:T(8,128)(2,1)S(1)}, u32[]{:S(2)}, u32[]{:S(2)}) async-start(bf16[8,8,16,128]{3,2,1,0:T(8,128)(2,1)} %broadcast_in_dim.4), calls=%async_computation.1 | async-start | bytes 524288 | tf_op jit(solution)/shard_map/all_to_all | solution.py:204
  28.5 1.9 %collective-permute-start = (bf16[8,16,128]{2,1,0:T(8,128)(2,1)S(1)}, bf16[8,16,128]{2,1,0:T(8,128)(2,1)S(1)}, u32[]{:S(2)}, u32[]{:S(2)}) collective-permute-start(bf16[8,16,128]{2,1,0:T(8,128)(2,1)S(1)} %get-tuple-element.30), channel_id=1, source_target_pairs={{0,16},{16,0},{1,17},{17,1},{2,18},{18,2},{3,19},{19,3},{4,20},{20... | collective-permute-start | bytes 98312 | tf_op jit(solution)/shard_map/ppermute | solution.py:208
  30.4 1.2 %collective-permute-done = bf16[8,16,128]{2,1,0:T(8,128)(2,1)S(1)} collective-permute-done((bf16[8,16,128]{2,1,0:T(8,128)(2,1)S(1)}, bf16[8,16,128]{2,1,0:T(8,128)(2,1)S(1)}, u32[]{:S(2)}, u32[]{:S(2)}) %collective-permute-start) | collective-permute-done | bytes 32800 | tf_op jit(solution)/shard_map/ppermute | solution.py:208
  31.6 7.6 %all-to-all-done.1.kv_in_ref = bf16[8,8,16,128]{3,2,1,0:T(8,128)(2,1)S(1)} async-done(((bf16[8,8,16,128]{3,2,1,0:T(8,128)(2,1)}), bf16[8,8,16,128]{3,2,1,0:T(8,128)(2,1)S(1)}, u32[]{:S(2)}, u32[]{:S(2)}) %all-to-all-start.1) | async-done | bytes 262176 | tf_op jit(solution)/shard_map/all_to_all | solution.py:204
  39.2 9.2 %all_to_all.31.bias_in_ref = bf16[4,2,8,16,128]{4,3,2,1,0:T(8,128)(2,1)S(1)} all-to-all(bf16[4,2,8,16,128]{4,3,2,1,0:T(8,128)(2,1)S(1)} %broadcast_in_dim.5), channel_id=1, replica_groups=mesh['x'=4,'zh'=4,'core'=2,'zl'=2,'y'=8] {'x'}, dimensions={0} | all-to-all | bytes 524288 | tf_op jit(solution)/shard_map/all_to_all | solution.py:204
  48.4 5.0 %shard_map.77 = (bf16[8,16,128]{2,1,0:T(8,128)(2,1)S(1)}, bf16[8,8,16,128]{3,2,1,0:T(8,128)(2,1)}, bf16[4,8,16,128]{3,2,1,0:T(8,128)(2,1)S(1)}, bf16[4,8,16,128]{3,2,1,0:T(8,128)(2,1)S(1)}) custom-call(bf16[8,48,128]{2,1,0:T(8,128)(2,1)S(1)} %all_to_all.30.pack_ref, bf16[8,8,16,128]{3,2,1,0:T(8,128)(2,1)S(1)} %all-to-all-done.1.kv_in_ref, ...), custom_call_target="tpu_custom_call" | custom-call | tf_op jit(solution)/shard_map/pallas_call | solution.py:189
  53.4 3.4 %all-to-all-start.3 = ((bf16[8,8,16,128]{3,2,1,0:T(8,128)(2,1)}), bf16[8,8,16,128]{3,2,1,0:T(8,128)(2,1)S(1)}, u32[]{:S(2)}, u32[]{:S(2)}) async-start(bf16[8,8,16,128]{3,2,1,0:T(8,128)(2,1)} %get-tuple-element.20), calls=%async_computation.3 | async-start | bytes 524288 | tf_op jit(solution)/shard_map/all_to_all | solution.py:204
  56.8 1.9 %collective-permute-start.1 = (bf16[4,8,16,128]{3,2,1,0:T(8,128)(2,1)S(1)}, bf16[4,8,16,128]{3,2,1,0:T(8,128)(2,1)S(1)}, u32[]{:S(2)}, u32[]{:S(2)}) collective-permute-start(bf16[4,8,16,128]{3,2,1,0:T(8,128)(2,1)S(1)} %get-tuple-element.22), channel_id=1, source_target_pairs={{0,16},{16,0},{1,17},{17,1},{2,18},{18,2},{3,19},{19,3},{4,20},{20... | collective-permute-start | bytes 393224 | tf_op jit(solution)/shard_map/ppermute | solution.py:208
  58.7 1.3 %collective-permute-done.1.got_ref = bf16[4,8,16,128]{3,2,1,0:T(8,128)(2,1)S(1)} collective-permute-done((bf16[4,8,16,128]{3,2,1,0:T(8,128)(2,1)S(1)}, bf16[4,8,16,128]{3,2,1,0:T(8,128)(2,1)S(1)}, u32[]{:S(2)}, u32[]{:S(2)}) %collective-permute-start.1) | collective-permute-done | bytes 131104 | tf_op jit(solution)/shard_map/ppermute | solution.py:208
  60.1 7.1 %all-to-all-done.3.dkv_ref = bf16[8,8,16,128]{3,2,1,0:T(8,128)(2,1)S(1)} async-done(((bf16[8,8,16,128]{3,2,1,0:T(8,128)(2,1)}), bf16[8,8,16,128]{3,2,1,0:T(8,128)(2,1)S(1)}, u32[]{:S(2)}, u32[]{:S(2)}) %all-to-all-start.3) | async-done | bytes 262176 | tf_op jit(solution)/shard_map/all_to_all | solution.py:204
  67.2 8.3 %all_to_all.32.db_ref = bf16[4,8,16,128]{3,2,1,0:T(8,128)(2,1)S(1)} all-to-all(bf16[4,8,16,128]{3,2,1,0:T(8,128)(2,1)S(1)} %shard_map.78), channel_id=1, replica_groups=mesh['x'=4,'zh'=4,'core'=2,'zl'=2,'y'=8] {'x'}, dimensions={0} | all-to-all | bytes 262144 | tf_op jit(solution)/shard_map/all_to_all | solution.py:204
  75.5 0.1 shard_map.79
  75.6 0.0 copy-start
  75.6 0.0 copy-start.1
  75.6 0.0 copy-start.2
  75.6 10.7 %all_to_all.33.pack_ref = bf16[8,48,128]{2,1,0:T(8,128)(2,1)S(1)} all-to-all(bf16[8,48,128]{2,1,0:T(8,128)(2,1)S(1)} %shard_map.79), channel_id=1, replica_groups=mesh['x'=4,'zh'=4,'core'=2,'zl'=2,'y'=8] {'zl','zh'}, dimensions={0} | all-to-all | bytes 196608 | tf_op jit(solution)/shard_map/all_to_all | solution.py:204
  86.3 0.0 copy-done
  86.3 0.0 copy-done.1
  86.3 0.0 copy-done.2
  86.3 1.0 %shard_map.80 = (bf16[128,64]{1,0:T(8,128)(2,1)}, bf16[128,64]{1,0:T(8,128)(2,1)}, f32[8,2,1024]{2,1,0:T(2,128)}) custom-call(bf16[8,48,128]{2,1,0:T(8,128)(2,1)S(1)} %all_to_all.33.pack_ref, f32[200,128]{1,0:T(8,128)S(1)} %copy-done.1, bf16[64,256]{1,0:T(8,128)(2,1)S(1)} %copy-done, bf16[64,64]{1,0:T(8,128)(2,1)S(1)} %copy-done.2), custom_call_target="tpu_custom_call" | custom-call | tf_op jit(solution)/shard_map/pallas_call | solution.py:189
  (4 shorter events, 0.1 us)
Async XLA Ops:
  21.4 17.8 %all-to-all-start.1 = ((bf16[8,8,16,128]{3,2,1,0:T(8,128)(2,1)}), bf16[8,8,16,128]{3,2,1,0:T(8,128)(2,1)S(1)}, u32[]{:S(2)}, u32[]{:S(2)}) async-start(bf16[8,8,16,128]{3,2,1,0:T(8,128)(2,1)} %broadcast_in_dim.4), calls=%async_computation.1 | async-start | bytes 524288 | tf_op jit(solution)/shard_map/all_to_all | solution.py:204
  28.5 3.1 %collective-permute-start = (bf16[8,16,128]{2,1,0:T(8,128)(2,1)S(1)}, bf16[8,16,128]{2,1,0:T(8,128)(2,1)S(1)}, u32[]{:S(2)}, u32[]{:S(2)}) collective-permute-start(bf16[8,16,128]{2,1,0:T(8,128)(2,1)S(1)} %get-tuple-element.30), channel_id=1, source_target_pairs={{0,16},{16,0},{1,17},{17,1},{2,18},{18,2},{3,19},{19,3},{4,20},{20... | collective-permute-start | bytes 98312 | tf_op jit(solution)/shard_map/ppermute | solution.py:208
  53.4 13.8 %all-to-all-start.3 = ((bf16[8,8,16,128]{3,2,1,0:T(8,128)(2,1)}), bf16[8,8,16,128]{3,2,1,0:T(8,128)(2,1)S(1)}, u32[]{:S(2)}, u32[]{:S(2)}) async-start(bf16[8,8,16,128]{3,2,1,0:T(8,128)(2,1)} %get-tuple-element.20), calls=%async_computation.3 | async-start | bytes 524288 | tf_op jit(solution)/shard_map/all_to_all | solution.py:204
  56.8 3.2 %collective-permute-start.1 = (bf16[4,8,16,128]{3,2,1,0:T(8,128)(2,1)S(1)}, bf16[4,8,16,128]{3,2,1,0:T(8,128)(2,1)S(1)}, u32[]{:S(2)}, u32[]{:S(2)}) collective-permute-start(bf16[4,8,16,128]{3,2,1,0:T(8,128)(2,1)S(1)} %get-tuple-element.22), channel_id=1, source_target_pairs={{0,16},{16,0},{1,17},{17,1},{2,18},{18,2},{3,19},{19,3},{4,20},{20... | collective-permute-start | bytes 393224 | tf_op jit(solution)/shard_map/ppermute | solution.py:208
  75.6 10.7 %copy-start = (bf16[64,256]{1,0:T(8,128)(2,1)S(1)}, bf16[64,256]{1,0:T(8,128)(2,1)}, u32[]{:S(2)}) copy-start(bf16[64,256]{1,0:T(8,128)(2,1)} %wm_ref.1) | copy-start | bytes 98308
  75.6 10.7 %copy-start.1 = (f32[200,128]{1,0:T(8,128)S(1)}, f32[200,128]{1,0:T(8,128)}, u32[]{:S(2)}) copy-start(f32[200,128]{1,0:T(8,128)} %get-tuple-element.25.save_ref) | copy-start | bytes 307204
  75.6 10.7 %copy-start.2 = (bf16[64,64]{1,0:T(8,128)(2,1)S(1)}, bf16[64,64]{1,0:T(8,128)(2,1)}, u32[]{:S(2)}) copy-start(bf16[64,64]{1,0:T(8,128)(2,1)} %wf_ref.1) | copy-start | bytes 24580

commit v8 on v7

--- a/solution.py
+++ b/solution.py
@@ -47,15 +47,16 @@
         pack_ref[h] = jnp.concatenate(parts, 0).astype(jnp.bfloat16)
 
 
-def attend_kernel(pack_ref, kv_in_ref, bias_in_ref, oq_ref, dkv_ref, keep_ref, give_ref,
-                  wide_ref, bias_ref, acc_ref, tmp_ref, kv_ref, t_ref, pair_ref):
+GROUPS = [(zl, x) for zl in range(2) for x in range(4)]
+
+
+def bias_kernel(own_ref, sibling_ref, bias_ref, wide_ref, tmp_ref):
     core = lax.axis_index("core")
     for x in range(4):
         for h in range(8):
-            wide_ref[x * 2 + core, h] = bias_in_ref[x, 0, h].astype(jnp.float32)
-            wide_ref[x * 2 + 1 - core, h] = bias_in_ref[x, 1, h].astype(jnp.float32)
-    groups = [(zl, x) for zl in range(2) for x in range(4)]
-    for i, (zl, x) in enumerate(groups):
+            wide_ref[x * 2 + core, h] = own_ref[x, h].astype(jnp.float32)
+            wide_ref[x * 2 + 1 - core, h] = sibling_ref[x, h].astype(jnp.float32)
+    for i, (zl, x) in enumerate(GROUPS):
         for zh in range(4):
             for half in range(2):
                 at = (zh * 2 + half) * 16
@@ -63,6 +64,25 @@
     for i in range(8):
         for c in range(8):
             bias_ref[i * 16 : i * 16 + 16, c * 128 : c * 128 + 128] = tmp_ref[i, pl.ds(c, 16, stride=8)]
+
+
+def bias_grad_kernel(acc_ref, keep_ref, give_ref, wide_ref, tmp_ref):
+    core = lax.axis_index("core")
+    for i in range(8):
+        for c in range(8):
+            tmp_ref[i, pl.ds(c, 16, stride=8)] = acc_ref[i * 16 : i * 16 + 16, c * 128 : c * 128 + 128]
+    for i, (zl, x) in enumerate(GROUPS):
+        for zh in range(4):
+            for half in range(2):
+                at = (zh * 2 + half) * 16
+                wide_ref[x * 2 + half, zl * 4 + zh] = tmp_ref[i, at : at + 16]
+    for x in range(4):
+        for h in range(8):
+            keep_ref[x, h] = wide_ref[x * 2 + core, h].astype(jnp.bfloat16)
+            give_ref[x, h] = wide_ref[x * 2 + 1 - core, h].astype(jnp.bfloat16)
+
+
+def attend_kernel(pack_ref, kv_in_ref, bias_ref, oq_ref, dkv_ref, acc_ref, kv_ref, t_ref, pair_ref):
     left = lax.broadcasted_iota(jnp.int32, (128, 16), 1) < HEAD_DIM
     blocks = [slice(at, at + 16) for at in range(0, 128, 16)]
     queries, cots, tops, sums, deltas, scaled, attns = [], [], [], [], [], [], []
@@ -76,10 +96,12 @@
         queries.append(jnp.where(left, rows, 0.0))
         cots.append(jnp.where(left, 0.0, rows))
     for n in range(8):
-        scores = tdot(queries[n].astype(jnp.bfloat16), kv_ref[n], 1, 0)
+        q = queries[n].astype(jnp.bfloat16)
         top = []
-        for b in blocks:
-            t = scores[b] + bias_ref[b]
+        for i, b in enumerate(blocks):
+            if i % 4 == 0:
+                scores = tdot(q[i * 16 : i * 16 + 64], kv_ref[n], 1, 0)
+            t = scores[i % 4 * 16 : i % 4 * 16 + 16] + bias_ref[b]
             t_ref[n, b] = t
             top.append(jnp.max(t, 1, keepdims=True))
         tops.append(top)
@@ -97,16 +119,18 @@
         scaled.append(d)
         attns.append(attn)
         deltas.append(jnp.sum(d.astype(jnp.float32) * attn, 1, keepdims=True))
-    for n in range(8):
-        dp = tdot(scaled[n], kv_ref[n], 1, 0)
-        for i, b in enumerate(blocks):
-            e = pair_ref[n, 128 + i * 16 : 144 + i * 16].astype(jnp.float32)
-            ds = e * (dp[b] - deltas[n][b])
-            pair_ref[n, b] = ds.astype(jnp.bfloat16)
-            if n == 0:
-                acc_ref[b] = ds
-            else:
-                acc_ref[b] += ds
+    for n in range(0, 8, 2):
+        for half in (slice(0, 64), slice(64, 128)):
+            dps = [tdot(scaled[m][half], kv_ref[m], 1, 0) for m in (n, n + 1)]
+            for at in range(0, 64, 16):
+                b = slice(half.start + at, half.start + at + 16)
+                both = None
+                for m, dp in zip((n, n + 1), dps):
+                    e = pair_ref[m, 128 + b.start : 128 + b.stop].astype(jnp.float32)
+                    ds = e * (dp[at : at + 16] - deltas[m][b])
+                    pair_ref[m, b] = ds.astype(jnp.bfloat16)
+                    both = ds if both is None else both + ds
+                acc_ref[b] = both if n == 0 else acc_ref[b] + both
     outs, grads = [], []
     for n in range(8):
         dq = tdot(pair_ref[n, 0:128], kv_ref[n], 1, 1)
@@ -123,18 +147,6 @@
                 dkv_ref[y, zl * 4 + dl] = jnp.concatenate(
                     [grads[dl * 2 + s][:, part_y] for s in range(2)], 1
                 )
-    for i in range(8):
-        for c in range(8):
-            tmp_ref[i, pl.ds(c, 16, stride=8)] = acc_ref[i * 16 : i * 16 + 16, c * 128 : c * 128 + 128]
-    for i, (zl, x) in enumerate(groups):
-        for zh in range(4):
-            for half in range(2):
-                at = (zh * 2 + half) * 16
-                wide_ref[x * 2 + half, zl * 4 + zh] = tmp_ref[i, at : at + 16]
-    for x in range(4):
-        for h in range(8):
-            keep_ref[x, h] = wide_ref[x * 2 + core, h].astype(jnp.bfloat16)
-            give_ref[x, h] = wide_ref[x * 2 + 1 - core, h].astype(jnp.bfloat16)
 
 
 def join_kernel(keep_ref, got_ref, out_ref):
@@ -220,23 +232,22 @@
         space=pltpu.HBM, limit=60,
     )
     pack = exchange(pack, HEAD_AXES)
-    own = pack[:, 16:32]
+    rows = pack[:, 32:48]
+    rows = exchange(jnp.broadcast_to(rows[None], (4,) + rows.shape), ("x",))
+    own, rows = lax.optimization_barrier((pack[:, 16:32], rows))
     kv = exchange(jnp.broadcast_to(own[None], (8,) + own.shape), KEY_AXES)
-    own = pack[:, 32:48]
-    pair = jnp.stack([own, swap_core(own)])
-    kv, pair = lax.optimization_barrier((kv, pair))
-    bias_rows = exchange(jnp.broadcast_to(pair[None], (4,) + pair.shape), ("x",))
+    layout = [pltpu.VMEM((8, 8, 16, 128), f32), pltpu.VMEM((8, 128, 128), f32)]
+    (bias_rows,) = call(bias_kernel, [shape(128, 1024, dtype=f32)], rows, swap_core(rows), scratch=layout)
     block, quad, octet = shape(8, 16, 128), shape(4, 8, 16, 128), shape(8, 8, 16, 128)
-    oq, dkv, keep, give = call(
+    oq, dkv, acc = call(
         attend_kernel,
-        [block, octet, quad, quad],
+        [block, octet, shape(128, 1024, dtype=f32)],
         pack, kv, bias_rows,
-        scratch=[pltpu.VMEM((8, 8, 16, 128), f32), pltpu.VMEM((128, 1024), f32),
-                 pltpu.VMEM((128, 1024), f32), pltpu.VMEM((8, 128, 128), f32),
-                 pltpu.VMEM((8, 16, 1024), jnp.bfloat16), pltpu.VMEM((8, 128, 1024), f32),
+        scratch=[pltpu.VMEM((8, 16, 1024), jnp.bfloat16), pltpu.VMEM((8, 128, 1024), f32),
                  pltpu.VMEM((8, 256, 1024), jnp.bfloat16)],
     )
     dkv = exchange(dkv, KEY_AXES)
+    keep, give = call(bias_grad_kernel, [quad, quad], acc, scratch=layout)
     (db,) = call(join_kernel, [quad], keep, swap_core(give))
     dkv, db = lax.optimization_barrier((dkv, db))
     db = exchange(db, ("x",))

time: 88.6 us -> 87.4 us (0.986)
    pallas_call x5 -> x7, Pallas kernels: 7.88 us -> 8.03 us  [call(): pl.pallas_call(kernel, out_shape=outs, in_specs=[pl.BlockSpec(memory_spac...]
where the time goes in v8:
time: 87.4 us; the launch traced here: 86.1 us
  blocking collectives  45.6 us (52%)
  waiting for transfers between devices  16.7 us (19%)
  starting transfers between devices  14.3 us (16%)
  Pallas kernels  8.03 us (9%)
    all_to_all x4, blocking collectives, exchange(): return lax.all_to_all(a, axes, 0, 0, tiled=True)  45.6 us
    all_to_all x2, waiting for transfers between devices, exchange(): return lax.all_to_all(a, axes, 0, 0, tiled=True)  14 us
    all_to_all x2, starting transfers between devices, exchange(): return lax.all_to_all(a, axes, 0, 0, tiled=True)  10.5 us
    pallas_call x7, Pallas kernels, call(): pl.pallas_call(kernel, out_shape=outs, in_specs=[pl.BlockSpec(memory_spac...  8.03 us
    ppermute x2, starting transfers between devices, swap_core(): return lax.ppermute(a, 'core', [(0, 1), (1, 0)])  3.83 us
    ppermute x2, waiting for transfers between devices, swap_core(): return lax.ppermute(a, 'core', [(0, 1), (1, 0)])  2.63 us
  transfers between devices with their start and end apart: 4, of which 4 were waited for; matrix products, arithmetic and copies ran while one was open for 0% of the time, Pallas kernels for 0%

profile of v8, /device:TPU:6, one launch (start us, length us, event | category | flops | bytes accessed | tf_op | source)
XLA Modules:
  0.0 86.1 jit_solution(14962971687687222126)
XLA Ops:
  0.6 1.8 %shard_map.76 = (bf16[8,48,128]{2,1,0:T(8,128)(2,1)}, f32[200,128]{1,0:T(8,128)}) custom-call(bf16[128,64]{1,0:T(8,128)(2,1)} %bitcast.4, bf16[128,64]{1,0:T(8,128)(2,1)} %bitcast.5, bf16[64,256]{1,0:T(8,128)(2,1)} %wm_ref.1, bf16[64,64]{1,0:T(8,128)(2,1)} %wf_ref.1, bf16[8,2,1024]{2,1,0:T(2,128)(2,1)} %bias_hbm.1), custom_call_target="tpu_custom_call" | custom-call | tf_op jit(solution)/shard_map/pallas_call | solution.py:201
  2.5 18.1 %all_to_all.30.pack_ref = bf16[8,48,128]{2,1,0:T(8,128)(2,1)S(1)} all-to-all(bf16[8,48,128]{2,1,0:T(8,128)(2,1)} %get-tuple-element.17), channel_id=1, replica_groups=mesh['x'=4,'zh'=4,'core'=2,'zl'=2,'y'=8] {'zl','zh'}, dimensions={0} | all-to-all | bytes 196608 | tf_op jit(solution)/shard_map/all_to_all | solution.py:216
  20.6 8.5 %all_to_all.31.own_ref = bf16[4,8,16,128]{3,2,1,0:T(8,128)(2,1)S(1)} all-to-all(bf16[4,8,16,128]{3,2,1,0:T(8,128)(2,1)S(1)} %broadcast_in_dim.4), channel_id=1, replica_groups=mesh['x'=4,'zh'=4,'core'=2,'zl'=2,'y'=8] {'x'}, dimensions={0} | all-to-all | bytes 262144 | tf_op jit(solution)/shard_map/all_to_all | solution.py:216
  29.1 0.7 broadcast_in_dim.5
  29.8 7.1 %all-to-all-start.2 = ((bf16[8,8,16,128]{3,2,1,0:T(8,128)(2,1)}), bf16[8,8,16,128]{3,2,1,0:T(8,128)(2,1)S(1)}, u32[]{:S(2)}, u32[]{:S(2)}) async-start(bf16[8,8,16,128]{3,2,1,0:T(8,128)(2,1)} %broadcast_in_dim.5), calls=%async_computation.2 | async-start | bytes 524288 | tf_op jit(solution)/shard_map/all_to_all | solution.py:216
  37.0 1.9 %collective-permute-start = (bf16[4,8,16,128]{3,2,1,0:T(8,128)(2,1)S(1)}, bf16[4,8,16,128]{3,2,1,0:T(8,128)(2,1)S(1)}, u32[]{:S(2)}, u32[]{:S(2)}) collective-permute-start(bf16[4,8,16,128]{3,2,1,0:T(8,128)(2,1)S(1)} %all_to_all.31.own_ref), channel_id=1, source_target_pairs={{0,16},{16,0},{1,17},{17,1},{2,18},{18,2},{3,19},{19,3},{4,20},{20... | collective-permute-start | bytes 393224 | tf_op jit(solution)/shard_map/ppermute | solution.py:220
  38.9 1.3 %collective-permute-done.sibling_ref = bf16[4,8,16,128]{3,2,1,0:T(8,128)(2,1)S(1)} collective-permute-done((bf16[4,8,16,128]{3,2,1,0:T(8,128)(2,1)S(1)}, bf16[4,8,16,128]{3,2,1,0:T(8,128)(2,1)S(1)}, u32[]{:S(2)}, u32[]{:S(2)}) %collective-permute-start) | collective-permute-done | bytes 131104 | tf_op jit(solution)/shard_map/ppermute | solution.py:220
  40.2 0.2 shard_map.77.bias_ref
  40.4 7.1 %all-to-all-done.2.kv_in_ref = bf16[8,8,16,128]{3,2,1,0:T(8,128)(2,1)S(1)} async-done(((bf16[8,8,16,128]{3,2,1,0:T(8,128)(2,1)}), bf16[8,8,16,128]{3,2,1,0:T(8,128)(2,1)S(1)}, u32[]{:S(2)}, u32[]{:S(2)}) %all-to-all-start.2) | async-done | bytes 262176 | tf_op jit(solution)/shard_map/all_to_all | solution.py:216
  47.4 4.8 %shard_map.78 = (bf16[8,16,128]{2,1,0:T(8,128)(2,1)S(1)}, bf16[8,8,16,128]{3,2,1,0:T(8,128)(2,1)}, f32[128,1024]{1,0:T(8,128)S(1)}) custom-call(bf16[8,48,128]{2,1,0:T(8,128)(2,1)S(1)} %all_to_all.30.pack_ref, bf16[8,8,16,128]{3,2,1,0:T(8,128)(2,1)S(1)} %all-to-all-done.2.kv_in_ref, f32[128,1024]{1,0:T(8,128)S(1)} %shard_map.77.bias_ref), custom_call_target="tpu_custom_call" | custom-call | tf_op jit(solution)/shard_map/pallas_call | solution.py:201
  52.3 3.4 %all-to-all-start.3 = ((bf16[8,8,16,128]{3,2,1,0:T(8,128)(2,1)}), bf16[8,8,16,128]{3,2,1,0:T(8,128)(2,1)S(1)}, u32[]{:S(2)}, u32[]{:S(2)}) async-start(bf16[8,8,16,128]{3,2,1,0:T(8,128)(2,1)} %get-tuple-element.21), calls=%async_computation.3 | async-start | bytes 524288 | tf_op jit(solution)/shard_map/all_to_all | solution.py:216
  55.7 0.1 shard_map.79
  55.8 1.9 %collective-permute-start.1 = (bf16[4,8,16,128]{3,2,1,0:T(8,128)(2,1)S(1)}, bf16[4,8,16,128]{3,2,1,0:T(8,128)(2,1)S(1)}, u32[]{:S(2)}, u32[]{:S(2)}) collective-permute-start(bf16[4,8,16,128]{3,2,1,0:T(8,128)(2,1)S(1)} %get-tuple-element.24), channel_id=1, source_target_pairs={{0,16},{16,0},{1,17},{17,1},{2,18},{18,2},{3,19},{19,3},{4,20},{20... | collective-permute-start | bytes 393224 | tf_op jit(solution)/shard_map/ppermute | solution.py:220
  57.8 1.3 %collective-permute-done.1.got_ref = bf16[4,8,16,128]{3,2,1,0:T(8,128)(2,1)S(1)} collective-permute-done((bf16[4,8,16,128]{3,2,1,0:T(8,128)(2,1)S(1)}, bf16[4,8,16,128]{3,2,1,0:T(8,128)(2,1)S(1)}, u32[]{:S(2)}, u32[]{:S(2)}) %collective-permute-start.1) | collective-permute-done | bytes 131104 | tf_op jit(solution)/shard_map/ppermute | solution.py:220
  59.1 7.0 %all-to-all-done.3.dkv_ref = bf16[8,8,16,128]{3,2,1,0:T(8,128)(2,1)S(1)} async-done(((bf16[8,8,16,128]{3,2,1,0:T(8,128)(2,1)}), bf16[8,8,16,128]{3,2,1,0:T(8,128)(2,1)S(1)}, u32[]{:S(2)}, u32[]{:S(2)}) %all-to-all-start.3) | async-done | bytes 262176 | tf_op jit(solution)/shard_map/all_to_all | solution.py:216
  66.1 8.4 %all_to_all.32.db_ref = bf16[4,8,16,128]{3,2,1,0:T(8,128)(2,1)S(1)} all-to-all(bf16[4,8,16,128]{3,2,1,0:T(8,128)(2,1)S(1)} %shard_map.80), channel_id=1, replica_groups=mesh['x'=4,'zh'=4,'core'=2,'zl'=2,'y'=8] {'x'}, dimensions={0} | all-to-all | bytes 262144 | tf_op jit(solution)/shard_map/all_to_all | solution.py:216
  74.4 0.1 shard_map.81
  74.5 0.0 copy-start
  74.5 0.0 copy-start.1
  74.5 0.0 copy-start.2
  74.5 10.6 %all_to_all.33.pack_ref = bf16[8,48,128]{2,1,0:T(8,128)(2,1)S(1)} all-to-all(bf16[8,48,128]{2,1,0:T(8,128)(2,1)S(1)} %shard_map.81), channel_id=1, replica_groups=mesh['x'=4,'zh'=4,'core'=2,'zl'=2,'y'=8] {'zl','zh'}, dimensions={0} | all-to-all | bytes 196608 | tf_op jit(solution)/shard_map/all_to_all | solution.py:216
  85.1 0.0 copy-done
  85.1 0.0 copy-done.1
  85.1 0.0 copy-done.2
  85.1 1.0 %shard_map.82 = (bf16[128,64]{1,0:T(8,128)(2,1)}, bf16[128,64]{1,0:T(8,128)(2,1)}, f32[8,2,1024]{2,1,0:T(2,128)}) custom-call(bf16[8,48,128]{2,1,0:T(8,128)(2,1)S(1)} %all_to_all.33.pack_ref, f32[200,128]{1,0:T(8,128)S(1)} %copy-done.1, bf16[64,256]{1,0:T(8,128)(2,1)S(1)} %copy-done, bf16[64,64]{1,0:T(8,128)(2,1)S(1)} %copy-done.2), custom_call_target="tpu_custom_call" | custom-call | tf_op jit(solution)/shard_map/pallas_call | solution.py:201
  (3 shorter events, 0.1 us)
Async XLA Ops:
  29.8 17.6 %all-to-all-start.2 = ((bf16[8,8,16,128]{3,2,1,0:T(8,128)(2,1)}), bf16[8,8,16,128]{3,2,1,0:T(8,128)(2,1)S(1)}, u32[]{:S(2)}, u32[]{:S(2)}) async-start(bf16[8,8,16,128]{3,2,1,0:T(8,128)(2,1)} %broadcast_in_dim.5), calls=%async_computation.2 | async-start | bytes 524288 | tf_op jit(solution)/shard_map/all_to_all | solution.py:216
  37.0 3.2 %collective-permute-start = (bf16[4,8,16,128]{3,2,1,0:T(8,128)(2,1)S(1)}, bf16[4,8,16,128]{3,2,1,0:T(8,128)(2,1)S(1)}, u32[]{:S(2)}, u32[]{:S(2)}) collective-permute-start(bf16[4,8,16,128]{3,2,1,0:T(8,128)(2,1)S(1)} %all_to_all.31.own_ref), channel_id=1, source_target_pairs={{0,16},{16,0},{1,17},{17,1},{2,18},{18,2},{3,19},{19,3},{4,20},{20... | collective-permute-start | bytes 393224 | tf_op jit(solution)/shard_map/ppermute | solution.py:220
  52.3 13.8 %all-to-all-start.3 = ((bf16[8,8,16,128]{3,2,1,0:T(8,128)(2,1)}), bf16[8,8,16,128]{3,2,1,0:T(8,128)(2,1)S(1)}, u32[]{:S(2)}, u32[]{:S(2)}) async-start(bf16[8,8,16,128]{3,2,1,0:T(8,128)(2,1)} %get-tuple-element.21), calls=%async_computation.3 | async-start | bytes 524288 | tf_op jit(solution)/shard_map/all_to_all | solution.py:216
  55.8 3.2 %collective-permute-start.1 = (bf16[4,8,16,128]{3,2,1,0:T(8,128)(2,1)S(1)}, bf16[4,8,16,128]{3,2,1,0:T(8,128)(2,1)S(1)}, u32[]{:S(2)}, u32[]{:S(2)}) collective-permute-start(bf16[4,8,16,128]{3,2,1,0:T(8,128)(2,1)S(1)} %get-tuple-element.24), channel_id=1, source_target_pairs={{0,16},{16,0},{1,17},{17,1},{2,18},{18,2},{3,19},{19,3},{4,20},{20... | collective-permute-start | bytes 393224 | tf_op jit(solution)/shard_map/ppermute | solution.py:220
  74.5 10.7 %copy-start = (bf16[64,256]{1,0:T(8,128)(2,1)S(1)}, bf16[64,256]{1,0:T(8,128)(2,1)}, u32[]{:S(2)}) copy-start(bf16[64,256]{1,0:T(8,128)(2,1)} %wm_ref.1) | copy-start | bytes 98308
  74.5 10.6 %copy-start.1 = (f32[200,128]{1,0:T(8,128)S(1)}, f32[200,128]{1,0:T(8,128)}, u32[]{:S(2)}) copy-start(f32[200,128]{1,0:T(8,128)} %get-tuple-element.27.save_ref) | copy-start | bytes 307204
  74.5 10.6 %copy-start.2 = (bf16[64,64]{1,0:T(8,128)(2,1)S(1)}, bf16[64,64]{1,0:T(8,128)(2,1)}, u32[]{:S(2)}) copy-start(bf16[64,64]{1,0:T(8,128)(2,1)} %wf_ref.1) | copy-start | bytes 24580

commit v9 on v8

--- a/solution.py
+++ b/solution.py
@@ -28,14 +28,17 @@
     copies = [pltpu.make_async_copy(a, b, sems.at[i]) for i, (a, b) in enumerate(pairs)]
     for copy in copies:
         copy.start()
-    for copy in copies:
-        copy.wait()
+    copies[0].wait()
     x = x_ref[...].astype(jnp.float32).T
     cent = x - jnp.mean(x, 0, keepdims=True)
     rstd = lax.rsqrt(jnp.mean(cent * cent, 0, keepdims=True) + EPS)
     xhat = cent * rstd
+    copies[1].wait()
     proj = tdot(wm_ref[...], xhat.astype(jnp.bfloat16), 0, 0)
     g = jax.nn.sigmoid(proj[192:256])
+    copies[2].wait()
+    copies[3].wait()
+    copies[4].wait()
     d_gated = tdot(wf_ref[...], rc_ref[...], 1, 1)
     d_attn = d_gated * g
     save_ref[...] = jnp.concatenate([xhat, g, d_gated, jnp.broadcast_to(rstd, (8, 128))], 0)
@@ -85,58 +88,60 @@
 def attend_kernel(pack_ref, kv_in_ref, bias_ref, oq_ref, dkv_ref, acc_ref, kv_ref, t_ref, pair_ref):
     left = lax.broadcasted_iota(jnp.int32, (128, 16), 1) < HEAD_DIM
     blocks = [slice(at, at + 16) for at in range(0, 128, 16)]
-    queries, cots, tops, sums, deltas, scaled, attns = [], [], [], [], [], [], []
-    for n in range(8):
+    upper = lax.broadcasted_iota(jnp.int32, (16, 128), 0) < HEAD_DIM
+    state = [{} for n in range(8)]
+
+    def score(n, at):
         dl, lanes = n // 2, slice(n % 2 * 64, n % 2 * 64 + 64)
         kv_ref[n] = jnp.concatenate(
             [kv_in_ref[y, zl * 4 + dl][:, lanes] for zl in range(2) for y in range(8)], 1
         )
         qd = jnp.concatenate([pack_ref[zl * 4 + dl, 0:16][:, lanes] for zl in range(2)], 1)
-        rows = qd.astype(jnp.float32).T
-        queries.append(jnp.where(left, rows, 0.0))
-        cots.append(jnp.where(left, 0.0, rows))
-    for n in range(8):
-        q = queries[n].astype(jnp.bfloat16)
-        top = []
-        for i, b in enumerate(blocks):
-            if i % 4 == 0:
-                scores = tdot(q[i * 16 : i * 16 + 64], kv_ref[n], 1, 0)
-            t = scores[i % 4 * 16 : i % 4 * 16 + 16] + bias_ref[b]
+        qd = qd.astype(jnp.float32)
+        rows = qd.T
+        q = jnp.where(left, rows, 0.0).astype(jnp.bfloat16)
+        at["q"], at["d"] = jnp.where(upper, qd, 0.0), jnp.where(left, 0.0, rows)
+        scores = tdot(q, kv_ref[n], 1, 0)
+        at["top"] = []
+        for b in blocks:
+            t = scores[b] + bias_ref[b]
             t_ref[n, b] = t
-            top.append(jnp.max(t, 1, keepdims=True))
-        tops.append(top)
-    for n in range(8):
+            at["top"].append(jnp.max(t, 1, keepdims=True))
+
+    def exponentiate(n, at):
         total = []
         for i, b in enumerate(blocks):
-            e = jnp.exp(t_ref[n, b] - tops[n][i])
+            e = jnp.exp(t_ref[n, b] - at["top"][i])
             total.append(jnp.sum(e, 1, keepdims=True))
             pair_ref[n, 128 + i * 16 : 144 + i * 16] = e.astype(jnp.bfloat16)
-        sums.append(jnp.concatenate(total, 0))
-    for n in range(8):
-        inverse = 1.0 / sums[n]
-        attn = tdot(pair_ref[n, 128:256], kv_ref[n], 1, 1) * inverse
-        d = (cots[n] * inverse).astype(jnp.bfloat16)
-        scaled.append(d)
-        attns.append(attn)
-        deltas.append(jnp.sum(d.astype(jnp.float32) * attn, 1, keepdims=True))
-    for n in range(0, 8, 2):
-        for half in (slice(0, 64), slice(64, 128)):
-            dps = [tdot(scaled[m][half], kv_ref[m], 1, 0) for m in (n, n + 1)]
-            for at in range(0, 64, 16):
-                b = slice(half.start + at, half.start + at + 16)
-                both = None
-                for m, dp in zip((n, n + 1), dps):
-                    e = pair_ref[m, 128 + b.start : 128 + b.stop].astype(jnp.float32)
-                    ds = e * (dp[at : at + 16] - deltas[m][b])
-                    pair_ref[m, b] = ds.astype(jnp.bfloat16)
-                    both = ds if both is None else both + ds
-                acc_ref[b] = both if n == 0 else acc_ref[b] + both
-    outs, grads = [], []
-    for n in range(8):
+        at["sum"] = jnp.concatenate(total, 0)
+
+    def attend(n, at):
+        inverse = 1.0 / at["sum"]
+        at["attn"] = tdot(pair_ref[n, 128:256], kv_ref[n], 1, 1) * inverse
+        at["scaled"] = (at["d"] * inverse).astype(jnp.bfloat16)
+        at["delta"] = jnp.sum(at["scaled"].astype(jnp.float32) * at["attn"], 1, keepdims=True)
+
+    def differentiate(n, at):
+        dp = tdot(at["scaled"], kv_ref[n], 1, 0)
+        for i, b in enumerate(blocks):
+            e = pair_ref[n, 128 + i * 16 : 144 + i * 16].astype(jnp.float32)
+            ds = e * (dp[b] - at["delta"][b])
+            pair_ref[n, b] = ds.astype(jnp.bfloat16)
+            acc_ref[b] = ds if n == 0 else acc_ref[b] + ds
+
+    def multiply(n, at):
         dq = tdot(pair_ref[n, 0:128], kv_ref[n], 1, 1)
-        outs.append(jnp.where(left, dq, attns[n]).T.astype(jnp.bfloat16))
-        lhs = jnp.concatenate([queries[n].T, scaled[n].astype(jnp.float32).T], 1)
-        grads.append(tdot(lhs.astype(jnp.bfloat16), pair_ref[n], 1, 0).astype(jnp.bfloat16))
+        at["out"] = jnp.where(left, dq, at["attn"]).T.astype(jnp.bfloat16)
+        lhs = jnp.concatenate([at["q"], at["scaled"].astype(jnp.float32).T], 1)
+        at["grad"] = tdot(lhs.astype(jnp.bfloat16), pair_ref[n], 1, 0).astype(jnp.bfloat16)
+
+    stages = [score, exponentiate, attend, differentiate, multiply]
+    for step in range(8 + len(stages) - 1):
+        for lag, stage in enumerate(stages):
+            if 0 <= step - lag < 8:
+                stage(step - lag, state[step - lag])
+    outs, grads = [at["out"] for at in state], [at["grad"] for at in state]
     for dl in range(4):
         for zl in range(2):
             part = slice(zl * 64, zl * 64 + 64)

time: 87.4 us -> 87.3 us (level)
  no operation moved by 1% of the time
where the time goes in v9:
time: 87.3 us; the launch traced here: 86 us
  blocking collectives  45.6 us (52%)
  waiting for transfers between devices  16.7 us (19%)
  starting transfers between devices  14.3 us (16%)
  Pallas kernels  7.88 us (9%)
    all_to_all x4, blocking collectives, exchange(): return lax.all_to_all(a, axes, 0, 0, tiled=True)  45.6 us
    all_to_all x2, waiting for transfers between devices, exchange(): return lax.all_to_all(a, axes, 0, 0, tiled=True)  14 us
    all_to_all x2, starting transfers between devices, exchange(): return lax.all_to_all(a, axes, 0, 0, tiled=True)  10.5 us
    pallas_call x7, Pallas kernels, call(): pl.pallas_call(kernel, out_shape=outs, in_specs=[pl.BlockSpec(memory_spac...  7.88 us
    ppermute x2, starting transfers between devices, swap_core(): return lax.ppermute(a, 'core', [(0, 1), (1, 0)])  3.83 us
    ppermute x2, waiting for transfers between devices, swap_core(): return lax.ppermute(a, 'core', [(0, 1), (1, 0)])  2.63 us
  transfers between devices with their start and end apart: 4, of which 4 were waited for; matrix products, arithmetic and copies ran while one was open for 0% of the time, Pallas kernels for 0%

profile of v9, /device:TPU:6, one launch (start us, length us, event | category | flops | bytes accessed | tf_op | source)
XLA Modules:
  0.0 86.0 jit_solution(12937090170156152662)
XLA Ops:
  0.6 2.0 %shard_map.76 = (bf16[8,48,128]{2,1,0:T(8,128)(2,1)}, f32[200,128]{1,0:T(8,128)}) custom-call(bf16[128,64]{1,0:T(8,128)(2,1)} %bitcast.4, bf16[128,64]{1,0:T(8,128)(2,1)} %bitcast.5, bf16[64,256]{1,0:T(8,128)(2,1)} %wm_ref.1, bf16[64,64]{1,0:T(8,128)(2,1)} %wf_ref.1, bf16[8,2,1024]{2,1,0:T(2,128)(2,1)} %bias_hbm.1), custom_call_target="tpu_custom_call" | custom-call | tf_op jit(solution)/shard_map/pallas_call | solution.py:206
  2.6 18.1 %all_to_all.30.pack_ref = bf16[8,48,128]{2,1,0:T(8,128)(2,1)S(1)} all-to-all(bf16[8,48,128]{2,1,0:T(8,128)(2,1)} %get-tuple-element.17), channel_id=1, replica_groups=mesh['x'=4,'zh'=4,'core'=2,'zl'=2,'y'=8] {'zl','zh'}, dimensions={0} | all-to-all | bytes 196608 | tf_op jit(solution)/shard_map/all_to_all | solution.py:221
  20.8 8.5 %all_to_all.31.own_ref = bf16[4,8,16,128]{3,2,1,0:T(8,128)(2,1)S(1)} all-to-all(bf16[4,8,16,128]{3,2,1,0:T(8,128)(2,1)S(1)} %broadcast_in_dim.4), channel_id=1, replica_groups=mesh['x'=4,'zh'=4,'core'=2,'zl'=2,'y'=8] {'x'}, dimensions={0} | all-to-all | bytes 262144 | tf_op jit(solution)/shard_map/all_to_all | solution.py:221
  29.3 0.7 broadcast_in_dim.5
  30.0 7.1 %all-to-all-start.2 = ((bf16[8,8,16,128]{3,2,1,0:T(8,128)(2,1)}), bf16[8,8,16,128]{3,2,1,0:T(8,128)(2,1)S(1)}, u32[]{:S(2)}, u32[]{:S(2)}) async-start(bf16[8,8,16,128]{3,2,1,0:T(8,128)(2,1)} %broadcast_in_dim.5), calls=%async_computation.2 | async-start | bytes 524288 | tf_op jit(solution)/shard_map/all_to_all | solution.py:221
  37.1 1.9 %collective-permute-start = (bf16[4,8,16,128]{3,2,1,0:T(8,128)(2,1)S(1)}, bf16[4,8,16,128]{3,2,1,0:T(8,128)(2,1)S(1)}, u32[]{:S(2)}, u32[]{:S(2)}) collective-permute-start(bf16[4,8,16,128]{3,2,1,0:T(8,128)(2,1)S(1)} %all_to_all.31.own_ref), channel_id=1, source_target_pairs={{0,16},{16,0},{1,17},{17,1},{2,18},{18,2},{3,19},{19,3},{4,20},{20... | collective-permute-start | bytes 393224 | tf_op jit(solution)/shard_map/ppermute | solution.py:225
  39.0 1.3 %collective-permute-done.sibling_ref = bf16[4,8,16,128]{3,2,1,0:T(8,128)(2,1)S(1)} collective-permute-done((bf16[4,8,16,128]{3,2,1,0:T(8,128)(2,1)S(1)}, bf16[4,8,16,128]{3,2,1,0:T(8,128)(2,1)S(1)}, u32[]{:S(2)}, u32[]{:S(2)}) %collective-permute-start) | collective-permute-done | bytes 131104 | tf_op jit(solution)/shard_map/ppermute | solution.py:225
  40.3 0.2 shard_map.77.bias_ref
  40.5 7.1 %all-to-all-done.2.kv_in_ref = bf16[8,8,16,128]{3,2,1,0:T(8,128)(2,1)S(1)} async-done(((bf16[8,8,16,128]{3,2,1,0:T(8,128)(2,1)}), bf16[8,8,16,128]{3,2,1,0:T(8,128)(2,1)S(1)}, u32[]{:S(2)}, u32[]{:S(2)}) %all-to-all-start.2) | async-done | bytes 262176 | tf_op jit(solution)/shard_map/all_to_all | solution.py:221
  47.6 4.5 %shard_map.78 = (bf16[8,16,128]{2,1,0:T(8,128)(2,1)S(1)}, bf16[8,8,16,128]{3,2,1,0:T(8,128)(2,1)}, f32[128,1024]{1,0:T(8,128)S(1)}) custom-call(bf16[8,48,128]{2,1,0:T(8,128)(2,1)S(1)} %all_to_all.30.pack_ref, bf16[8,8,16,128]{3,2,1,0:T(8,128)(2,1)S(1)} %all-to-all-done.2.kv_in_ref, f32[128,1024]{1,0:T(8,128)S(1)} %shard_map.77.bias_ref), custom_call_target="tpu_custom_call" | custom-call | tf_op jit(solution)/shard_map/pallas_call | solution.py:206
  52.1 3.4 %all-to-all-start.3 = ((bf16[8,8,16,128]{3,2,1,0:T(8,128)(2,1)}), bf16[8,8,16,128]{3,2,1,0:T(8,128)(2,1)S(1)}, u32[]{:S(2)}, u32[]{:S(2)}) async-start(bf16[8,8,16,128]{3,2,1,0:T(8,128)(2,1)} %get-tuple-element.21), calls=%async_computation.3 | async-start | bytes 524288 | tf_op jit(solution)/shard_map/all_to_all | solution.py:221
  55.5 0.1 shard_map.79
  55.7 1.9 %collective-permute-start.1 = (bf16[4,8,16,128]{3,2,1,0:T(8,128)(2,1)S(1)}, bf16[4,8,16,128]{3,2,1,0:T(8,128)(2,1)S(1)}, u32[]{:S(2)}, u32[]{:S(2)}) collective-permute-start(bf16[4,8,16,128]{3,2,1,0:T(8,128)(2,1)S(1)} %get-tuple-element.24), channel_id=1, source_target_pairs={{0,16},{16,0},{1,17},{17,1},{2,18},{18,2},{3,19},{19,3},{4,20},{20... | collective-permute-start | bytes 393224 | tf_op jit(solution)/shard_map/ppermute | solution.py:225
  57.6 1.3 %collective-permute-done.1.got_ref = bf16[4,8,16,128]{3,2,1,0:T(8,128)(2,1)S(1)} collective-permute-done((bf16[4,8,16,128]{3,2,1,0:T(8,128)(2,1)S(1)}, bf16[4,8,16,128]{3,2,1,0:T(8,128)(2,1)S(1)}, u32[]{:S(2)}, u32[]{:S(2)}) %collective-permute-start.1) | collective-permute-done | bytes 131104 | tf_op jit(solution)/shard_map/ppermute | solution.py:225
  59.0 7.0 %all-to-all-done.3.dkv_ref = bf16[8,8,16,128]{3,2,1,0:T(8,128)(2,1)S(1)} async-done(((bf16[8,8,16,128]{3,2,1,0:T(8,128)(2,1)}), bf16[8,8,16,128]{3,2,1,0:T(8,128)(2,1)S(1)}, u32[]{:S(2)}, u32[]{:S(2)}) %all-to-all-start.3) | async-done | bytes 262176 | tf_op jit(solution)/shard_map/all_to_all | solution.py:221
  65.9 8.3 %all_to_all.32.db_ref = bf16[4,8,16,128]{3,2,1,0:T(8,128)(2,1)S(1)} all-to-all(bf16[4,8,16,128]{3,2,1,0:T(8,128)(2,1)S(1)} %shard_map.80), channel_id=1, replica_groups=mesh['x'=4,'zh'=4,'core'=2,'zl'=2,'y'=8] {'x'}, dimensions={0} | all-to-all | bytes 262144 | tf_op jit(solution)/shard_map/all_to_all | solution.py:221
  74.3 0.1 shard_map.81
  74.3 0.0 copy-start
  74.3 0.0 copy-start.1
  74.3 0.0 copy-start.2
  74.4 10.6 %all_to_all.33.pack_ref = bf16[8,48,128]{2,1,0:T(8,128)(2,1)S(1)} all-to-all(bf16[8,48,128]{2,1,0:T(8,128)(2,1)S(1)} %shard_map.81), channel_id=1, replica_groups=mesh['x'=4,'zh'=4,'core'=2,'zl'=2,'y'=8] {'zl','zh'}, dimensions={0} | all-to-all | bytes 196608 | tf_op jit(solution)/shard_map/all_to_all | solution.py:221
  85.0 0.0 copy-done
  85.0 0.0 copy-done.1
  85.0 0.0 copy-done.2
  85.0 1.0 %shard_map.82 = (bf16[128,64]{1,0:T(8,128)(2,1)}, bf16[128,64]{1,0:T(8,128)(2,1)}, f32[8,2,1024]{2,1,0:T(2,128)}) custom-call(bf16[8,48,128]{2,1,0:T(8,128)(2,1)S(1)} %all_to_all.33.pack_ref, f32[200,128]{1,0:T(8,128)S(1)} %copy-done.1, bf16[64,256]{1,0:T(8,128)(2,1)S(1)} %copy-done, bf16[64,64]{1,0:T(8,128)(2,1)S(1)} %copy-done.2), custom_call_target="tpu_custom_call" | custom-call | tf_op jit(solution)/shard_map/pallas_call | solution.py:206
  (3 shorter events, 0.1 us)
Async XLA Ops:
  30.0 17.6 %all-to-all-start.2 = ((bf16[8,8,16,128]{3,2,1,0:T(8,128)(2,1)}), bf16[8,8,16,128]{3,2,1,0:T(8,128)(2,1)S(1)}, u32[]{:S(2)}, u32[]{:S(2)}) async-start(bf16[8,8,16,128]{3,2,1,0:T(8,128)(2,1)} %broadcast_in_dim.5), calls=%async_computation.2 | async-start | bytes 524288 | tf_op jit(solution)/shard_map/all_to_all | solution.py:221
  37.1 3.2 %collective-permute-start = (bf16[4,8,16,128]{3,2,1,0:T(8,128)(2,1)S(1)}, bf16[4,8,16,128]{3,2,1,0:T(8,128)(2,1)S(1)}, u32[]{:S(2)}, u32[]{:S(2)}) collective-permute-start(bf16[4,8,16,128]{3,2,1,0:T(8,128)(2,1)S(1)} %all_to_all.31.own_ref), channel_id=1, source_target_pairs={{0,16},{16,0},{1,17},{17,1},{2,18},{18,2},{3,19},{19,3},{4,20},{20... | collective-permute-start | bytes 393224 | tf_op jit(solution)/shard_map/ppermute | solution.py:225
  52.1 13.8 %all-to-all-start.3 = ((bf16[8,8,16,128]{3,2,1,0:T(8,128)(2,1)}), bf16[8,8,16,128]{3,2,1,0:T(8,128)(2,1)S(1)}, u32[]{:S(2)}, u32[]{:S(2)}) async-start(bf16[8,8,16,128]{3,2,1,0:T(8,128)(2,1)} %get-tuple-element.21), calls=%async_computation.3 | async-start | bytes 524288 | tf_op jit(solution)/shard_map/all_to_all | solution.py:221
  55.7 3.2 %collective-permute-start.1 = (bf16[4,8,16,128]{3,2,1,0:T(8,128)(2,1)S(1)}, bf16[4,8,16,128]{3,2,1,0:T(8,128)(2,1)S(1)}, u32[]{:S(2)}, u32[]{:S(2)}) collective-permute-start(bf16[4,8,16,128]{3,2,1,0:T(8,128)(2,1)S(1)} %get-tuple-element.24), channel_id=1, source_target_pairs={{0,16},{16,0},{1,17},{17,1},{2,18},{18,2},{3,19},{19,3},{4,20},{20... | collective-permute-start | bytes 393224 | tf_op jit(solution)/shard_map/ppermute | solution.py:225
  74.3 10.7 %copy-start = (bf16[64,256]{1,0:T(8,128)(2,1)S(1)}, bf16[64,256]{1,0:T(8,128)(2,1)}, u32[]{:S(2)}) copy-start(bf16[64,256]{1,0:T(8,128)(2,1)} %wm_ref.1) | copy-start | bytes 98308
  74.3 10.7 %copy-start.1 = (f32[200,128]{1,0:T(8,128)S(1)}, f32[200,128]{1,0:T(8,128)}, u32[]{:S(2)}) copy-start(f32[200,128]{1,0:T(8,128)} %get-tuple-element.27.save_ref) | copy-start | bytes 307204
  74.3 10.7 %copy-start.2 = (bf16[64,64]{1,0:T(8,128)(2,1)S(1)}, bf16[64,64]{1,0:T(8,128)(2,1)}, u32[]{:S(2)}) copy-start(bf16[64,64]{1,0:T(8,128)(2,1)} %wf_ref.1) | copy-start | bytes 24580

commit v10 on v9

--- a/solution.py
+++ b/solution.py
@@ -28,17 +28,14 @@
     copies = [pltpu.make_async_copy(a, b, sems.at[i]) for i, (a, b) in enumerate(pairs)]
     for copy in copies:
         copy.start()
-    copies[0].wait()
+    for copy in copies:
+        copy.wait()
     x = x_ref[...].astype(jnp.float32).T
     cent = x - jnp.mean(x, 0, keepdims=True)
     rstd = lax.rsqrt(jnp.mean(cent * cent, 0, keepdims=True) + EPS)
     xhat = cent * rstd
-    copies[1].wait()
     proj = tdot(wm_ref[...], xhat.astype(jnp.bfloat16), 0, 0)
     g = jax.nn.sigmoid(proj[192:256])
-    copies[2].wait()
-    copies[3].wait()
-    copies[4].wait()
     d_gated = tdot(wf_ref[...], rc_ref[...], 1, 1)
     d_attn = d_gated * g
     save_ref[...] = jnp.concatenate([xhat, g, d_gated, jnp.broadcast_to(rstd, (8, 128))], 0)
@@ -90,18 +87,20 @@
     blocks = [slice(at, at + 16) for at in range(0, 128, 16)]
     upper = lax.broadcasted_iota(jnp.int32, (16, 128), 0) < HEAD_DIM
     state = [{} for n in range(8)]
+    ones = jnp.ones((16, 1024), jnp.bfloat16)
 
     def score(n, at):
         dl, lanes = n // 2, slice(n % 2 * 64, n % 2 * 64 + 64)
-        kv_ref[n] = jnp.concatenate(
+        kv_ref[n, 0:16] = jnp.concatenate(
             [kv_in_ref[y, zl * 4 + dl][:, lanes] for zl in range(2) for y in range(8)], 1
         )
+        kv_ref[n, 16:32] = ones
         qd = jnp.concatenate([pack_ref[zl * 4 + dl, 0:16][:, lanes] for zl in range(2)], 1)
         qd = qd.astype(jnp.float32)
         rows = qd.T
         q = jnp.where(left, rows, 0.0).astype(jnp.bfloat16)
         at["q"], at["d"] = jnp.where(upper, qd, 0.0), jnp.where(left, 0.0, rows)
-        scores = tdot(q, kv_ref[n], 1, 0)
+        scores = tdot(q, kv_ref[n, 0:16], 1, 0)
         at["top"] = []
         for b in blocks:
             t = scores[b] + bias_ref[b]
@@ -109,21 +108,19 @@
             at["top"].append(jnp.max(t, 1, keepdims=True))
 
     def exponentiate(n, at):
-        total = []
         for i, b in enumerate(blocks):
             e = jnp.exp(t_ref[n, b] - at["top"][i])
-            total.append(jnp.sum(e, 1, keepdims=True))
             pair_ref[n, 128 + i * 16 : 144 + i * 16] = e.astype(jnp.bfloat16)
-        at["sum"] = jnp.concatenate(total, 0)
 
     def attend(n, at):
-        inverse = 1.0 / at["sum"]
-        at["attn"] = tdot(pair_ref[n, 128:256], kv_ref[n], 1, 1) * inverse
+        summed = tdot(pair_ref[n, 128:256], kv_ref[n], 1, 1)
+        inverse = 1.0 / summed[:, 16:32]
+        at["attn"] = summed[:, 0:16] * inverse
         at["scaled"] = (at["d"] * inverse).astype(jnp.bfloat16)
         at["delta"] = jnp.sum(at["scaled"].astype(jnp.float32) * at["attn"], 1, keepdims=True)
 
     def differentiate(n, at):
-        dp = tdot(at["scaled"], kv_ref[n], 1, 0)
+        dp = tdot(at["scaled"], kv_ref[n, 0:16], 1, 0)
         for i, b in enumerate(blocks):
             e = pair_ref[n, 128 + i * 16 : 144 + i * 16].astype(jnp.float32)
             ds = e * (dp[b] - at["delta"][b])
@@ -131,7 +128,7 @@
             acc_ref[b] = ds if n == 0 else acc_ref[b] + ds
 
     def multiply(n, at):
-        dq = tdot(pair_ref[n, 0:128], kv_ref[n], 1, 1)
+        dq = tdot(pair_ref[n, 0:128], kv_ref[n, 0:16], 1, 1)
         at["out"] = jnp.where(left, dq, at["attn"]).T.astype(jnp.bfloat16)
         lhs = jnp.concatenate([at["q"], at["scaled"].astype(jnp.float32).T], 1)
         at["grad"] = tdot(lhs.astype(jnp.bfloat16), pair_ref[n], 1, 0).astype(jnp.bfloat16)
@@ -239,8 +236,9 @@
     pack = exchange(pack, HEAD_AXES)
     rows = pack[:, 32:48]
     rows = exchange(jnp.broadcast_to(rows[None], (4,) + rows.shape), ("x",))
-    own, rows = lax.optimization_barrier((pack[:, 16:32], rows))
-    kv = exchange(jnp.broadcast_to(own[None], (8,) + own.shape), KEY_AXES)
+    own = jnp.broadcast_to(pack[None, :, 16:32], (8, 8, 16, 128))
+    own, rows = lax.optimization_barrier((own, rows))
+    kv = exchange(own, KEY_AXES)
     layout = [pltpu.VMEM((8, 8, 16, 128), f32), pltpu.VMEM((8, 128, 128), f32)]
     (bias_rows,) = call(bias_kernel, [shape(128, 1024, dtype=f32)], rows, swap_core(rows), scratch=layout)
     block, quad, octet = shape(8, 16, 128), shape(4, 8, 16, 128), shape(8, 8, 16, 128)
@@ -248,7 +246,7 @@
         attend_kernel,
         [block, octet, shape(128, 1024, dtype=f32)],
         pack, kv, bias_rows,
-        scratch=[pltpu.VMEM((8, 16, 1024), jnp.bfloat16), pltpu.VMEM((8, 128, 1024), f32),
+        scratch=[pltpu.VMEM((8, 32, 1024), jnp.bfloat16), pltpu.VMEM((8, 128, 1024), f32),
                  pltpu.VMEM((8, 256, 1024), jnp.bfloat16)],
     )
     dkv = exchange(dkv, KEY_AXES)

time: 87.3 us -> 87 us (level)
  no operation moved by 1% of the time
where the time goes in v10:
time: 87 us; the launch traced here: 85.7 us
  blocking collectives  45.6 us (52%)
  waiting for transfers between devices  16.7 us (19%)
  starting transfers between devices  14.3 us (16%)
  Pallas kernels  7.64 us (9%)
    all_to_all x4, blocking collectives, exchange(): return lax.all_to_all(a, axes, 0, 0, tiled=True)  45.6 us
    all_to_all x2, waiting for transfers between devices, exchange(): return lax.all_to_all(a, axes, 0, 0, tiled=True)  14 us
    all_to_all x2, starting transfers between devices, exchange(): return lax.all_to_all(a, axes, 0, 0, tiled=True)  10.5 us
    pallas_call x7, Pallas kernels, call(): pl.pallas_call(kernel, out_shape=outs, in_specs=[pl.BlockSpec(memory_spac...  7.64 us
    ppermute x2, starting transfers between devices, swap_core(): return lax.ppermute(a, 'core', [(0, 1), (1, 0)])  3.83 us
    ppermute x2, waiting for transfers between devices, swap_core(): return lax.ppermute(a, 'core', [(0, 1), (1, 0)])  2.63 us
  transfers between devices with their start and end apart: 4, of which 4 were waited for; matrix products, arithmetic and copies ran while one was open for 0% of the time, Pallas kernels for 0%

profile of v10, /device:TPU:6, one launch (start us, length us, event | category | flops | bytes accessed | tf_op | source)
XLA Modules:
  0.0 85.7 jit_solution(1464478613619087577)
XLA Ops:
  0.6 1.8 %shard_map.76 = (bf16[8,48,128]{2,1,0:T(8,128)(2,1)}, f32[200,128]{1,0:T(8,128)}) custom-call(bf16[128,64]{1,0:T(8,128)(2,1)} %bitcast.4, bf16[128,64]{1,0:T(8,128)(2,1)} %bitcast.5, bf16[64,256]{1,0:T(8,128)(2,1)} %wm_ref.1, bf16[64,64]{1,0:T(8,128)(2,1)} %wf_ref.1, bf16[8,2,1024]{2,1,0:T(2,128)(2,1)} %bias_hbm.1), custom_call_target="tpu_custom_call" | custom-call | tf_op jit(solution)/shard_map/pallas_call | solution.py:203
  2.5 18.1 %all_to_all.30.pack_ref = bf16[8,48,128]{2,1,0:T(8,128)(2,1)S(1)} all-to-all(bf16[8,48,128]{2,1,0:T(8,128)(2,1)} %get-tuple-element.17), channel_id=1, replica_groups=mesh['x'=4,'zh'=4,'core'=2,'zl'=2,'y'=8] {'zl','zh'}, dimensions={0} | all-to-all | bytes 196608 | tf_op jit(solution)/shard_map/all_to_all | solution.py:218
  20.6 8.5 %all_to_all.31.own_ref = bf16[4,8,16,128]{3,2,1,0:T(8,128)(2,1)S(1)} all-to-all(bf16[4,8,16,128]{3,2,1,0:T(8,128)(2,1)S(1)} %broadcast_in_dim.5), channel_id=1, replica_groups=mesh['x'=4,'zh'=4,'core'=2,'zl'=2,'y'=8] {'x'}, dimensions={0} | all-to-all | bytes 262144 | tf_op jit(solution)/shard_map/all_to_all | solution.py:218
  29.1 0.7 broadcast_in_dim.4
  29.8 7.1 %all-to-all-start.2 = ((bf16[8,8,16,128]{3,2,1,0:T(8,128)(2,1)}), bf16[8,8,16,128]{3,2,1,0:T(8,128)(2,1)S(1)}, u32[]{:S(2)}, u32[]{:S(2)}) async-start(bf16[8,8,16,128]{3,2,1,0:T(8,128)(2,1)} %broadcast_in_dim.4), calls=%async_computation.2 | async-start | bytes 524288 | tf_op jit(solution)/shard_map/all_to_all | solution.py:218
  37.0 1.9 %collective-permute-start = (bf16[4,8,16,128]{3,2,1,0:T(8,128)(2,1)S(1)}, bf16[4,8,16,128]{3,2,1,0:T(8,128)(2,1)S(1)}, u32[]{:S(2)}, u32[]{:S(2)}) collective-permute-start(bf16[4,8,16,128]{3,2,1,0:T(8,128)(2,1)S(1)} %all_to_all.31.own_ref), channel_id=1, source_target_pairs={{0,16},{16,0},{1,17},{17,1},{2,18},{18,2},{3,19},{19,3},{4,20},{20... | collective-permute-start | bytes 393224 | tf_op jit(solution)/shard_map/ppermute | solution.py:222
  38.9 1.3 %collective-permute-done.sibling_ref = bf16[4,8,16,128]{3,2,1,0:T(8,128)(2,1)S(1)} collective-permute-done((bf16[4,8,16,128]{3,2,1,0:T(8,128)(2,1)S(1)}, bf16[4,8,16,128]{3,2,1,0:T(8,128)(2,1)S(1)}, u32[]{:S(2)}, u32[]{:S(2)}) %collective-permute-start) | collective-permute-done | bytes 131104 | tf_op jit(solution)/shard_map/ppermute | solution.py:222
  40.2 0.2 shard_map.77.bias_ref
  40.4 7.1 %all-to-all-done.2.kv_in_ref = bf16[8,8,16,128]{3,2,1,0:T(8,128)(2,1)S(1)} async-done(((bf16[8,8,16,128]{3,2,1,0:T(8,128)(2,1)}), bf16[8,8,16,128]{3,2,1,0:T(8,128)(2,1)S(1)}, u32[]{:S(2)}, u32[]{:S(2)}) %all-to-all-start.2) | async-done | bytes 262176 | tf_op jit(solution)/shard_map/all_to_all | solution.py:218
  47.4 4.4 %shard_map.78 = (bf16[8,16,128]{2,1,0:T(8,128)(2,1)S(1)}, bf16[8,8,16,128]{3,2,1,0:T(8,128)(2,1)}, f32[128,1024]{1,0:T(8,128)S(1)}) custom-call(bf16[8,48,128]{2,1,0:T(8,128)(2,1)S(1)} %all_to_all.30.pack_ref, bf16[8,8,16,128]{3,2,1,0:T(8,128)(2,1)S(1)} %all-to-all-done.2.kv_in_ref, f32[128,1024]{1,0:T(8,128)S(1)} %shard_map.77.bias_ref), custom_call_target="tpu_custom_call" | custom-call | tf_op jit(solution)/shard_map/pallas_call | solution.py:203
  51.9 3.4 %all-to-all-start.3 = ((bf16[8,8,16,128]{3,2,1,0:T(8,128)(2,1)}), bf16[8,8,16,128]{3,2,1,0:T(8,128)(2,1)S(1)}, u32[]{:S(2)}, u32[]{:S(2)}) async-start(bf16[8,8,16,128]{3,2,1,0:T(8,128)(2,1)} %get-tuple-element.21), calls=%async_computation.3 | async-start | bytes 524288 | tf_op jit(solution)/shard_map/all_to_all | solution.py:218
  55.3 0.1 shard_map.79
  55.4 1.9 %collective-permute-start.1 = (bf16[4,8,16,128]{3,2,1,0:T(8,128)(2,1)S(1)}, bf16[4,8,16,128]{3,2,1,0:T(8,128)(2,1)S(1)}, u32[]{:S(2)}, u32[]{:S(2)}) collective-permute-start(bf16[4,8,16,128]{3,2,1,0:T(8,128)(2,1)S(1)} %get-tuple-element.24), channel_id=1, source_target_pairs={{0,16},{16,0},{1,17},{17,1},{2,18},{18,2},{3,19},{19,3},{4,20},{20... | collective-permute-start | bytes 393224 | tf_op jit(solution)/shard_map/ppermute | solution.py:222
  57.4 1.3 %collective-permute-done.1.got_ref = bf16[4,8,16,128]{3,2,1,0:T(8,128)(2,1)S(1)} collective-permute-done((bf16[4,8,16,128]{3,2,1,0:T(8,128)(2,1)S(1)}, bf16[4,8,16,128]{3,2,1,0:T(8,128)(2,1)S(1)}, u32[]{:S(2)}, u32[]{:S(2)}) %collective-permute-start.1) | collective-permute-done | bytes 131104 | tf_op jit(solution)/shard_map/ppermute | solution.py:222
  58.7 7.0 %all-to-all-done.3.dkv_ref = bf16[8,8,16,128]{3,2,1,0:T(8,128)(2,1)S(1)} async-done(((bf16[8,8,16,128]{3,2,1,0:T(8,128)(2,1)}), bf16[8,8,16,128]{3,2,1,0:T(8,128)(2,1)S(1)}, u32[]{:S(2)}, u32[]{:S(2)}) %all-to-all-start.3) | async-done | bytes 262176 | tf_op jit(solution)/shard_map/all_to_all | solution.py:218
  65.7 8.3 %all_to_all.32.db_ref = bf16[4,8,16,128]{3,2,1,0:T(8,128)(2,1)S(1)} all-to-all(bf16[4,8,16,128]{3,2,1,0:T(8,128)(2,1)S(1)} %shard_map.80), channel_id=1, replica_groups=mesh['x'=4,'zh'=4,'core'=2,'zl'=2,'y'=8] {'x'}, dimensions={0} | all-to-all | bytes 262144 | tf_op jit(solution)/shard_map/all_to_all | solution.py:218
  74.0 0.1 shard_map.81
  74.1 0.0 copy-start
  74.1 0.0 copy-start.1
  74.1 0.0 copy-start.2
  74.1 10.6 %all_to_all.33.pack_ref = bf16[8,48,128]{2,1,0:T(8,128)(2,1)S(1)} all-to-all(bf16[8,48,128]{2,1,0:T(8,128)(2,1)S(1)} %shard_map.81), channel_id=1, replica_groups=mesh['x'=4,'zh'=4,'core'=2,'zl'=2,'y'=8] {'zl','zh'}, dimensions={0} | all-to-all | bytes 196608 | tf_op jit(solution)/shard_map/all_to_all | solution.py:218
  84.7 0.0 copy-done
  84.7 0.0 copy-done.1
  84.7 0.0 copy-done.2
  84.8 1.0 %shard_map.82 = (bf16[128,64]{1,0:T(8,128)(2,1)}, bf16[128,64]{1,0:T(8,128)(2,1)}, f32[8,2,1024]{2,1,0:T(2,128)}) custom-call(bf16[8,48,128]{2,1,0:T(8,128)(2,1)S(1)} %all_to_all.33.pack_ref, f32[200,128]{1,0:T(8,128)S(1)} %copy-done.1, bf16[64,256]{1,0:T(8,128)(2,1)S(1)} %copy-done, bf16[64,64]{1,0:T(8,128)(2,1)S(1)} %copy-done.2), custom_call_target="tpu_custom_call" | custom-call | tf_op jit(solution)/shard_map/pallas_call | solution.py:203
  (3 shorter events, 0.1 us)
Async XLA Ops:
  29.8 17.6 %all-to-all-start.2 = ((bf16[8,8,16,128]{3,2,1,0:T(8,128)(2,1)}), bf16[8,8,16,128]{3,2,1,0:T(8,128)(2,1)S(1)}, u32[]{:S(2)}, u32[]{:S(2)}) async-start(bf16[8,8,16,128]{3,2,1,0:T(8,128)(2,1)} %broadcast_in_dim.4), calls=%async_computation.2 | async-start | bytes 524288 | tf_op jit(solution)/shard_map/all_to_all | solution.py:218
  37.0 3.2 %collective-permute-start = (bf16[4,8,16,128]{3,2,1,0:T(8,128)(2,1)S(1)}, bf16[4,8,16,128]{3,2,1,0:T(8,128)(2,1)S(1)}, u32[]{:S(2)}, u32[]{:S(2)}) collective-permute-start(bf16[4,8,16,128]{3,2,1,0:T(8,128)(2,1)S(1)} %all_to_all.31.own_ref), channel_id=1, source_target_pairs={{0,16},{16,0},{1,17},{17,1},{2,18},{18,2},{3,19},{19,3},{4,20},{20... | collective-permute-start | bytes 393224 | tf_op jit(solution)/shard_map/ppermute | solution.py:222
  51.9 13.8 %all-to-all-start.3 = ((bf16[8,8,16,128]{3,2,1,0:T(8,128)(2,1)}), bf16[8,8,16,128]{3,2,1,0:T(8,128)(2,1)S(1)}, u32[]{:S(2)}, u32[]{:S(2)}) async-start(bf16[8,8,16,128]{3,2,1,0:T(8,128)(2,1)} %get-tuple-element.21), calls=%async_computation.3 | async-start | bytes 524288 | tf_op jit(solution)/shard_map/all_to_all | solution.py:218
  55.4 3.2 %collective-permute-start.1 = (bf16[4,8,16,128]{3,2,1,0:T(8,128)(2,1)S(1)}, bf16[4,8,16,128]{3,2,1,0:T(8,128)(2,1)S(1)}, u32[]{:S(2)}, u32[]{:S(2)}) collective-permute-start(bf16[4,8,16,128]{3,2,1,0:T(8,128)(2,1)S(1)} %get-tuple-element.24), channel_id=1, source_target_pairs={{0,16},{16,0},{1,17},{17,1},{2,18},{18,2},{3,19},{19,3},{4,20},{20... | collective-permute-start | bytes 393224 | tf_op jit(solution)/shard_map/ppermute | solution.py:222
  74.1 10.7 %copy-start = (bf16[64,256]{1,0:T(8,128)(2,1)S(1)}, bf16[64,256]{1,0:T(8,128)(2,1)}, u32[]{:S(2)}) copy-start(bf16[64,256]{1,0:T(8,128)(2,1)} %wm_ref.1) | copy-start | bytes 98308
  74.1 10.6 %copy-start.1 = (f32[200,128]{1,0:T(8,128)S(1)}, f32[200,128]{1,0:T(8,128)}, u32[]{:S(2)}) copy-start(f32[200,128]{1,0:T(8,128)} %get-tuple-element.27.save_ref) | copy-start | bytes 307204
  74.1 10.6 %copy-start.2 = (bf16[64,64]{1,0:T(8,128)(2,1)S(1)}, bf16[64,64]{1,0:T(8,128)(2,1)}, u32[]{:S(2)}) copy-start(bf16[64,64]{1,0:T(8,128)(2,1)} %wf_ref.1) | copy-start | bytes 24580

commit v11 on v10

--- a/solution.py
+++ b/solution.py
@@ -8,14 +8,15 @@
 from jax.sharding import Mesh, PartitionSpec as P
 
 HEADS = 8
+PEER = [y % 4 * 2 + y // 4 for y in range(8)]
 HEAD_DIM = 8
 EPS = 1e-05
 SCALE = 1.0 / math.sqrt(HEAD_DIM)
 
 DEPTH = ("x", "zh", "core")
-RES = ("zl", "y")
+RES = ("zl", "yh", "yl")
 HEAD_AXES = ("zl", "zh")
-KEY_AXES = ("y",)
+KEY_AXES = ("yl", "yh")
 
 
 def tdot(a, b, ca, cb):
@@ -92,7 +93,7 @@
     def score(n, at):
         dl, lanes = n // 2, slice(n % 2 * 64, n % 2 * 64 + 64)
         kv_ref[n, 0:16] = jnp.concatenate(
-            [kv_in_ref[y, zl * 4 + dl][:, lanes] for zl in range(2) for y in range(8)], 1
+            [kv_in_ref[PEER[y], zl * 4 + dl][:, lanes] for zl in range(2) for y in range(8)], 1
         )
         kv_ref[n, 16:32] = ones
         qd = jnp.concatenate([pack_ref[zl * 4 + dl, 0:16][:, lanes] for zl in range(2)], 1)
@@ -146,7 +147,7 @@
             for y in range(8):
                 r = zl * 8 + y
                 part_y = slice(r * 64, r * 64 + 64)
-                dkv_ref[y, zl * 4 + dl] = jnp.concatenate(
+                dkv_ref[PEER[y], zl * 4 + dl] = jnp.concatenate(
                     [grads[dl * 2 + s][:, part_y] for s in range(2)], 1
                 )
 
@@ -265,7 +266,7 @@
 
 
 def solution(mesh):
-    fine = Mesh(mesh.devices.reshape(4, 4, 2, 2, 8), DEPTH + RES)
+    fine = Mesh(mesh.devices.reshape(4, 4, 2, 2, 2, 4), DEPTH + RES)
     tokens = P(DEPTH, RES, None)
     rows = P(None, RES + DEPTH, None)
     return jax.shard_map(

time: 87 us -> 85.1 us (0.978)
  the two profiles are of different devices: /device:TPU:6 before, /device:TPU:8 now
where the time goes in v11:
time: 85.1 us; the launch traced here: 84.5 us
  blocking collectives  47.2 us (55%)
  starting transfers between devices  15 us (18%)
  waiting for transfers between devices  13.2 us (16%)
  Pallas kernels  7.64 us (9%)
    all_to_all x4, blocking collectives, exchange(): return lax.all_to_all(a, axes, 0, 0, tiled=True)  47.2 us
    all_to_all x2, starting transfers between devices, exchange(): return lax.all_to_all(a, axes, 0, 0, tiled=True)  11.2 us
    all_to_all x2, waiting for transfers between devices, exchange(): return lax.all_to_all(a, axes, 0, 0, tiled=True)  10.5 us
    pallas_call x7, Pallas kernels, call(): pl.pallas_call(kernel, out_shape=outs, in_specs=[pl.BlockSpec(memory_spac...  7.64 us
    ppermute x2, starting transfers between devices, swap_core(): return lax.ppermute(a, 'core', [(0, 1), (1, 0)])  3.83 us
    ppermute x2, waiting for transfers between devices, swap_core(): return lax.ppermute(a, 'core', [(0, 1), (1, 0)])  2.63 us
  transfers between devices with their start and end apart: 4, of which 4 were waited for; matrix products, arithmetic and copies ran while one was open for 0% of the time, Pallas kernels for 0%

profile of v11, /device:TPU:8, one launch (start us, length us, event | category | flops | bytes accessed | tf_op | source)
XLA Modules:
  0.0 84.5 jit_solution(15814394006490525504)
XLA Ops:
  0.6 1.8 %shard_map.76 = (bf16[8,48,128]{2,1,0:T(8,128)(2,1)}, f32[200,128]{1,0:T(8,128)}) custom-call(bf16[128,64]{1,0:T(8,128)(2,1)} %bitcast.4, bf16[128,64]{1,0:T(8,128)(2,1)} %bitcast.5, bf16[64,256]{1,0:T(8,128)(2,1)} %wm_ref.1, bf16[64,64]{1,0:T(8,128)(2,1)} %wf_ref.1, bf16[8,2,1024]{2,1,0:T(2,128)(2,1)} %bias_hbm.1), custom_call_target="tpu_custom_call" | custom-call | tf_op jit(solution)/shard_map/pallas_call | solution.py:204
  2.5 18.1 %all_to_all.30.pack_ref = bf16[8,48,128]{2,1,0:T(8,128)(2,1)S(1)} all-to-all(bf16[8,48,128]{2,1,0:T(8,128)(2,1)} %get-tuple-element.17), channel_id=1, replica_groups=mesh['x'=4,'zh'=4,'core'=2,'zl'=2,'yh'=2,'yl'=4] {'zl','zh'}, dimensions={0} | all-to-all | bytes 196608 | tf_op jit(solution)/shard_map/all_to_all | solution.py:219
  20.6 10.1 %all_to_all.31.own_ref = bf16[4,8,16,128]{3,2,1,0:T(8,128)(2,1)S(1)} all-to-all(bf16[4,8,16,128]{3,2,1,0:T(8,128)(2,1)S(1)} %broadcast_in_dim.5), channel_id=1, replica_groups=mesh['x'=4,'zh'=4,'core'=2,'zl'=2,'yh'=2,'yl'=4] {'x'}, dimensions={0} | all-to-all | bytes 262144 | tf_op jit(solution)/shard_map/all_to_all | solution.py:219
  30.7 0.7 broadcast_in_dim.4
  31.4 7.5 %all-to-all-start.2 = ((bf16[8,8,16,128]{3,2,1,0:T(8,128)(2,1)}), bf16[8,8,16,128]{3,2,1,0:T(8,128)(2,1)S(1)}, u32[]{:S(2)}, u32[]{:S(2)}) async-start(bf16[8,8,16,128]{3,2,1,0:T(8,128)(2,1)} %broadcast_in_dim.4), calls=%async_computation.2 | async-start | bytes 524288 | tf_op jit(solution)/shard_map/all_to_all | solution.py:219
  39.0 1.9 %collective-permute-start = (bf16[4,8,16,128]{3,2,1,0:T(8,128)(2,1)S(1)}, bf16[4,8,16,128]{3,2,1,0:T(8,128)(2,1)S(1)}, u32[]{:S(2)}, u32[]{:S(2)}) collective-permute-start(bf16[4,8,16,128]{3,2,1,0:T(8,128)(2,1)S(1)} %all_to_all.31.own_ref), channel_id=1, source_target_pairs={{0,16},{16,0},{1,17},{17,1},{2,18},{18,2},{3,19},{19,3},{4,20},{20... | collective-permute-start | bytes 393224 | tf_op jit(solution)/shard_map/ppermute | solution.py:223
  40.9 1.3 %collective-permute-done.sibling_ref = bf16[4,8,16,128]{3,2,1,0:T(8,128)(2,1)S(1)} collective-permute-done((bf16[4,8,16,128]{3,2,1,0:T(8,128)(2,1)S(1)}, bf16[4,8,16,128]{3,2,1,0:T(8,128)(2,1)S(1)}, u32[]{:S(2)}, u32[]{:S(2)}) %collective-permute-start) | collective-permute-done | bytes 131104 | tf_op jit(solution)/shard_map/ppermute | solution.py:223
  42.2 0.2 shard_map.77.bias_ref
  42.4 5.3 %all-to-all-done.2.kv_in_ref = bf16[8,8,16,128]{3,2,1,0:T(8,128)(2,1)S(1)} async-done(((bf16[8,8,16,128]{3,2,1,0:T(8,128)(2,1)}), bf16[8,8,16,128]{3,2,1,0:T(8,128)(2,1)S(1)}, u32[]{:S(2)}, u32[]{:S(2)}) %all-to-all-start.2) | async-done | bytes 262176 | tf_op jit(solution)/shard_map/all_to_all | solution.py:219
  47.7 4.4 %shard_map.78 = (bf16[8,16,128]{2,1,0:T(8,128)(2,1)S(1)}, bf16[8,8,16,128]{3,2,1,0:T(8,128)(2,1)}, f32[128,1024]{1,0:T(8,128)S(1)}) custom-call(bf16[8,48,128]{2,1,0:T(8,128)(2,1)S(1)} %all_to_all.30.pack_ref, bf16[8,8,16,128]{3,2,1,0:T(8,128)(2,1)S(1)} %all-to-all-done.2.kv_in_ref, f32[128,1024]{1,0:T(8,128)S(1)} %shard_map.77.bias_ref), custom_call_target="tpu_custom_call" | custom-call | tf_op jit(solution)/shard_map/pallas_call | solution.py:204
  52.1 3.7 %all-to-all-start.3 = ((bf16[8,8,16,128]{3,2,1,0:T(8,128)(2,1)}), bf16[8,8,16,128]{3,2,1,0:T(8,128)(2,1)S(1)}, u32[]{:S(2)}, u32[]{:S(2)}) async-start(bf16[8,8,16,128]{3,2,1,0:T(8,128)(2,1)} %get-tuple-element.21), calls=%async_computation.3 | async-start | bytes 524288 | tf_op jit(solution)/shard_map/all_to_all | solution.py:219
  55.8 0.1 shard_map.79
  55.9 1.9 %collective-permute-start.1 = (bf16[4,8,16,128]{3,2,1,0:T(8,128)(2,1)S(1)}, bf16[4,8,16,128]{3,2,1,0:T(8,128)(2,1)S(1)}, u32[]{:S(2)}, u32[]{:S(2)}) collective-permute-start(bf16[4,8,16,128]{3,2,1,0:T(8,128)(2,1)S(1)} %get-tuple-element.24), channel_id=1, source_target_pairs={{0,16},{16,0},{1,17},{17,1},{2,18},{18,2},{3,19},{19,3},{4,20},{20... | collective-permute-start | bytes 393224 | tf_op jit(solution)/shard_map/ppermute | solution.py:223
  57.8 1.3 %collective-permute-done.1.got_ref = bf16[4,8,16,128]{3,2,1,0:T(8,128)(2,1)S(1)} collective-permute-done((bf16[4,8,16,128]{3,2,1,0:T(8,128)(2,1)S(1)}, bf16[4,8,16,128]{3,2,1,0:T(8,128)(2,1)S(1)}, u32[]{:S(2)}, u32[]{:S(2)}) %collective-permute-start.1) | collective-permute-done | bytes 131104 | tf_op jit(solution)/shard_map/ppermute | solution.py:223
  59.2 5.3 %all-to-all-done.3.dkv_ref = bf16[8,8,16,128]{3,2,1,0:T(8,128)(2,1)S(1)} async-done(((bf16[8,8,16,128]{3,2,1,0:T(8,128)(2,1)}), bf16[8,8,16,128]{3,2,1,0:T(8,128)(2,1)S(1)}, u32[]{:S(2)}, u32[]{:S(2)}) %all-to-all-start.3) | async-done | bytes 262176 | tf_op jit(solution)/shard_map/all_to_all | solution.py:219
  64.4 8.3 %all_to_all.32.db_ref = bf16[4,8,16,128]{3,2,1,0:T(8,128)(2,1)S(1)} all-to-all(bf16[4,8,16,128]{3,2,1,0:T(8,128)(2,1)S(1)} %shard_map.80), channel_id=1, replica_groups=mesh['x'=4,'zh'=4,'core'=2,'zl'=2,'yh'=2,'yl'=4] {'x'}, dimensions={0} | all-to-all | bytes 262144 | tf_op jit(solution)/shard_map/all_to_all | solution.py:219
  72.8 0.1 shard_map.81
  72.9 0.0 copy-start
  72.9 0.0 copy-start.1
  72.9 0.0 copy-start.2
  72.9 10.6 %all_to_all.33.pack_ref = bf16[8,48,128]{2,1,0:T(8,128)(2,1)S(1)} all-to-all(bf16[8,48,128]{2,1,0:T(8,128)(2,1)S(1)} %shard_map.81), channel_id=1, replica_groups=mesh['x'=4,'zh'=4,'core'=2,'zl'=2,'yh'=2,'yl'=4] {'zl','zh'}, dimensions={0} | all-to-all | bytes 196608 | tf_op jit(solution)/shard_map/all_to_all | solution.py:219
  83.5 0.0 copy-done
  83.5 0.0 copy-done.1
  83.5 0.0 copy-done.2
  83.5 1.0 %shard_map.82 = (bf16[128,64]{1,0:T(8,128)(2,1)}, bf16[128,64]{1,0:T(8,128)(2,1)}, f32[8,2,1024]{2,1,0:T(2,128)}) custom-call(bf16[8,48,128]{2,1,0:T(8,128)(2,1)S(1)} %all_to_all.33.pack_ref, f32[200,128]{1,0:T(8,128)S(1)} %copy-done.1, bf16[64,256]{1,0:T(8,128)(2,1)S(1)} %copy-done, bf16[64,64]{1,0:T(8,128)(2,1)S(1)} %copy-done.2), custom_call_target="tpu_custom_call" | custom-call | tf_op jit(solution)/shard_map/pallas_call | solution.py:204
  (3 shorter events, 0.1 us)
Async XLA Ops:
  31.4 16.2 %all-to-all-start.2 = ((bf16[8,8,16,128]{3,2,1,0:T(8,128)(2,1)}), bf16[8,8,16,128]{3,2,1,0:T(8,128)(2,1)S(1)}, u32[]{:S(2)}, u32[]{:S(2)}) async-start(bf16[8,8,16,128]{3,2,1,0:T(8,128)(2,1)} %broadcast_in_dim.4), calls=%async_computation.2 | async-start | bytes 524288 | tf_op jit(solution)/shard_map/all_to_all | solution.py:219
  39.0 3.2 %collective-permute-start = (bf16[4,8,16,128]{3,2,1,0:T(8,128)(2,1)S(1)}, bf16[4,8,16,128]{3,2,1,0:T(8,128)(2,1)S(1)}, u32[]{:S(2)}, u32[]{:S(2)}) collective-permute-start(bf16[4,8,16,128]{3,2,1,0:T(8,128)(2,1)S(1)} %all_to_all.31.own_ref), channel_id=1, source_target_pairs={{0,16},{16,0},{1,17},{17,1},{2,18},{18,2},{3,19},{19,3},{4,20},{20... | collective-permute-start | bytes 393224 | tf_op jit(solution)/shard_map/ppermute | solution.py:223
  52.1 12.3 %all-to-all-start.3 = ((bf16[8,8,16,128]{3,2,1,0:T(8,128)(2,1)}), bf16[8,8,16,128]{3,2,1,0:T(8,128)(2,1)S(1)}, u32[]{:S(2)}, u32[]{:S(2)}) async-start(bf16[8,8,16,128]{3,2,1,0:T(8,128)(2,1)} %get-tuple-element.21), calls=%async_computation.3 | async-start | bytes 524288 | tf_op jit(solution)/shard_map/all_to_all | solution.py:219
  55.9 3.2 %collective-permute-start.1 = (bf16[4,8,16,128]{3,2,1,0:T(8,128)(2,1)S(1)}, bf16[4,8,16,128]{3,2,1,0:T(8,128)(2,1)S(1)}, u32[]{:S(2)}, u32[]{:S(2)}) collective-permute-start(bf16[4,8,16,128]{3,2,1,0:T(8,128)(2,1)S(1)} %get-tuple-element.24), channel_id=1, source_target_pairs={{0,16},{16,0},{1,17},{17,1},{2,18},{18,2},{3,19},{19,3},{4,20},{20... | collective-permute-start | bytes 393224 | tf_op jit(solution)/shard_map/ppermute | solution.py:223
  72.9 10.7 %copy-start = (bf16[64,256]{1,0:T(8,128)(2,1)S(1)}, bf16[64,256]{1,0:T(8,128)(2,1)}, u32[]{:S(2)}) copy-start(bf16[64,256]{1,0:T(8,128)(2,1)} %wm_ref.1) | copy-start | bytes 98308
  72.9 10.6 %copy-start.1 = (f32[200,128]{1,0:T(8,128)S(1)}, f32[200,128]{1,0:T(8,128)}, u32[]{:S(2)}) copy-start(f32[200,128]{1,0:T(8,128)} %get-tuple-element.27.save_ref) | copy-start | bytes 307204
  72.9 10.6 %copy-start.2 = (bf16[64,64]{1,0:T(8,128)(2,1)S(1)}, bf16[64,64]{1,0:T(8,128)(2,1)}, u32[]{:S(2)}) copy-start(bf16[64,64]{1,0:T(8,128)(2,1)} %wf_ref.1) | copy-start | bytes 24580

commit v12 on v11

--- a/solution.py
+++ b/solution.py
@@ -8,14 +8,15 @@
 from jax.sharding import Mesh, PartitionSpec as P
 
 HEADS = 8
-PEER = [y % 4 * 2 + y // 4 for y in range(8)]
+PEER = [i % 4 * 2 + i // 4 for i in range(8)]
+SOURCE = [[PEER[zh * 2 + zl] for zh in range(4)] for zl in range(2)]
 HEAD_DIM = 8
 EPS = 1e-05
 SCALE = 1.0 / math.sqrt(HEAD_DIM)
 
-DEPTH = ("x", "zh", "core")
+DEPTH = ("x", "zhh", "zhl", "core")
 RES = ("zl", "yh", "yl")
-HEAD_AXES = ("zl", "zh")
+HEAD_AXES = ("zhl", "zl", "zhh")
 KEY_AXES = ("yl", "yh")
 
 
@@ -61,7 +62,7 @@
         for zh in range(4):
             for half in range(2):
                 at = (zh * 2 + half) * 16
-                tmp_ref[i, at : at + 16] = wide_ref[x * 2 + half, zl * 4 + zh]
+                tmp_ref[i, at : at + 16] = wide_ref[x * 2 + half, SOURCE[zl][zh]]
     for i in range(8):
         for c in range(8):
             bias_ref[i * 16 : i * 16 + 16, c * 128 : c * 128 + 128] = tmp_ref[i, pl.ds(c, 16, stride=8)]
@@ -76,7 +77,7 @@
         for zh in range(4):
             for half in range(2):
                 at = (zh * 2 + half) * 16
-                wide_ref[x * 2 + half, zl * 4 + zh] = tmp_ref[i, at : at + 16]
+                wide_ref[x * 2 + half, SOURCE[zl][zh]] = tmp_ref[i, at : at + 16]
     for x in range(4):
         for h in range(8):
             keep_ref[x, h] = wide_ref[x * 2 + core, h].astype(jnp.bfloat16)
@@ -93,10 +94,10 @@
     def score(n, at):
         dl, lanes = n // 2, slice(n % 2 * 64, n % 2 * 64 + 64)
         kv_ref[n, 0:16] = jnp.concatenate(
-            [kv_in_ref[PEER[y], zl * 4 + dl][:, lanes] for zl in range(2) for y in range(8)], 1
+            [kv_in_ref[PEER[y], SOURCE[zl][dl]][:, lanes] for zl in range(2) for y in range(8)], 1
         )
         kv_ref[n, 16:32] = ones
-        qd = jnp.concatenate([pack_ref[zl * 4 + dl, 0:16][:, lanes] for zl in range(2)], 1)
+        qd = jnp.concatenate([pack_ref[SOURCE[zl][dl], 0:16][:, lanes] for zl in range(2)], 1)
         qd = qd.astype(jnp.float32)
         rows = qd.T
         q = jnp.where(left, rows, 0.0).astype(jnp.bfloat16)
@@ -143,11 +144,11 @@
     for dl in range(4):
         for zl in range(2):
             part = slice(zl * 64, zl * 64 + 64)
-            oq_ref[zl * 4 + dl] = jnp.concatenate([outs[dl * 2 + s][:, part] for s in range(2)], 1)
+            oq_ref[SOURCE[zl][dl]] = jnp.concatenate([outs[dl * 2 + s][:, part] for s in range(2)], 1)
             for y in range(8):
                 r = zl * 8 + y
                 part_y = slice(r * 64, r * 64 + 64)
-                dkv_ref[PEER[y], zl * 4 + dl] = jnp.concatenate(
+                dkv_ref[PEER[y], SOURCE[zl][dl]] = jnp.concatenate(
                     [grads[dl * 2 + s][:, part_y] for s in range(2)], 1
                 )
 
@@ -266,7 +267,7 @@
 
 
 def solution(mesh):
-    fine = Mesh(mesh.devices.reshape(4, 4, 2, 2, 2, 4), DEPTH + RES)
+    fine = Mesh(mesh.devices.reshape(4, 2, 2, 2, 2, 2, 4), DEPTH + RES)
     tokens = P(DEPTH, RES, None)
     rows = P(None, RES + DEPTH, None)
     return jax.shard_map(

time: 85.1 us -> 85 us (level)
  no operation moved by 1% of the time
where the time goes in v12:
time: 85 us; the launch traced here: 84.4 us
  blocking collectives  47.1 us (55%)
  starting transfers between devices  14.7 us (17%)
  waiting for transfers between devices  13.4 us (16%)
  Pallas kernels  7.65 us (9%)
    all_to_all x4, blocking collectives, exchange(): return lax.all_to_all(a, axes, 0, 0, tiled=True)  47.1 us
    all_to_all x2, starting transfers between devices, exchange(): return lax.all_to_all(a, axes, 0, 0, tiled=True)  10.9 us
    all_to_all x2, waiting for transfers between devices, exchange(): return lax.all_to_all(a, axes, 0, 0, tiled=True)  10.8 us
    pallas_call x7, Pallas kernels, call(): pl.pallas_call(kernel, out_shape=outs, in_specs=[pl.BlockSpec(memory_spac...  7.65 us
    ppermute x2, starting transfers between devices, swap_core(): return lax.ppermute(a, 'core', [(0, 1), (1, 0)])  3.83 us
    ppermute x2, waiting for transfers between devices, swap_core(): return lax.ppermute(a, 'core', [(0, 1), (1, 0)])  2.63 us
  transfers between devices with their start and end apart: 4, of which 4 were waited for; matrix products, arithmetic and copies ran while one was open for 0% of the time, Pallas kernels for 0%

profile of v12, /device:TPU:8, one launch (start us, length us, event | category | flops | bytes accessed | tf_op | source)
XLA Modules:
  0.0 84.4 jit_solution(3792895780377126901)
XLA Ops:
  0.6 1.8 %shard_map.76 = (bf16[8,48,128]{2,1,0:T(8,128)(2,1)}, f32[200,128]{1,0:T(8,128)}) custom-call(bf16[128,64]{1,0:T(8,128)(2,1)} %bitcast.4, bf16[128,64]{1,0:T(8,128)(2,1)} %bitcast.5, bf16[64,256]{1,0:T(8,128)(2,1)} %wm_ref.1, bf16[64,64]{1,0:T(8,128)(2,1)} %wf_ref.1, bf16[8,2,1024]{2,1,0:T(2,128)(2,1)} %bias_hbm.1), custom_call_target="tpu_custom_call" | custom-call | tf_op jit(solution)/shard_map/pallas_call | solution.py:205
  2.5 18.1 %all_to_all.30.pack_ref = bf16[8,48,128]{2,1,0:T(8,128)(2,1)S(1)} all-to-all(bf16[8,48,128]{2,1,0:T(8,128)(2,1)} %get-tuple-element.17), channel_id=1, replica_groups=mesh['x'=4,'zhh'=2,'zhl'=2,'core'=2,'zl'=2,'yh'=2,'yl'=4] {'zhl','zl','z..., dimensions={0} | all-to-all | bytes 196608 | tf_op jit(solution)/shard_map/all_to_all | solution.py:220
  20.6 10.1 %all_to_all.31.own_ref = bf16[4,8,16,128]{3,2,1,0:T(8,128)(2,1)S(1)} all-to-all(bf16[4,8,16,128]{3,2,1,0:T(8,128)(2,1)S(1)} %broadcast_in_dim.5), channel_id=1, replica_groups=mesh['x'=4,'zhh'=2,'zhl'=2,'core'=2,'zl'=2,'yh'=2,'yl'=4] {'x'}, dimensions={0} | all-to-all | bytes 262144 | tf_op jit(solution)/shard_map/all_to_all | solution.py:220
  30.7 0.7 broadcast_in_dim.4
  31.4 7.5 %all-to-all-start.2 = ((bf16[8,8,16,128]{3,2,1,0:T(8,128)(2,1)}), bf16[8,8,16,128]{3,2,1,0:T(8,128)(2,1)S(1)}, u32[]{:S(2)}, u32[]{:S(2)}) async-start(bf16[8,8,16,128]{3,2,1,0:T(8,128)(2,1)} %broadcast_in_dim.4), calls=%async_computation.2 | async-start | bytes 524288 | tf_op jit(solution)/shard_map/all_to_all | solution.py:220
  39.0 1.9 %collective-permute-start = (bf16[4,8,16,128]{3,2,1,0:T(8,128)(2,1)S(1)}, bf16[4,8,16,128]{3,2,1,0:T(8,128)(2,1)S(1)}, u32[]{:S(2)}, u32[]{:S(2)}) collective-permute-start(bf16[4,8,16,128]{3,2,1,0:T(8,128)(2,1)S(1)} %all_to_all.31.own_ref), channel_id=1, source_target_pairs={{0,16},{16,0},{1,17},{17,1},{2,18},{18,2},{3,19},{19,3},{4,20},{20... | collective-permute-start | bytes 393224 | tf_op jit(solution)/shard_map/ppermute | solution.py:224
  40.9 1.3 %collective-permute-done.sibling_ref = bf16[4,8,16,128]{3,2,1,0:T(8,128)(2,1)S(1)} collective-permute-done((bf16[4,8,16,128]{3,2,1,0:T(8,128)(2,1)S(1)}, bf16[4,8,16,128]{3,2,1,0:T(8,128)(2,1)S(1)}, u32[]{:S(2)}, u32[]{:S(2)}) %collective-permute-start) | collective-permute-done | bytes 131104 | tf_op jit(solution)/shard_map/ppermute | solution.py:224
  42.2 0.2 shard_map.77.bias_ref
  42.4 5.5 %all-to-all-done.2.kv_in_ref = bf16[8,8,16,128]{3,2,1,0:T(8,128)(2,1)S(1)} async-done(((bf16[8,8,16,128]{3,2,1,0:T(8,128)(2,1)}), bf16[8,8,16,128]{3,2,1,0:T(8,128)(2,1)S(1)}, u32[]{:S(2)}, u32[]{:S(2)}) %all-to-all-start.2) | async-done | bytes 262176 | tf_op jit(solution)/shard_map/all_to_all | solution.py:220
  47.9 4.4 %shard_map.78 = (bf16[8,16,128]{2,1,0:T(8,128)(2,1)S(1)}, bf16[8,8,16,128]{3,2,1,0:T(8,128)(2,1)}, f32[128,1024]{1,0:T(8,128)S(1)}) custom-call(bf16[8,48,128]{2,1,0:T(8,128)(2,1)S(1)} %all_to_all.30.pack_ref, bf16[8,8,16,128]{3,2,1,0:T(8,128)(2,1)S(1)} %all-to-all-done.2.kv_in_ref, f32[128,1024]{1,0:T(8,128)S(1)} %shard_map.77.bias_ref), custom_call_target="tpu_custom_call" | custom-call | tf_op jit(solution)/shard_map/pallas_call | solution.py:205
  52.4 3.4 %all-to-all-start.3 = ((bf16[8,8,16,128]{3,2,1,0:T(8,128)(2,1)}), bf16[8,8,16,128]{3,2,1,0:T(8,128)(2,1)S(1)}, u32[]{:S(2)}, u32[]{:S(2)}) async-start(bf16[8,8,16,128]{3,2,1,0:T(8,128)(2,1)} %get-tuple-element.21), calls=%async_computation.3 | async-start | bytes 524288 | tf_op jit(solution)/shard_map/all_to_all | solution.py:220
  55.8 0.1 shard_map.79
  55.9 1.9 %collective-permute-start.1 = (bf16[4,8,16,128]{3,2,1,0:T(8,128)(2,1)S(1)}, bf16[4,8,16,128]{3,2,1,0:T(8,128)(2,1)S(1)}, u32[]{:S(2)}, u32[]{:S(2)}) collective-permute-start(bf16[4,8,16,128]{3,2,1,0:T(8,128)(2,1)S(1)} %get-tuple-element.24), channel_id=1, source_target_pairs={{0,16},{16,0},{1,17},{17,1},{2,18},{18,2},{3,19},{19,3},{4,20},{20... | collective-permute-start | bytes 393224 | tf_op jit(solution)/shard_map/ppermute | solution.py:224
  57.8 1.3 %collective-permute-done.1.got_ref = bf16[4,8,16,128]{3,2,1,0:T(8,128)(2,1)S(1)} collective-permute-done((bf16[4,8,16,128]{3,2,1,0:T(8,128)(2,1)S(1)}, bf16[4,8,16,128]{3,2,1,0:T(8,128)(2,1)S(1)}, u32[]{:S(2)}, u32[]{:S(2)}) %collective-permute-start.1) | collective-permute-done | bytes 131104 | tf_op jit(solution)/shard_map/ppermute | solution.py:224
  59.2 5.3 %all-to-all-done.3.dkv_ref = bf16[8,8,16,128]{3,2,1,0:T(8,128)(2,1)S(1)} async-done(((bf16[8,8,16,128]{3,2,1,0:T(8,128)(2,1)}), bf16[8,8,16,128]{3,2,1,0:T(8,128)(2,1)S(1)}, u32[]{:S(2)}, u32[]{:S(2)}) %all-to-all-start.3) | async-done | bytes 262176 | tf_op jit(solution)/shard_map/all_to_all | solution.py:220
  64.4 8.3 %all_to_all.32.db_ref = bf16[4,8,16,128]{3,2,1,0:T(8,128)(2,1)S(1)} all-to-all(bf16[4,8,16,128]{3,2,1,0:T(8,128)(2,1)S(1)} %shard_map.80), channel_id=1, replica_groups=mesh['x'=4,'zhh'=2,'zhl'=2,'core'=2,'zl'=2,'yh'=2,'yl'=4] {'x'}, dimensions={0} | all-to-all | bytes 262144 | tf_op jit(solution)/shard_map/all_to_all | solution.py:220
  72.8 0.1 shard_map.81
  72.9 0.0 copy-start
  72.9 0.0 copy-start.1
  72.9 0.0 copy-start.2
  72.9 10.5 %all_to_all.33.pack_ref = bf16[8,48,128]{2,1,0:T(8,128)(2,1)S(1)} all-to-all(bf16[8,48,128]{2,1,0:T(8,128)(2,1)S(1)} %shard_map.81), channel_id=1, replica_groups=mesh['x'=4,'zhh'=2,'zhl'=2,'core'=2,'zl'=2,'yh'=2,'yl'=4] {'zhl','zl','z..., dimensions={0} | all-to-all | bytes 196608 | tf_op jit(solution)/shard_map/all_to_all | solution.py:220
  83.4 0.0 copy-done
  83.4 0.0 copy-done.1
  83.4 0.0 copy-done.2
  83.4 1.0 %shard_map.82 = (bf16[128,64]{1,0:T(8,128)(2,1)}, bf16[128,64]{1,0:T(8,128)(2,1)}, f32[8,2,1024]{2,1,0:T(2,128)}) custom-call(bf16[8,48,128]{2,1,0:T(8,128)(2,1)S(1)} %all_to_all.33.pack_ref, f32[200,128]{1,0:T(8,128)S(1)} %copy-done.1, bf16[64,256]{1,0:T(8,128)(2,1)S(1)} %copy-done, bf16[64,64]{1,0:T(8,128)(2,1)S(1)} %copy-done.2), custom_call_target="tpu_custom_call" | custom-call | tf_op jit(solution)/shard_map/pallas_call | solution.py:205
  (3 shorter events, 0.1 us)
Async XLA Ops:
  31.4 16.5 %all-to-all-start.2 = ((bf16[8,8,16,128]{3,2,1,0:T(8,128)(2,1)}), bf16[8,8,16,128]{3,2,1,0:T(8,128)(2,1)S(1)}, u32[]{:S(2)}, u32[]{:S(2)}) async-start(bf16[8,8,16,128]{3,2,1,0:T(8,128)(2,1)} %broadcast_in_dim.4), calls=%async_computation.2 | async-start | bytes 524288 | tf_op jit(solution)/shard_map/all_to_all | solution.py:220
  39.0 3.2 %collective-permute-start = (bf16[4,8,16,128]{3,2,1,0:T(8,128)(2,1)S(1)}, bf16[4,8,16,128]{3,2,1,0:T(8,128)(2,1)S(1)}, u32[]{:S(2)}, u32[]{:S(2)}) collective-permute-start(bf16[4,8,16,128]{3,2,1,0:T(8,128)(2,1)S(1)} %all_to_all.31.own_ref), channel_id=1, source_target_pairs={{0,16},{16,0},{1,17},{17,1},{2,18},{18,2},{3,19},{19,3},{4,20},{20... | collective-permute-start | bytes 393224 | tf_op jit(solution)/shard_map/ppermute | solution.py:224
  52.4 12.1 %all-to-all-start.3 = ((bf16[8,8,16,128]{3,2,1,0:T(8,128)(2,1)}), bf16[8,8,16,128]{3,2,1,0:T(8,128)(2,1)S(1)}, u32[]{:S(2)}, u32[]{:S(2)}) async-start(bf16[8,8,16,128]{3,2,1,0:T(8,128)(2,1)} %get-tuple-element.21), calls=%async_computation.3 | async-start | bytes 524288 | tf_op jit(solution)/shard_map/all_to_all | solution.py:220
  55.9 3.2 %collective-permute-start.1 = (bf16[4,8,16,128]{3,2,1,0:T(8,128)(2,1)S(1)}, bf16[4,8,16,128]{3,2,1,0:T(8,128)(2,1)S(1)}, u32[]{:S(2)}, u32[]{:S(2)}) collective-permute-start(bf16[4,8,16,128]{3,2,1,0:T(8,128)(2,1)S(1)} %get-tuple-element.24), channel_id=1, source_target_pairs={{0,16},{16,0},{1,17},{17,1},{2,18},{18,2},{3,19},{19,3},{4,20},{20... | collective-permute-start | bytes 393224 | tf_op jit(solution)/shard_map/ppermute | solution.py:224
  72.9 10.5 %copy-start = (bf16[64,256]{1,0:T(8,128)(2,1)S(1)}, bf16[64,256]{1,0:T(8,128)(2,1)}, u32[]{:S(2)}) copy-start(bf16[64,256]{1,0:T(8,128)(2,1)} %wm_ref.1) | copy-start | bytes 98308
  72.9 10.5 %copy-start.1 = (f32[200,128]{1,0:T(8,128)S(1)}, f32[200,128]{1,0:T(8,128)}, u32[]{:S(2)}) copy-start(f32[200,128]{1,0:T(8,128)} %get-tuple-element.27.save_ref) | copy-start | bytes 307204
  72.9 10.5 %copy-start.2 = (bf16[64,64]{1,0:T(8,128)(2,1)S(1)}, bf16[64,64]{1,0:T(8,128)(2,1)}, u32[]{:S(2)}) copy-start(bf16[64,64]{1,0:T(8,128)(2,1)} %wf_ref.1) | copy-start | bytes 24580

commit v13 on v12

--- a/solution.py
+++ b/solution.py
@@ -15,9 +15,9 @@
 SCALE = 1.0 / math.sqrt(HEAD_DIM)
 
 DEPTH = ("x", "zhh", "zhl", "core")
-RES = ("zl", "yh", "yl")
+RES = ("zl", "y")
 HEAD_AXES = ("zhl", "zl", "zhh")
-KEY_AXES = ("yl", "yh")
+RING = [i * 3 % 8 for i in range(8)]
 
 
 def tdot(a, b, ca, cb):
@@ -94,7 +94,7 @@
     def score(n, at):
         dl, lanes = n // 2, slice(n % 2 * 64, n % 2 * 64 + 64)
         kv_ref[n, 0:16] = jnp.concatenate(
-            [kv_in_ref[PEER[y], SOURCE[zl][dl]][:, lanes] for zl in range(2) for y in range(8)], 1
+            [kv_in_ref[RING[y], SOURCE[zl][dl]][:, lanes] for zl in range(2) for y in range(8)], 1
         )
         kv_ref[n, 16:32] = ones
         qd = jnp.concatenate([pack_ref[SOURCE[zl][dl], 0:16][:, lanes] for zl in range(2)], 1)
@@ -148,7 +148,7 @@
             for y in range(8):
                 r = zl * 8 + y
                 part_y = slice(r * 64, r * 64 + 64)
-                dkv_ref[PEER[y], SOURCE[zl][dl]] = jnp.concatenate(
+                dkv_ref[RING[y], SOURCE[zl][dl]] = jnp.concatenate(
                     [grads[dl * 2 + s][:, part_y] for s in range(2)], 1
                 )
 
@@ -216,8 +216,8 @@
     return jax.ShapeDtypeStruct(dims, dtype)
 
 
-def exchange(a, axes):
-    return lax.all_to_all(a, axes, 0, 0, tiled=True)
+def exchange(a, axes, groups=None):
+    return lax.all_to_all(a, axes, 0, 0, axis_index_groups=groups, tiled=True)
 
 
 def swap_core(a):
@@ -240,7 +240,7 @@
     rows = exchange(jnp.broadcast_to(rows[None], (4,) + rows.shape), ("x",))
     own = jnp.broadcast_to(pack[None, :, 16:32], (8, 8, 16, 128))
     own, rows = lax.optimization_barrier((own, rows))
-    kv = exchange(own, KEY_AXES)
+    kv = exchange(own, "y", [RING])
     layout = [pltpu.VMEM((8, 8, 16, 128), f32), pltpu.VMEM((8, 128, 128), f32)]
     (bias_rows,) = call(bias_kernel, [shape(128, 1024, dtype=f32)], rows, swap_core(rows), scratch=layout)
     block, quad, octet = shape(8, 16, 128), shape(4, 8, 16, 128), shape(8, 8, 16, 128)
@@ -251,7 +251,7 @@
         scratch=[pltpu.VMEM((8, 32, 1024), jnp.bfloat16), pltpu.VMEM((8, 128, 1024), f32),
                  pltpu.VMEM((8, 256, 1024), jnp.bfloat16)],
     )
-    dkv = exchange(dkv, KEY_AXES)
+    dkv = exchange(dkv, "y", [RING])
     keep, give = call(bias_grad_kernel, [quad, quad], acc, scratch=layout)
     (db,) = call(join_kernel, [quad], keep, swap_core(give))
     dkv, db = lax.optimization_barrier((dkv, db))
@@ -267,7 +267,7 @@
 
 
 def solution(mesh):
-    fine = Mesh(mesh.devices.reshape(4, 2, 2, 2, 2, 2, 4), DEPTH + RES)
+    fine = Mesh(mesh.devices.reshape(4, 2, 2, 2, 2, 8), DEPTH + RES)
     tokens = P(DEPTH, RES, None)
     rows = P(None, RES + DEPTH, None)
     return jax.shard_map(

time: 85 us -> 86.4 us (1.016)
  the two profiles are of different devices: /device:TPU:8 before, /device:TPU:6 now
where the time goes in v13:
time: 86.4 us; the launch traced here: 84.8 us
  blocking collectives  45.4 us (53%)
  waiting for transfers between devices  15.9 us (18%)
  starting transfers between devices  14.3 us (17%)
  Pallas kernels  7.65 us (9%)
    all_to_all x4, blocking collectives, exchange(): return lax.all_to_all(a, axes, 0, 0, axis_index_groups=groups, tiled=True)  45.4 us
    all_to_all x2, waiting for transfers between devices, exchange(): return lax.all_to_all(a, axes, 0, 0, axis_index_groups=groups, tiled=True)  13.3 us
    all_to_all x2, starting transfers between devices, exchange(): return lax.all_to_all(a, axes, 0, 0, axis_index_groups=groups, tiled=True)  10.5 us
    pallas_call x7, Pallas kernels, call(): pl.pallas_call(kernel, out_shape=outs, in_specs=[pl.BlockSpec(memory_spac...  7.65 us
    ppermute x2, starting transfers between devices, swap_core(): return lax.ppermute(a, 'core', [(0, 1), (1, 0)])  3.83 us
    ppermute x2, waiting for transfers between devices, swap_core(): return lax.ppermute(a, 'core', [(0, 1), (1, 0)])  2.63 us
  transfers between devices with their start and end apart: 4, of which 4 were waited for; matrix products, arithmetic and copies ran while one was open for 0% of the time, Pallas kernels for 0%

profile of v13, /device:TPU:6, one launch (start us, length us, event | category | flops | bytes accessed | tf_op | source)
XLA Modules:
  0.0 84.8 jit_solution(13590259106351076021)
XLA Ops:
  0.6 1.8 %shard_map.76 = (bf16[8,48,128]{2,1,0:T(8,128)(2,1)}, f32[200,128]{1,0:T(8,128)}) custom-call(bf16[128,64]{1,0:T(8,128)(2,1)} %bitcast.4, bf16[128,64]{1,0:T(8,128)(2,1)} %bitcast.5, bf16[64,256]{1,0:T(8,128)(2,1)} %wm_ref.1, bf16[64,64]{1,0:T(8,128)(2,1)} %wf_ref.1, bf16[8,2,1024]{2,1,0:T(2,128)(2,1)} %bias_hbm.1), custom_call_target="tpu_custom_call" | custom-call | tf_op jit(solution)/shard_map/pallas_call | solution.py:205
  2.5 18.1 %all_to_all.30.pack_ref = bf16[8,48,128]{2,1,0:T(8,128)(2,1)S(1)} all-to-all(bf16[8,48,128]{2,1,0:T(8,128)(2,1)} %get-tuple-element.17), channel_id=1, replica_groups=mesh['x'=4,'zhh'=2,'zhl'=2,'core'=2,'zl'=2,'y'=8] {'zhl','zl','zhh'}, dimensions={0} | all-to-all | bytes 196608 | tf_op jit(solution)/shard_map/all_to_all | solution.py:220
  20.6 8.5 %all_to_all.31.own_ref = bf16[4,8,16,128]{3,2,1,0:T(8,128)(2,1)S(1)} all-to-all(bf16[4,8,16,128]{3,2,1,0:T(8,128)(2,1)S(1)} %broadcast_in_dim.5), channel_id=1, replica_groups=mesh['x'=4,'zhh'=2,'zhl'=2,'core'=2,'zl'=2,'y'=8] {'x'}, dimensions={0} | all-to-all | bytes 262144 | tf_op jit(solution)/shard_map/all_to_all | solution.py:220
  29.1 0.7 broadcast_in_dim.4
  29.8 7.1 %all-to-all-start.2 = ((bf16[8,8,16,128]{3,2,1,0:T(8,128)(2,1)}), bf16[8,8,16,128]{3,2,1,0:T(8,128)(2,1)S(1)}, u32[]{:S(2)}, u32[]{:S(2)}) async-start(bf16[8,8,16,128]{3,2,1,0:T(8,128)(2,1)} %broadcast_in_dim.4), calls=%async_computation.2 | async-start | bytes 524288 | tf_op jit(solution)/shard_map/all_to_all | solution.py:220
  36.9 1.9 %collective-permute-start = (bf16[4,8,16,128]{3,2,1,0:T(8,128)(2,1)S(1)}, bf16[4,8,16,128]{3,2,1,0:T(8,128)(2,1)S(1)}, u32[]{:S(2)}, u32[]{:S(2)}) collective-permute-start(bf16[4,8,16,128]{3,2,1,0:T(8,128)(2,1)S(1)} %all_to_all.31.own_ref), channel_id=1, source_target_pairs={{0,16},{16,0},{1,17},{17,1},{2,18},{18,2},{3,19},{19,3},{4,20},{20... | collective-permute-start | bytes 393224 | tf_op jit(solution)/shard_map/ppermute | solution.py:224
  38.9 1.3 %collective-permute-done.sibling_ref = bf16[4,8,16,128]{3,2,1,0:T(8,128)(2,1)S(1)} collective-permute-done((bf16[4,8,16,128]{3,2,1,0:T(8,128)(2,1)S(1)}, bf16[4,8,16,128]{3,2,1,0:T(8,128)(2,1)S(1)}, u32[]{:S(2)}, u32[]{:S(2)}) %collective-permute-start) | collective-permute-done | bytes 131104 | tf_op jit(solution)/shard_map/ppermute | solution.py:224
  40.2 0.2 shard_map.77.bias_ref
  40.4 6.7 %all-to-all-done.2.kv_in_ref = bf16[8,8,16,128]{3,2,1,0:T(8,128)(2,1)S(1)} async-done(((bf16[8,8,16,128]{3,2,1,0:T(8,128)(2,1)}), bf16[8,8,16,128]{3,2,1,0:T(8,128)(2,1)S(1)}, u32[]{:S(2)}, u32[]{:S(2)}) %all-to-all-start.2) | async-done | bytes 262176 | tf_op jit(solution)/shard_map/all_to_all | solution.py:220
  47.1 4.4 %shard_map.78 = (bf16[8,16,128]{2,1,0:T(8,128)(2,1)S(1)}, bf16[8,8,16,128]{3,2,1,0:T(8,128)(2,1)}, f32[128,1024]{1,0:T(8,128)S(1)}) custom-call(bf16[8,48,128]{2,1,0:T(8,128)(2,1)S(1)} %all_to_all.30.pack_ref, bf16[8,8,16,128]{3,2,1,0:T(8,128)(2,1)S(1)} %all-to-all-done.2.kv_in_ref, f32[128,1024]{1,0:T(8,128)S(1)} %shard_map.77.bias_ref), custom_call_target="tpu_custom_call" | custom-call | tf_op jit(solution)/shard_map/pallas_call | solution.py:205
  51.5 3.4 %all-to-all-start.3 = ((bf16[8,8,16,128]{3,2,1,0:T(8,128)(2,1)}), bf16[8,8,16,128]{3,2,1,0:T(8,128)(2,1)S(1)}, u32[]{:S(2)}, u32[]{:S(2)}) async-start(bf16[8,8,16,128]{3,2,1,0:T(8,128)(2,1)} %get-tuple-element.21), calls=%async_computation.3 | async-start | bytes 524288 | tf_op jit(solution)/shard_map/all_to_all | solution.py:220
  54.9 0.1 shard_map.79
  55.1 1.9 %collective-permute-start.1 = (bf16[4,8,16,128]{3,2,1,0:T(8,128)(2,1)S(1)}, bf16[4,8,16,128]{3,2,1,0:T(8,128)(2,1)S(1)}, u32[]{:S(2)}, u32[]{:S(2)}) collective-permute-start(bf16[4,8,16,128]{3,2,1,0:T(8,128)(2,1)S(1)} %get-tuple-element.24), channel_id=1, source_target_pairs={{0,16},{16,0},{1,17},{17,1},{2,18},{18,2},{3,19},{19,3},{4,20},{20... | collective-permute-start | bytes 393224 | tf_op jit(solution)/shard_map/ppermute | solution.py:224
  57.0 1.3 %collective-permute-done.1.got_ref = bf16[4,8,16,128]{3,2,1,0:T(8,128)(2,1)S(1)} collective-permute-done((bf16[4,8,16,128]{3,2,1,0:T(8,128)(2,1)S(1)}, bf16[4,8,16,128]{3,2,1,0:T(8,128)(2,1)S(1)}, u32[]{:S(2)}, u32[]{:S(2)}) %collective-permute-start.1) | collective-permute-done | bytes 131104 | tf_op jit(solution)/shard_map/ppermute | solution.py:224
  58.4 6.6 %all-to-all-done.3.dkv_ref = bf16[8,8,16,128]{3,2,1,0:T(8,128)(2,1)S(1)} async-done(((bf16[8,8,16,128]{3,2,1,0:T(8,128)(2,1)}), bf16[8,8,16,128]{3,2,1,0:T(8,128)(2,1)S(1)}, u32[]{:S(2)}, u32[]{:S(2)}) %all-to-all-start.3) | async-done | bytes 262176 | tf_op jit(solution)/shard_map/all_to_all | solution.py:220
  65.0 8.3 %all_to_all.32.db_ref = bf16[4,8,16,128]{3,2,1,0:T(8,128)(2,1)S(1)} all-to-all(bf16[4,8,16,128]{3,2,1,0:T(8,128)(2,1)S(1)} %shard_map.80), channel_id=1, replica_groups=mesh['x'=4,'zhh'=2,'zhl'=2,'core'=2,'zl'=2,'y'=8] {'x'}, dimensions={0} | all-to-all | bytes 262144 | tf_op jit(solution)/shard_map/all_to_all | solution.py:220
  73.3 0.1 shard_map.81
  73.4 0.0 copy-start
  73.4 0.0 copy-start.1
  73.4 0.0 copy-start.2
  73.4 10.4 %all_to_all.33.pack_ref = bf16[8,48,128]{2,1,0:T(8,128)(2,1)S(1)} all-to-all(bf16[8,48,128]{2,1,0:T(8,128)(2,1)S(1)} %shard_map.81), channel_id=1, replica_groups=mesh['x'=4,'zhh'=2,'zhl'=2,'core'=2,'zl'=2,'y'=8] {'zhl','zl','zhh'}, dimensions={0} | all-to-all | bytes 196608 | tf_op jit(solution)/shard_map/all_to_all | solution.py:220
  83.8 0.0 copy-done
  83.8 0.0 copy-done.1
  83.8 0.0 copy-done.2
  83.8 1.0 %shard_map.82 = (bf16[128,64]{1,0:T(8,128)(2,1)}, bf16[128,64]{1,0:T(8,128)(2,1)}, f32[8,2,1024]{2,1,0:T(2,128)}) custom-call(bf16[8,48,128]{2,1,0:T(8,128)(2,1)S(1)} %all_to_all.33.pack_ref, f32[200,128]{1,0:T(8,128)S(1)} %copy-done.1, bf16[64,256]{1,0:T(8,128)(2,1)S(1)} %copy-done, bf16[64,64]{1,0:T(8,128)(2,1)S(1)} %copy-done.2), custom_call_target="tpu_custom_call" | custom-call | tf_op jit(solution)/shard_map/pallas_call | solution.py:205
  (3 shorter events, 0.1 us)
Async XLA Ops:
  29.8 17.2 %all-to-all-start.2 = ((bf16[8,8,16,128]{3,2,1,0:T(8,128)(2,1)}), bf16[8,8,16,128]{3,2,1,0:T(8,128)(2,1)S(1)}, u32[]{:S(2)}, u32[]{:S(2)}) async-start(bf16[8,8,16,128]{3,2,1,0:T(8,128)(2,1)} %broadcast_in_dim.4), calls=%async_computation.2 | async-start | bytes 524288 | tf_op jit(solution)/shard_map/all_to_all | solution.py:220
  36.9 3.2 %collective-permute-start = (bf16[4,8,16,128]{3,2,1,0:T(8,128)(2,1)S(1)}, bf16[4,8,16,128]{3,2,1,0:T(8,128)(2,1)S(1)}, u32[]{:S(2)}, u32[]{:S(2)}) collective-permute-start(bf16[4,8,16,128]{3,2,1,0:T(8,128)(2,1)S(1)} %all_to_all.31.own_ref), channel_id=1, source_target_pairs={{0,16},{16,0},{1,17},{17,1},{2,18},{18,2},{3,19},{19,3},{4,20},{20... | collective-permute-start | bytes 393224 | tf_op jit(solution)/shard_map/ppermute | solution.py:224
  51.5 13.4 %all-to-all-start.3 = ((bf16[8,8,16,128]{3,2,1,0:T(8,128)(2,1)}), bf16[8,8,16,128]{3,2,1,0:T(8,128)(2,1)S(1)}, u32[]{:S(2)}, u32[]{:S(2)}) async-start(bf16[8,8,16,128]{3,2,1,0:T(8,128)(2,1)} %get-tuple-element.21), calls=%async_computation.3 | async-start | bytes 524288 | tf_op jit(solution)/shard_map/all_to_all | solution.py:220
  55.1 3.2 %collective-permute-start.1 = (bf16[4,8,16,128]{3,2,1,0:T(8,128)(2,1)S(1)}, bf16[4,8,16,128]{3,2,1,0:T(8,128)(2,1)S(1)}, u32[]{:S(2)}, u32[]{:S(2)}) collective-permute-start(bf16[4,8,16,128]{3,2,1,0:T(8,128)(2,1)S(1)} %get-tuple-element.24), channel_id=1, source_target_pairs={{0,16},{16,0},{1,17},{17,1},{2,18},{18,2},{3,19},{19,3},{4,20},{20... | collective-permute-start | bytes 393224 | tf_op jit(solution)/shard_map/ppermute | solution.py:224
  73.4 10.5 %copy-start = (bf16[64,256]{1,0:T(8,128)(2,1)S(1)}, bf16[64,256]{1,0:T(8,128)(2,1)}, u32[]{:S(2)}) copy-start(bf16[64,256]{1,0:T(8,128)(2,1)} %wm_ref.1) | copy-start | bytes 98308
  73.4 10.5 %copy-start.1 = (f32[200,128]{1,0:T(8,128)S(1)}, f32[200,128]{1,0:T(8,128)}, u32[]{:S(2)}) copy-start(f32[200,128]{1,0:T(8,128)} %get-tuple-element.27.save_ref) | copy-start | bytes 307204
  73.4 10.5 %copy-start.2 = (bf16[64,64]{1,0:T(8,128)(2,1)S(1)}, bf16[64,64]{1,0:T(8,128)(2,1)}, u32[]{:S(2)}) copy-start(bf16[64,64]{1,0:T(8,128)(2,1)} %wf_ref.1) | copy-start | bytes 24580
